TPU v7x, 128 devices: a whole 4x4x4 slice. The times are simulated.
128 devices in a mesh: row: 32 (over y, z, core), col: 4 (over x).
Axes of the slice: x: 4, y: 4, z: 4, core: 2. Of those that a mesh axis runs over, the one named last changes fastest.
Arguments:
- tile_values: bfloat16 [5632, 4, 256, 256], P('row', 'col'), may hold values from -0.375 to 0.375
- tile_rows: int32 [5632, 4], P('row', 'col'), may hold values from 0 to 15, as said below
- tile_source: int32 [5632, 4], P('row', 'col'), may hold values from 0 to 31
- tile_slot: int32 [5632, 4], P('row', 'col'), may hold values from 0 to 1
- send_lists: int32 [32, 4, 32, 2], P('row', 'col'), may hold values from 0 to 7
- basis_blocks: bfloat16 [256, 4, 256, 256], P('row', 'col'), may hold values from -6 to 6
Outputs:
- new_basis: float32 [131072, 256], P(('row', 'col'))
- triangle: float32 [256, 256], replicated
Inputs may be any that keep to these rules, and one draw needn't show every extreme that they name: `tile_rows`: in every slab and group each of the 16 block rows holds at least one tile.
All inputs are finite; a program needn't handle non-finite values.
Results may differ from a plain program's by a relative error of at most 0.0015.
Values may be sent and summed in bfloat16 or wider, within the bound.
No kernel may reach another device: no remote copies, remote signals or barrier semaphores. Data moves between devices by JAX's collectives and lax.ppermute only.
A program may use at most 256 MiB of HBM per device.

v0:
```python
import jax
import jax.numpy as jnp
from jax import lax
from jax.sharding import PartitionSpec as P

BR_DEV = 16


def upper_factor(gram):
    width = gram.shape[0]
    index = jnp.arange(width, dtype=jnp.int32)

    def row_fill(j, upper):
        unit = (index == j).astype(jnp.float32)
        known = jnp.dot(upper, unit, precision=lax.Precision.HIGHEST)
        target = lax.dynamic_index_in_dim(gram, j, 0, keepdims=False)
        residue = target - jnp.dot(known, upper, precision=lax.Precision.HIGHEST)
        pivot = jnp.sqrt(lax.dynamic_index_in_dim(residue, j, 0, keepdims=False))
        filled = jnp.where(index >= j, residue / pivot, jnp.float32(0.0))
        return upper + unit[:, None] * filled[None, :]

    return lax.fori_loop(0, width, row_fill, jnp.zeros((width, width), jnp.float32))


def upper_inverse(upper):
    width = upper.shape[0]
    index = jnp.arange(width, dtype=jnp.int32)

    def row_step(step, inverse):
        i = (width - 1 - step).astype(jnp.int32)
        row_now = lax.dynamic_index_in_dim(upper, i, 0, keepdims=False)
        pivot = lax.dynamic_index_in_dim(row_now, i, 0, keepdims=False)
        unit = (index == i).astype(jnp.float32)
        solved = (unit - jnp.dot(row_now, inverse, precision=lax.Precision.HIGHEST)) / pivot
        return jnp.where((index == i)[:, None], solved[None, :], inverse)

    return lax.fori_loop(0, width, row_step, jnp.zeros((width, width), jnp.float32))


def local(tile_values, tile_rows, tile_source, tile_slot, send_lists, basis_blocks):
    values = tile_values[:, 0]
    blocks_row = tile_rows[:, 0]
    source = tile_source[:, 0]
    slotted = tile_slot[:, 0]
    owned = basis_blocks[:, 0]
    slot_count = send_lists.shape[3]
    rank_width = owned.shape[2]
    outgoing = owned[send_lists[0, 0]]
    arrived = lax.all_to_all(outgoing, "row", split_axis=0, concat_axis=0, tiled=True)
    flatten = arrived.reshape(-1, arrived.shape[2], arrived.shape[3])
    chosen = flatten[source * slot_count + slotted]
    product = jnp.einsum("tij,tjk->tik", values, chosen, preferred_element_type=jnp.float32)
    selector = (blocks_row[None, :] == jnp.arange(BR_DEV, dtype=jnp.int32)[:, None]).astype(
        jnp.float32
    )
    partial_value = jnp.einsum("bt,tik->bik", selector, product, precision=lax.Precision.HIGHEST)
    partial_value = partial_value.reshape(-1, rank_width)
    local_y = lax.psum_scatter(partial_value, "col", scatter_dimension=0, tiled=True)
    gram = jnp.dot(local_y.T, local_y, precision=lax.Precision.HIGHEST)
    summed = lax.psum(gram, ("row", "col"))
    upper = upper_factor(summed)
    cells_all = local_y.shape[0] * lax.axis_size("row") * lax.axis_size("col")
    scale = jnp.sqrt(jnp.float32(cells_all))
    solved = jnp.dot(local_y, upper_inverse(upper), precision=lax.Precision.HIGHEST)
    return (solved * scale, upper / scale)


def solution(mesh):
    return jax.shard_map(
        local,
        mesh=mesh,
        in_specs=(
            P("row", "col", None, None),
            P("row", "col"),
            P("row", "col"),
            P("row", "col"),
            P("row", "col", None, None),
            P("row", "col", None, None),
        ),
        out_specs=(P(("row", "col"), None), P()),
        check_vma=False,
    )
```

profile of v0, /device:TPU:1, one launch (start us, length us, event | category | flops | bytes accessed | tf_op | source)
XLA Modules:
  0.0 1576.3 jit_solution(10319401639767442812)
XLA Ops:
  7.2 0.8 compare_select_fusion.2
  8.4 5.5 gather_fusion
  13.9 9.7 all-to-all-start
  23.7 108.4 %all-to-all-done = bf16[32,2,256,256]{3,2,1,0:T(8,128)(2,1)} async-done(((bf16[32,2,256,256]{3,2,1,0:T(8,128)(2,1)}), bf16[32,2,256,256]{3,2,1,0:T(8,128)(2,1)}, u32[]{:S(2)}, u32[]{:S(2)}) %all-to-all-start) | async-done | bytes 8388640 | tf_op jit(solution)/shard_map/all_to_all | solution.py:49
  132.1 13.8 gather_fusion.1
  146.0 37.6 %fusion.24 = f32[176,256,256]{2,1,0:T(8,128)} fusion(bf16[176,256,256]{2,1,0:T(8,128)(2,1)} %gather_fusion.1, bf16[176,1,256,256]{3,2,1,0:T(8,128)(2,1)} %param.10), kind=kOutput, calls=%fused_computation.32 | convolution fusion | flops 5905580032 | bytes 92274688 | tf_op jit(solution)/shard_map/tij,tjk->tik/dot_general | solution.py:52
  183.6 46.6 %copy.11 = f32[176,256,256]{1,0,2:T(8,128)} copy(f32[176,256,256]{2,1,0:T(8,128)} %fusion.24) | data formatting | bytes 92274688 | tf_op jit(solution)/shard_map/tij,tjk->tik/dot_general | solution.py:52
  230.2 20.4 %fusion.22 = f32[16,256,256]{2,0,1:T(8,128)S(1)} fusion(f32[176,256,256]{1,0,2:T(8,128)} %copy.11, s32[176]{0:T(256)S(1)} %bitcast.63), kind=kOutput, calls=%fused_computation.30 | convolution fusion | flops 2214595328 | bytes 50332352 | tf_op jit(solution)/shard_map/bt,tik->bik/dot_general | solution.py:56
  250.6 4.4 copy.10
  255.2 61.8 %reduce-scatter.2.cloned.1.call-done = f32[1024,256]{1,0:T(8,128)} async-done(((f32[4096,256]{1,0:T(8,128)}), f32[1024,256]{1,0:T(8,128)}) %reduce-scatter.2.cloned.1.call-update) | async-done | bytes 1048592 | tf_op jit(solution)/shard_map/reduce_scatter | solution.py:58
  317.0 4.1 fusion.29
  321.1 143.2 %all-reduce.2.cloned.1.call-done = f32[256,256]{1,0:T(8,128)} async-done(((f32[256,256]{1,0:T(8,128)}), f32[256,256]{1,0:T(8,128)}) %all-reduce.2.cloned.1.call-update) | async-done | bytes 262160 | tf_op jit(solution)/shard_map/psum | solution.py:60
  464.4 680.8 %while.33 = (s32[]{:T(128)}, f32[256,256]{1,0:T(8,128)S(1)}, f32[256,256]{1,0:T(8,128)}, s32[]{:T(128)}, s32[]{:T(128)}) while((s32[]{:T(128)}, f32[256,256]{1,0:T(8,128)S(1)}, f32[256,256]{1,0:T(8,128)}, s32[]{:T(128)}, s32[]{:T(128)}) %tuple.80), condition=%wide.region_3.4_spmd.clone.clone, body=%wide.region_2.3_spmd.clone.clone.sunk | while | flops 1902083 | bytes 1063021 | solution.py:22
  467.5 0.7 constant_dynamic-slice_fusion.2
  470.2 0.7 constant_dynamic-slice_fusion.2
  475.5 0.7 constant_dynamic-slice_fusion.2
  478.1 0.7 constant_dynamic-slice_fusion.2
  483.5 0.7 constant_dynamic-slice_fusion.2
  486.1 0.7 constant_dynamic-slice_fusion.2
  491.4 0.7 constant_dynamic-slice_fusion.2
  494.1 0.7 constant_dynamic-slice_fusion.2
  499.4 0.7 constant_dynamic-slice_fusion.2
  502.1 0.7 constant_dynamic-slice_fusion.2
  510.0 0.7 constant_dynamic-slice_fusion.2
  518.0 0.7 constant_dynamic-slice_fusion.2
  520.7 0.7 constant_dynamic-slice_fusion.2
  526.0 0.7 constant_dynamic-slice_fusion.2
  528.7 0.7 constant_dynamic-slice_fusion.2
  534.0 0.7 constant_dynamic-slice_fusion.2
  536.6 0.7 constant_dynamic-slice_fusion.2
  1145.9 420.4 %while.32 = (s32[]{:T(128)}, f32[256,256]{1,0:T(8,128)S(1)}, f32[256,256]{1,0:T(8,128)S(1)}, s32[]{:T(128)}, s32[]{:T(128)}, /*index=5*/s32[]{:T(128)}, s32[]{:T(128)}) while((s32[]{:T(128)}, f32[256,256]{1,0:T(8,128)S(1)}, f32[256,256]{1,0:T(8,128)S(1)}, s32[]{:T(128)}, s32[]{:T(128)}, /*index=5*/s32[]{:T(128)}, s32[]{:T(128)}) %tuple.83), condition=%wide.region_5.6_spmd.clone, body=%wide.region_4.5_spmd.clone.sunk | while | flops 984328 | bytes 792242 | solution.py:37
  1566.3 3.2 convolution_multiply_fusion
  (3589 shorter events, 888.5 us)
Async XLA Ops:
  7.2 1.2 copy-start
  7.2 16.5 %copy-start.4 = (s32[176,1]{0,1:T(1,128)S(1)}, s32[176,1]{0,1:T(1,128)}, u32[]{:S(2)}) copy-start(s32[176,1]{0,1:T(1,128)} %param.12) | copy-start | bytes 2116
  7.2 16.5 %copy-start.3 = (s32[176,1]{0,1:T(1,128)S(1)}, s32[176,1]{0,1:T(1,128)}, u32[]{:S(2)}) copy-start(s32[176,1]{0,1:T(1,128)} %param.13) | copy-start | bytes 2116
  13.9 118.2 %all-to-all-start = ((bf16[32,2,256,256]{3,2,1,0:T(8,128)(2,1)}), bf16[32,2,256,256]{3,2,1,0:T(8,128)(2,1)}, u32[]{:S(2)}, u32[]{:S(2)}) async-start(bf16[32,2,256,256]{3,2,1,0:T(8,128)(2,1)} %bitcast.57), calls=%async_computation | async-start | bytes 16777216 | tf_op jit(solution)/shard_map/all_to_all | solution.py:49
  23.6 293.4 %reduce-scatter.2.cloned.1.call-start = ((), (), s32[]{:S(2)}) async-start(), calls=%async_computation.2 | async-start | bytes 5242880 | tf_op jit(solution)/shard_map/reduce_scatter | solution.py:58
  183.6 46.6 %copy-start.2 = (s32[176,1]{0,1:T(1,128)S(1)}, s32[176,1]{0,1:T(1,128)}, u32[]{:S(2)}) copy-start(s32[176,1]{0,1:T(1,128)} %param.11) | copy-start | bytes 2116
  230.2 1339.3 %copy-start.1 = (bf16[8,1,256,256]{3,2,1,0:T(8,128)(2,1)S(1)}, bf16[8,1,256,256]{3,2,1,0:T(8,128)(2,1)}, u32[]{:S(2)}) copy-start(bf16[8,1,256,256]{3,2,1,0:T(8,128)(2,1)} %param.15) | copy-start | bytes 3145732
  255.0 209.4 %all-reduce.2.cloned.1.call-start = ((), (), s32[]{:S(2)}) async-start(), calls=%async_computation.3 | async-start | bytes 524288 | tf_op jit(solution)/shard_map/psum | solution.py:60
Sparse Core Ops, SparseCore 0:
  255.1 61.8 reduce-scatter.1
  323.1 141.2 all-reduce.1
where the time goes:
time: 1600 us; the launch traced here: 1580 us
  local copies, waits for them, and re-layouts  577 us (36%)
  waiting for transfers between devices  313 us (20%)
  matrix products  233 us (15%)
  other arithmetic  227 us (14%)
  loops' own time  202 us (13%)
    dynamic_slice x256, local copies, waits for them, and re-layouts, row_fill(): target = lax.dynamic_index_in_dim(gram, j, 0, keepdims=False)  190 us
    another operation x1, loops' own time, upper_factor(): lax.fori_loop(0, width, row_fill, jnp.zeros((width, width), jnp.float32))  189 us
    dynamic_slice x256, local copies, waits for them, and re-layouts, row_step(): pivot = lax.dynamic_index_in_dim(row_now, i, 0, keepdims=False)  164 us
    div x256, other arithmetic, row_step(): (unit - jnp.dot(row_now, inverse, precision=lax.Precision.HIGHEST)) / pivot  163 us
    dynamic_slice x256, local copies, waits for them, and re-layouts, row_fill(): pivot = jnp.sqrt(lax.dynamic_index_in_dim(residue, j, 0, keepdims=False))  150 us
    psum x1, waiting for transfers between devices, local(): summed = lax.psum(gram, ('row', 'col'))  143 us
    all_to_all x1, waiting for transfers between devices, local(): lax.all_to_all(outgoing, 'row', split_axis=0, concat_axis=0, tiled=True)  108 us
    reduce_scatter x1, waiting for transfers between devices, local(): lax.psum_scatter(partial_value, 'col', scatter_dimension=0, tiled=True)  61.8 us
  transfers between devices with their start and end apart: 3, of which 3 were waited for; matrix products, arithmetic and copies ran while one was open for 0% of the time, Pallas kernels for 0%

commit v1 on v0

v1 whole, which is shorter than its diff:
```python
import functools

import jax
import jax.numpy as jnp
from jax import lax
from jax.experimental import pallas as pl
from jax.experimental.pallas import tpu as pltpu
from jax.sharding import PartitionSpec as P

BR_DEV = 16
HALF = 128
GROUP = 8
STEP = 32704.0
LEAST = 2.0**-80
HIGHEST = lax.Precision.HIGHEST
F32 = jnp.float32


def pack_kernel(half, lists, owned, out, sems):
    count = out.shape[0]

    def one(i):
        return pltpu.make_async_copy(
            owned.at[lists[i], :, pl.ds(half * HALF, HALF)], out.at[i], sems.at[i]
        )

    for i in range(count):
        one(i).start()
    for i in range(count):
        one(i).wait()


def pack(lists, owned, half):
    count = lists.shape[0]
    height = owned.shape[1]
    return pl.pallas_call(
        functools.partial(pack_kernel, half),
        out_shape=jax.ShapeDtypeStruct((count, height, HALF), owned.dtype),
        in_specs=[
            pl.BlockSpec(memory_space=pltpu.SMEM),
            pl.BlockSpec(memory_space=pltpu.VMEM),
        ],
        out_specs=pl.BlockSpec(memory_space=pl.ANY),
        scratch_shapes=[pltpu.SemaphoreType.DMA((count,))],
        cost_estimate=pl.CostEstimate(
            flops=0, bytes_accessed=2 * count * height * HALF * 2, transcendentals=0
        ),
        name=f"pack{half}",
    )(lists, owned)


def encode(part):
    largest = jnp.max(jnp.abs(part), axis=0, keepdims=True)
    power = jnp.ceil(jnp.log2(jnp.maximum(largest, LEAST)))
    steps = jnp.floor(part * (jnp.exp2(-power) * STEP) + 0.5)
    return steps.astype(jnp.int32).astype(jnp.int16), power


def tiles_kernel(places, blocks, values, arrived, out, total):
    step = pl.program_id(0)

    @pl.when(step == 0)
    def _():
        total[...] = jnp.zeros_like(total)

    for u in range(GROUP):
        t = step * GROUP + u
        total[blocks[t]] += jnp.dot(values[u], arrived[places[t]], preferred_element_type=F32)

    @pl.when(step == pl.num_programs(0) - 1)
    def _():
        shares = out.shape[0]
        each = BR_DEV // shares
        for d in range(shares):
            part = total[d * each : (d + 1) * each]
            rows = each * part.shape[1]
            steps, power = encode(part.reshape(rows, HALF))
            out[d, pl.ds(0, rows)] = steps
            out[d, pl.ds(rows, 16)] = (
                jnp.broadcast_to(power, (16, HALF)).astype(jnp.int32).astype(jnp.int16)
            )


def tiles(places, blocks, values, arrived, shares, half):
    count, height, depth = values.shape
    rows = BR_DEV * height // shares
    return pl.pallas_call(
        tiles_kernel,
        grid_spec=pltpu.PrefetchScalarGridSpec(
            num_scalar_prefetch=2,
            grid=(count // GROUP,),
            in_specs=[
                pl.BlockSpec((GROUP, height, depth), lambda i, *_: (i, 0, 0)),
                pl.BlockSpec(arrived.shape, lambda i, *_: (0, 0, 0)),
            ],
            out_specs=pl.BlockSpec((shares, rows + 16, HALF), lambda i, *_: (0, 0, 0)),
            scratch_shapes=[pltpu.VMEM((BR_DEV, height, HALF), F32)],
        ),
        out_shape=jax.ShapeDtypeStruct((shares, rows + 16, HALF), jnp.int16),
        compiler_params=pltpu.CompilerParams(vmem_limit_bytes=40 * 2**20),
        cost_estimate=pl.CostEstimate(
            flops=2 * count * height * depth * HALF,
            bytes_accessed=count * height * depth * 2 + arrived.size * 2,
            transcendentals=0,
        ),
        name=f"tiles{half}",
    )(places, blocks, values, arrived)


def dot_t(a, b):
    return lax.dot_general(
        a, b, (((0,), (0,)), ((), ())), precision=HIGHEST, preferred_element_type=F32
    )


def dot_n(a, b):
    return jnp.dot(a, b, precision=HIGHEST, preferred_element_type=F32)


def dot_bt(a, b):
    return lax.dot_general(
        a, b, (((1,), (1,)), ((), ())), precision=HIGHEST, preferred_element_type=F32
    )


def decode(ref):
    shares, rows = ref.shape[0], ref.shape[1] - 16
    y = None
    for g in range(shares):
        power = ref[g, pl.ds(rows, 16)].astype(jnp.int32).astype(F32)[0:1]
        part = ref[g, pl.ds(0, rows)].astype(jnp.int32).astype(F32) * (
            jnp.exp2(power) * (1.0 / STEP)
        )
        y = part if y is None else y + part
    return y


def gram_kernel(*refs):
    (*before, coded, y_out, gram_out) = refs
    y = decode(coded)
    y_out[...] = y
    at = 0
    for ref in before:
        gram_out[pl.ds(at, HALF)] = dot_t(ref[...], y)
        at += HALF
    gram_out[pl.ds(at, HALF)] = dot_t(y, y)


def gram(coded, before):
    rows = coded.shape[1] - 16
    height = HALF * (len(before) + 1)
    return pl.pallas_call(
        gram_kernel,
        out_shape=(
            jax.ShapeDtypeStruct((rows, HALF), F32),
            jax.ShapeDtypeStruct((height, HALF), F32),
        ),
        compiler_params=pltpu.CompilerParams(vmem_limit_bytes=40 * 2**20),
        cost_estimate=pl.CostEstimate(
            flops=12 * rows * height * HALF, bytes_accessed=rows * HALF * 12, transcendentals=0
        ),
        name=f"gram{len(before)}",
    )(*before, coded)


def factor64(a):
    n = a.shape[0]
    row_at = lax.broadcasted_iota(jnp.int32, (n, n), 0)
    col_at = lax.broadcasted_iota(jnp.int32, (n, n), 1)
    unit = (row_at == col_at).astype(F32)
    wide = jnp.concatenate([a, unit], axis=1)
    strips = [wide[8 * i : 8 * i + 8] for i in range(n // 8)]
    in_strip = lax.broadcasted_iota(jnp.int32, (8, 2 * n), 0)
    for j in range(n):
        b, r = divmod(j, 8)
        row = strips[b][r : r + 1]
        scaled = row / row[:, j : j + 1]
        for i in range(b, n // 8):
            if i == b and r == 7:
                continue
            column = jnp.broadcast_to(strips[i][:, j : j + 1], (8, 2 * n))
            if i == b:
                column = jnp.where(in_strip > r, column, 0.0)
            strips[i] = strips[i] - column * scaled
    wide = jnp.concatenate(strips, axis=0)
    square, inverse = wide[:, :n], wide[:, n:]
    pivots = jnp.sum(jnp.where(row_at == col_at, square, 0.0), axis=1, keepdims=True)
    scale = 1.0 / jnp.sqrt(pivots)
    return (
        jnp.where(col_at >= row_at, square, 0.0) * scale,
        jnp.where(col_at <= row_at, inverse, 0.0) * scale,
    )


def factor128(a):
    n = a.shape[0] // 2
    r00, t00 = factor64(a[:n, :n])
    r01 = dot_n(t00, a[:n, n:])
    r11, t11 = factor64(a[n:, n:] - dot_t(r01, r01))
    t10 = -dot_n(t11, dot_n(r01.T, t00))
    none = jnp.zeros((n, n), F32)
    r = jnp.concatenate(
        [jnp.concatenate([r00, r01], axis=1), jnp.concatenate([none, r11], axis=1)], axis=0
    )
    t = jnp.concatenate(
        [jnp.concatenate([t00, none], axis=1), jnp.concatenate([t10, t11], axis=1)], axis=0
    )
    return r, t


def first_kernel(scale, g_ref, y_ref, r_out, t_out, z_out):
    r, t = factor128(g_ref[...])
    r_out[...] = r
    t_out[...] = t
    z_out[...] = dot_bt(y_ref[...], t)


def first(g, y, scale):
    return pl.pallas_call(
        functools.partial(first_kernel, scale),
        out_shape=(
            jax.ShapeDtypeStruct((HALF, HALF), F32),
            jax.ShapeDtypeStruct((HALF, HALF), F32),
            jax.ShapeDtypeStruct(y.shape, F32),
        ),
        compiler_params=pltpu.CompilerParams(vmem_limit_bytes=40 * 2**20),
        cost_estimate=pl.CostEstimate(
            flops=20 * 2**20 * 1000, bytes_accessed=8 * y.size, transcendentals=0
        ),
        name="first",
    )(g, y)


def last_kernel(scale, g_ref, r_ref, t_ref, z_ref, y_ref, basis_out, triangle_out):
    r01 = dot_n(t_ref[...], g_ref[pl.ds(0, HALF)])
    r11, t11 = factor128(g_ref[pl.ds(HALF, HALF)] - dot_t(r01, r01))
    z = z_ref[...]
    basis_out[:, pl.ds(0, HALF)] = z * scale
    basis_out[:, pl.ds(HALF, HALF)] = dot_bt(y_ref[...] - dot_n(z, r01), t11) * scale
    share = 1.0 / scale
    triangle_out[pl.ds(0, HALF), pl.ds(0, HALF)] = r_ref[...] * share
    triangle_out[pl.ds(0, HALF), pl.ds(HALF, HALF)] = r01 * share
    triangle_out[pl.ds(HALF, HALF), pl.ds(0, HALF)] = jnp.zeros((HALF, HALF), F32)
    triangle_out[pl.ds(HALF, HALF), pl.ds(HALF, HALF)] = r11 * share


def last(g, r, t, z, y, scale):
    return pl.pallas_call(
        functools.partial(last_kernel, scale),
        out_shape=(
            jax.ShapeDtypeStruct((y.shape[0], 2 * HALF), F32),
            jax.ShapeDtypeStruct((2 * HALF, 2 * HALF), F32),
        ),
        compiler_params=pltpu.CompilerParams(vmem_limit_bytes=40 * 2**20),
        name="last",
    )(g, r, t, z, y)


def sum_all(part):
    axes = ("row", "col")
    n = lax.axis_size("row") * lax.axis_size("col")
    height = part.shape[0]
    pieces = lax.all_to_all(part.reshape(n, height // n, HALF), axes, 0, 0, tiled=True)
    share = jnp.sum(pieces, axis=0, keepdims=True)
    copies = jnp.broadcast_to(share, (n, height // n, HALF))
    return lax.all_to_all(copies, axes, 0, 0, tiled=True).reshape(height, HALF)


def local(tile_values, tile_rows, tile_source, tile_slot, send_lists, basis_blocks):
    values = tile_values[:, 0]
    blocks = tile_rows[:, 0]
    slots = send_lists.shape[3]
    places = tile_source[:, 0] * slots + tile_slot[:, 0]
    lists = send_lists.reshape(-1)
    owned = basis_blocks[:, 0]
    rows, cols = lax.axis_size("row"), lax.axis_size("col")
    cells = BR_DEV * values.shape[1] * rows
    scale = float(cells) ** 0.5

    def product(half):
        arrived = lax.all_to_all(pack(lists, owned, half), "row", 0, 0, tiled=True)
        coded = tiles(places, blocks, values, arrived, cols, half)
        return lax.all_to_all(coded, "col", 0, 0, tiled=True)

    y0, g0 = gram(product(0), ())
    r, t, z = first(sum_all(g0), y0, scale)
    y1, g1 = gram(product(1), (y0,))
    return last(sum_all(g1), r, t, z, y1, scale)


def solution(mesh):
    return jax.shard_map(
        local,
        mesh=mesh,
        in_specs=(
            P("row", "col", None, None),
            P("row", "col"),
            P("row", "col"),
            P("row", "col"),
            P("row", "col", None, None),
            P("row", "col", None, None),
        ),
        out_specs=(P(("row", "col"), None), P()),
        check_vma=False,
    )
```

time: 1600 us -> 252 us (0.16); the launches traced: 1580 us -> 250 us
  local copies, waits for them, and re-layouts: 577 us -> 2.75 us
  matrix products: 233 us -> 0 us
  other arithmetic: 227 us -> 0.3 us
  loops' own time: 202 us -> 0 us
  waiting for transfers between devices: 313 us -> 117 us
  Pallas kernels: 0 us -> 83.5 us
  starting transfers between devices: 9.95 us -> 46.2 us
    dynamic_slice x768 -> x0, local copies, waits for them, and re-layouts: 504 us -> none  [the longest x256 190 us: row_fill(): target = lax.dynamic_index_in_dim(gram, j, 0, keepdims=False)]
    dot_general x772 -> x0, matrix products: 233 us -> none  [the longest x256 60.5 us: row_fill(): residue = target - jnp.dot(known, upper, precision=lax.Precision.HIGHEST)]
    another operation x2 -> x0, loops' own time: 202 us -> none  [the longest x1 189 us: upper_factor(): lax.fori_loop(0, width, row_fill, jnp.zeros((width, width), jnp.float32))]
    div x257 -> x0, other arithmetic: 164 us -> none  [the longest x256 163 us: row_step(): (unit - jnp.dot(row_now, inverse, precision=lax.Precision.HIGHEST)) / pivot]
    psum x1 -> x0, waiting for transfers between devices: 143 us -> none  [local(): summed = lax.psum(gram, ('row', 'col'))]
    pallas_call x0 -> x8, Pallas kernels: none -> 83.5 us  [the longest x2 46.8 us: tiles(): pl.pallas_call(tiles_kernel, grid_spec=pltpu.PrefetchScalarGridSpec(num_s...]
    reduce_scatter x1 -> x0, waiting for transfers between devices: 61.8 us -> none  [local(): lax.psum_scatter(partial_value, 'col', scatter_dimension=0, tiled=True)]
    dot_general x2 -> x0, local copies, waits for them, and re-layouts: 50.9 us -> none  [the longest x1 46.6 us: local(): jnp.einsum('tij,tjk->tik', values, chosen, preferred_element_type=jnp.flo...]
  transfers between devices with their start and end apart: 3 -> 8, of which waited for: 3 -> 6; matrix products, arithmetic and copies ran while one was open for 0% -> 0% of each run, Pallas kernels for 0% -> 26%
where the time goes in v1:
time: 252 us; the launch traced here: 250 us
  waiting for transfers between devices  117 us (46%)
  Pallas kernels  83.5 us (33%)
  starting transfers between devices  46.2 us (18%)
  local copies, waits for them, and re-layouts  2.75 us (1%)
    all_to_all x2, waiting for transfers between devices, product(): arrived = lax.all_to_all(pack(lists, owned, half), 'row', 0, 0, tiled=True)  77.1 us
    pallas_call x2, Pallas kernels, tiles(): pl.pallas_call(tiles_kernel, grid_spec=pltpu.PrefetchScalarGridSpec(num_s...  46.8 us
    all_to_all x2, waiting for transfers between devices, sum_all(): lax.all_to_all(part.reshape(n, height // n, HALF), axes, 0, 0, tiled=True)  17.8 us
    all_to_all x2, starting transfers between devices, product(): arrived = lax.all_to_all(pack(lists, owned, half), 'row', 0, 0, tiled=True)  16.8 us
    pallas_call x1, Pallas kernels, last(): pl.pallas_call(functools.partial(last_kernel, scale), out_shape=(jax.Shap...  13.8 us
    all_to_all x2, starting transfers between devices, sum_all(): lax.all_to_all(part.reshape(n, height // n, HALF), axes, 0, 0, tiled=True)  13 us
    all_to_all x2, waiting for transfers between devices, product(): return lax.all_to_all(coded, 'col', 0, 0, tiled=True)  12.2 us
    pallas_call x1, Pallas kernels, first(): pl.pallas_call(functools.partial(first_kernel, scale), out_shape=(jax.Sha...  12 us
  transfers between devices with their start and end apart: 8, of which 6 were waited for; matrix products, arithmetic and copies ran while one was open for 0% of the time, Pallas kernels for 26%

profile of v1, /device:TPU:1, one launch (start us, length us, event | category | flops | bytes accessed | tf_op | source)
XLA Modules:
  0.0 250.3 jit_solution(9919249209912207226)
XLA Ops:
  0.6 0.8 copy.10
  1.4 0.6 reshape.28.lists
  2.0 3.8 %pack0.1 = bf16[64,256,128]{2,1,0:T(8,128)(2,1)} custom-call(s32[64]{0:T(128)} %reshape.28.lists, bf16[8,256,256]{2,1,0:T(8,128)(2,1)} %bitcast.20), custom_call_target="tpu_custom_call" | custom-call | bytes 8388608 | tf_op jit(solution)/shard_map/pack0/pallas_call | solution.py:36
  5.8 9.7 %all-to-all-start = ((bf16[64,256,128]{2,1,0:T(8,128)(2,1)}), bf16[64,256,128]{2,1,0:T(8,128)(2,1)}, u32[]{:S(2)}, u32[]{:S(2)}) async-start(bf16[64,256,128]{2,1,0:T(8,128)(2,1)} %pack0.1), calls=%async_computation | async-start | bytes 8388608 | tf_op jit(solution)/shard_map/all_to_all | solution.py:281
  15.5 3.8 %pack1.1 = bf16[64,256,128]{2,1,0:T(8,128)(2,1)} custom-call(s32[64]{0:T(128)} %reshape.28.lists, bf16[8,256,256]{2,1,0:T(8,128)(2,1)} %bitcast.21), custom_call_target="tpu_custom_call" | custom-call | bytes 8388608 | tf_op jit(solution)/shard_map/pack1/pallas_call | solution.py:36
  19.3 0.0 copy-start.1
  19.3 0.0 copy-start.2
  19.3 0.0 copy-start
  19.3 48.4 %all-to-all-done.arrived = bf16[64,256,128]{2,1,0:T(8,128)(2,1)} async-done(((bf16[64,256,128]{2,1,0:T(8,128)(2,1)}), bf16[64,256,128]{2,1,0:T(8,128)(2,1)}, u32[]{:S(2)}, u32[]{:S(2)}) %all-to-all-start) | async-done | bytes 4194336 | tf_op jit(solution)/shard_map/all_to_all | solution.py:281
  67.7 7.2 %all-to-all-start.2 = ((bf16[64,256,128]{2,1,0:T(8,128)(2,1)}), bf16[64,256,128]{2,1,0:T(8,128)(2,1)}, u32[]{:S(2)}, u32[]{:S(2)}) async-start(bf16[64,256,128]{2,1,0:T(8,128)(2,1)} %pack1.1), calls=%async_computation.2 | async-start | bytes 8388608 | tf_op jit(solution)/shard_map/all_to_all | solution.py:281
  74.9 23.4 %tiles0.1 = s16[4,1040,128]{2,1,0:T(8,128)(2,1)} custom-call(s32[176]{0:T(256)S(1)} %bitcast.14, s32[176]{0:T(256)S(1)} %bitcast.16, bf16[176,256,256]{2,1,0:T(8,128)(2,1)} %bitcast.18, bf16[64,256,128]{2,1,0:T(8,128)(2,1)} %all-to-all-done.arrived), custom_call_target="tpu_custom_call" | custom-call | flops 2952790016 | bytes 27262976 | tf_op jit(solution)/shard_map/tiles0/pallas_call | solution.py:87
  98.3 28.7 %all-to-all-done.2.arrived = bf16[64,256,128]{2,1,0:T(8,128)(2,1)} async-done(((bf16[64,256,128]{2,1,0:T(8,128)(2,1)}), bf16[64,256,128]{2,1,0:T(8,128)(2,1)}, u32[]{:S(2)}, u32[]{:S(2)}) %all-to-all-start.2) | async-done | bytes 4194336 | tf_op jit(solution)/shard_map/all_to_all | solution.py:281
  127.1 4.0 %all-to-all-start.1 = ((s16[4,1040,128]{2,1,0:T(8,128)(2,1)}), s16[4,1040,128]{2,1,0:T(8,128)(2,1)S(1)}, u32[]{:S(2)}, u32[]{:S(2)}) async-start(s16[4,1040,128]{2,1,0:T(8,128)(2,1)} %tiles0.1), calls=%async_computation.1 | async-start | bytes 2129920 | tf_op jit(solution)/shard_map/all_to_all | solution.py:283
  131.1 23.4 %tiles1.1 = s16[4,1040,128]{2,1,0:T(8,128)(2,1)} custom-call(s32[176]{0:T(256)S(1)} %bitcast.15, s32[176]{0:T(256)S(1)} %bitcast.17, bf16[176,256,256]{2,1,0:T(8,128)(2,1)} %bitcast.19, bf16[64,256,128]{2,1,0:T(8,128)(2,1)} %all-to-all-done.2.arrived), custom_call_target="tpu_custom_call" | custom-call | flops 2952790016 | bytes 27262976 | tf_op jit(solution)/shard_map/tiles1/pallas_call | solution.py:87
  154.5 0.0 all-to-all-done.1.refs_0_
  154.5 4.2 %all-to-all-start.3 = ((s16[4,1040,128]{2,1,0:T(8,128)(2,1)}), s16[4,1040,128]{2,1,0:T(8,128)(2,1)S(1)}, u32[]{:S(2)}, u32[]{:S(2)}) async-start(s16[4,1040,128]{2,1,0:T(8,128)(2,1)} %tiles1.1), calls=%async_computation.3 | async-start | bytes 2129920 | tf_op jit(solution)/shard_map/all_to_all | solution.py:283
  158.7 1.4 gram0.1
  160.1 12.2 %all-to-all-done.3.refs_1_ = s16[4,1040,128]{2,1,0:T(8,128)(2,1)S(1)} async-done(((s16[4,1040,128]{2,1,0:T(8,128)(2,1)}), s16[4,1040,128]{2,1,0:T(8,128)(2,1)S(1)}, u32[]{:S(2)}, u32[]{:S(2)}) %all-to-all-start.3) | async-done | bytes 1064992 | tf_op jit(solution)/shard_map/all_to_all | solution.py:283
  172.3 8.9 %all-to-all-start.6 = ((f32[128,1,128]{2,1,0:T(1,128)}), f32[128,1,128]{2,1,0:T(1,128)S(1)}, u32[]{:S(2)}, u32[]{:S(2)}) async-start(f32[128,1,128]{2,1,0:T(1,128)} %bitcast.7), calls=%async_computation.6 | async-start | bytes 131072 | tf_op jit(solution)/shard_map/all_to_all | solution.py:263
  181.2 1.9 gram1.1
  183.1 7.9 %all-to-all-done.6 = f32[128,1,128]{2,1,0:T(1,128)S(1)} async-done(((f32[128,1,128]{2,1,0:T(1,128)}), f32[128,1,128]{2,1,0:T(1,128)S(1)}, u32[]{:S(2)}, u32[]{:S(2)}) %all-to-all-start.6) | async-done | bytes 65568 | tf_op jit(solution)/shard_map/all_to_all | solution.py:263
  191.1 4.1 %all-to-all-start.4 = ((f32[128,2,128]{2,1,0:T(2,128)}), f32[128,2,128]{2,1,0:T(2,128)S(1)}, u32[]{:S(2)}, u32[]{:S(2)}) async-start(f32[128,2,128]{2,1,0:T(2,128)} %bitcast.4), calls=%async_computation.4 | async-start | bytes 262144 | tf_op jit(solution)/shard_map/all_to_all | solution.py:263
  195.1 0.2 reduce_sum.19
  195.3 9.9 %all-to-all-done.4 = f32[128,2,128]{2,1,0:T(2,128)S(1)} async-done(((f32[128,2,128]{2,1,0:T(2,128)}), f32[128,2,128]{2,1,0:T(2,128)S(1)}, u32[]{:S(2)}, u32[]{:S(2)}) %all-to-all-start.4) | async-done | bytes 131104 | tf_op jit(solution)/shard_map/all_to_all | solution.py:263
  205.2 0.7 broadcast_in_dim.5
  205.8 4.1 %all-to-all-start.7 = ((f32[128,1,128]{2,1,0:T(1,128)}), f32[128,1,128]{2,1,0:T(1,128)S(1)}, u32[]{:S(2)}, u32[]{:S(2)}) async-start(f32[128,1,128]{2,1,0:T(1,128)} %broadcast_in_dim.5), calls=%async_computation.7 | async-start | bytes 131072 | tf_op jit(solution)/shard_map/all_to_all | solution.py:266
  209.9 0.1 reduce_sum.18
  210.1 9.7 %all-to-all-done.7 = f32[128,1,128]{2,1,0:T(1,128)S(1)} async-done(((f32[128,1,128]{2,1,0:T(1,128)}), f32[128,1,128]{2,1,0:T(1,128)S(1)}, u32[]{:S(2)}, u32[]{:S(2)}) %all-to-all-start.7) | async-done | bytes 65568 | tf_op jit(solution)/shard_map/all_to_all | solution.py:266
  219.7 0.7 broadcast_in_dim.4
  220.4 4.1 %all-to-all-start.5 = ((f32[128,2,128]{2,1,0:T(2,128)}), f32[128,2,128]{2,1,0:T(2,128)S(1)}, u32[]{:S(2)}, u32[]{:S(2)}) async-start(f32[128,2,128]{2,1,0:T(2,128)} %broadcast_in_dim.4), calls=%async_computation.5 | async-start | bytes 262144 | tf_op jit(solution)/shard_map/all_to_all | solution.py:266
  224.5 12.0 %first.1 = (f32[128,128]{1,0:T(8,128)S(1)}, f32[128,128]{1,0:T(8,128)S(1)}, f32[1024,128]{1,0:T(8,128)S(1)}) custom-call(f32[128,128]{1,0:T(8,128)S(1)} %bitcast.13, f32[1024,128]{1,0:T(8,128)S(1)} %get-tuple-element.9.refs_0_.y_ref), custom_call_target="tpu_custom_call" | custom-call | flops 20971520000 | bytes 1048576 | tf_op jit(solution)/shard_map/first/pallas_call | solution.py:219
  236.5 13.8 %last.1 = (f32[1024,256]{1,0:T(8,128)}, f32[256,256]{1,0:T(8,128)}) custom-call(f32[256,128]{1,0:T(8,128)S(1)} %bitcast.12, f32[128,128]{1,0:T(8,128)S(1)} %get-tuple-element.12.r_ref, f32[128,128]{1,0:T(8,128)S(1)} %get-tuple-element.13.t_ref, f32[1024,128]{1,0:T(8,128)S(1)} %get-tuple-element.14.z_ref, f32[1024,128]{1,0:T(8,128)S(1)} %get-tuple-element.15.y_ref), custom_call_target="tpu_custom_call" | custom-call | tf_op jit(solution)/shard_map/last/pallas_call | solution.py:248
  (5 shorter events, 0.0 us)
Async XLA Ops:
  5.8 61.9 %all-to-all-start = ((bf16[64,256,128]{2,1,0:T(8,128)(2,1)}), bf16[64,256,128]{2,1,0:T(8,128)(2,1)}, u32[]{:S(2)}, u32[]{:S(2)}) async-start(bf16[64,256,128]{2,1,0:T(8,128)(2,1)} %pack0.1), calls=%async_computation | async-start | bytes 8388608 | tf_op jit(solution)/shard_map/all_to_all | solution.py:281
  19.3 55.6 %copy-start.1 = (s32[176,1]{0,1:T(1,128)S(1)}, s32[176,1]{0,1:T(1,128)}, u32[]{:S(2)}) copy-start(s32[176,1]{0,1:T(1,128)} %param.9) | copy-start | bytes 2116
  19.3 55.6 %copy-start.2 = (s32[176,1]{0,1:T(1,128)S(1)}, s32[176,1]{0,1:T(1,128)}, u32[]{:S(2)}) copy-start(s32[176,1]{0,1:T(1,128)} %param.8) | copy-start | bytes 2116
  19.3 55.6 %copy-start = (s32[176,1]{0,1:T(1,128)S(1)}, s32[176,1]{0,1:T(1,128)}, u32[]{:S(2)}) copy-start(s32[176,1]{0,1:T(1,128)} %param.7) | copy-start | bytes 2116
  67.7 59.4 %all-to-all-start.2 = ((bf16[64,256,128]{2,1,0:T(8,128)(2,1)}), bf16[64,256,128]{2,1,0:T(8,128)(2,1)}, u32[]{:S(2)}, u32[]{:S(2)}) async-start(bf16[64,256,128]{2,1,0:T(8,128)(2,1)} %pack1.1), calls=%async_computation.2 | async-start | bytes 8388608 | tf_op jit(solution)/shard_map/all_to_all | solution.py:281
  127.1 27.4 %all-to-all-start.1 = ((s16[4,1040,128]{2,1,0:T(8,128)(2,1)}), s16[4,1040,128]{2,1,0:T(8,128)(2,1)S(1)}, u32[]{:S(2)}, u32[]{:S(2)}) async-start(s16[4,1040,128]{2,1,0:T(8,128)(2,1)} %tiles0.1), calls=%async_computation.1 | async-start | bytes 2129920 | tf_op jit(solution)/shard_map/all_to_all | solution.py:283
  154.5 17.8 %all-to-all-start.3 = ((s16[4,1040,128]{2,1,0:T(8,128)(2,1)}), s16[4,1040,128]{2,1,0:T(8,128)(2,1)S(1)}, u32[]{:S(2)}, u32[]{:S(2)}) async-start(s16[4,1040,128]{2,1,0:T(8,128)(2,1)} %tiles1.1), calls=%async_computation.3 | async-start | bytes 2129920 | tf_op jit(solution)/shard_map/all_to_all | solution.py:283
  172.3 18.7 %all-to-all-start.6 = ((f32[128,1,128]{2,1,0:T(1,128)}), f32[128,1,128]{2,1,0:T(1,128)S(1)}, u32[]{:S(2)}, u32[]{:S(2)}) async-start(f32[128,1,128]{2,1,0:T(1,128)} %bitcast.7), calls=%async_computation.6 | async-start | bytes 131072 | tf_op jit(solution)/shard_map/all_to_all | solution.py:263
  191.1 14.1 %all-to-all-start.4 = ((f32[128,2,128]{2,1,0:T(2,128)}), f32[128,2,128]{2,1,0:T(2,128)S(1)}, u32[]{:S(2)}, u32[]{:S(2)}) async-start(f32[128,2,128]{2,1,0:T(2,128)} %bitcast.4), calls=%async_computation.4 | async-start | bytes 262144 | tf_op jit(solution)/shard_map/all_to_all | solution.py:263
  205.8 13.9 %all-to-all-start.7 = ((f32[128,1,128]{2,1,0:T(1,128)}), f32[128,1,128]{2,1,0:T(1,128)S(1)}, u32[]{:S(2)}, u32[]{:S(2)}) async-start(f32[128,1,128]{2,1,0:T(1,128)} %broadcast_in_dim.5), calls=%async_computation.7 | async-start | bytes 131072 | tf_op jit(solution)/shard_map/all_to_all | solution.py:266
  220.4 16.1 %all-to-all-start.5 = ((f32[128,2,128]{2,1,0:T(2,128)}), f32[128,2,128]{2,1,0:T(2,128)S(1)}, u32[]{:S(2)}, u32[]{:S(2)}) async-start(f32[128,2,128]{2,1,0:T(2,128)} %broadcast_in_dim.4), calls=%async_computation.5 | async-start | bytes 262144 | tf_op jit(solution)/shard_map/all_to_all | solution.py:266

commit v2 on v1

--- a/solution.py
+++ b/solution.py
@@ -9,7 +9,8 @@
 
 BR_DEV = 16
 HALF = 128
-GROUP = 8
+GROUP = 88
+LOADS = 22
 STEP = 32704.0
 LEAST = 2.0**-80
 HIGHEST = lax.Precision.HIGHEST
@@ -56,55 +57,71 @@
     return steps.astype(jnp.int32).astype(jnp.int16), power
 
 
-def tiles_kernel(places, blocks, values, arrived, out, total):
-    step = pl.program_id(0)
-
-    @pl.when(step == 0)
-    def _():
-        total[...] = jnp.zeros_like(total)
-
-    for u in range(GROUP):
-        t = step * GROUP + u
-        total[blocks[t]] += jnp.dot(values[u], arrived[places[t]], preferred_element_type=F32)
-
-    @pl.when(step == pl.num_programs(0) - 1)
-    def _():
-        shares = out.shape[0]
-        each = BR_DEV // shares
-        for d in range(shares):
-            part = total[d * each : (d + 1) * each]
-            rows = each * part.shape[1]
-            steps, power = encode(part.reshape(rows, HALF))
-            out[d, pl.ds(0, rows)] = steps
-            out[d, pl.ds(rows, 16)] = (
-                jnp.broadcast_to(power, (16, HALF)).astype(jnp.int32).astype(jnp.int16)
-            )
-
-
-def tiles(places, blocks, values, arrived, shares, half):
+def tiles_kernel(shares, me, places, blocks, values_hbm, arrived_hbm, *refs):
+    *_, total, values, arrived, value_sems, arrived_sems = refs
+    outs = refs[-5 - shares : -5]
+    count, loads, parts = values.shape[0], value_sems.shape[0], arrived_sems.shape[0]
+
+    def bring(i):
+        part = pl.ds(i * (count // loads), count // loads)
+        return pltpu.make_async_copy(values_hbm.at[part], values.at[part], value_sems.at[i])
+
+    def bring_basis(i):
+        part = pl.ds(i * (arrived.shape[0] // parts), arrived.shape[0] // parts)
+        return pltpu.make_async_copy(arrived_hbm.at[part], arrived.at[part], arrived_sems.at[i])
+
+    for i in range(parts):
+        bring_basis(i).start()
+    for i in range(loads):
+        bring(i).start()
+    total[...] = jnp.zeros_like(total)
+    for i in range(parts):
+        bring_basis(i).wait()
+
+    @pl.loop(0, count // GROUP)
+    def _(step):
+        for i in range(loads * GROUP // count):
+            bring(step * (loads * GROUP // count) + i).wait()
+        for u in range(GROUP):
+            t = step * GROUP + u
+            total[blocks[t]] += jnp.dot(values[t], arrived[places[t]], preferred_element_type=F32)
+
+    each = BR_DEV // shares
+    rows = each * total.shape[1]
+    for k, out in enumerate(outs):
+        share = lax.rem(me[0] + k, shares)
+        steps, power = encode(total[pl.ds(share * each, each)].reshape(rows, HALF))
+        out[pl.ds(0, rows)] = steps
+        out[pl.ds(rows, 16)] = (
+            jnp.broadcast_to(power, (16, HALF)).astype(jnp.int32).astype(jnp.int16)
+        )
+
+
+def tiles(me, places, blocks, values, arrived, shares, half, after):
     count, height, depth = values.shape
     rows = BR_DEV * height // shares
-    return pl.pallas_call(
-        tiles_kernel,
-        grid_spec=pltpu.PrefetchScalarGridSpec(
-            num_scalar_prefetch=2,
-            grid=(count // GROUP,),
-            in_specs=[
-                pl.BlockSpec((GROUP, height, depth), lambda i, *_: (i, 0, 0)),
-                pl.BlockSpec(arrived.shape, lambda i, *_: (0, 0, 0)),
-            ],
-            out_specs=pl.BlockSpec((shares, rows + 16, HALF), lambda i, *_: (0, 0, 0)),
-            scratch_shapes=[pltpu.VMEM((BR_DEV, height, HALF), F32)],
-        ),
-        out_shape=jax.ShapeDtypeStruct((shares, rows + 16, HALF), jnp.int16),
-        compiler_params=pltpu.CompilerParams(vmem_limit_bytes=40 * 2**20),
+    inputs = [pl.BlockSpec(memory_space=pltpu.SMEM)] * 3
+    inputs += [pl.BlockSpec(memory_space=pl.ANY)] * (2 + len(after))
+    return pl.pallas_call(
+        functools.partial(tiles_kernel, shares),
+        in_specs=inputs,
+        out_specs=[pl.BlockSpec(memory_space=pltpu.VMEM)] * shares,
+        scratch_shapes=[
+            pltpu.VMEM((BR_DEV, height, HALF), F32),
+            pltpu.VMEM(values.shape, values.dtype),
+            pltpu.VMEM(arrived.shape, arrived.dtype),
+            pltpu.SemaphoreType.DMA((LOADS,)),
+            pltpu.SemaphoreType.DMA((4,)),
+        ],
+        out_shape=[jax.ShapeDtypeStruct((rows + 16, HALF), jnp.int16)] * shares,
+        compiler_params=pltpu.CompilerParams(vmem_limit_bytes=44 * 2**20),
         cost_estimate=pl.CostEstimate(
             flops=2 * count * height * depth * HALF,
             bytes_accessed=count * height * depth * 2 + arrived.size * 2,
             transcendentals=0,
         ),
         name=f"tiles{half}",
-    )(places, blocks, values, arrived)
+    )(me, places, blocks, values, arrived, *after)
 
 
 def dot_t(a, b):
@@ -123,20 +140,18 @@
     )
 
 
-def decode(ref):
-    shares, rows = ref.shape[0], ref.shape[1] - 16
+def decode(coded):
     y = None
-    for g in range(shares):
-        power = ref[g, pl.ds(rows, 16)].astype(jnp.int32).astype(F32)[0:1]
-        part = ref[g, pl.ds(0, rows)].astype(jnp.int32).astype(F32) * (
-            jnp.exp2(power) * (1.0 / STEP)
-        )
+    for ref in coded:
+        rows = ref.shape[0] - 16
+        power = ref[pl.ds(rows, 16)].astype(jnp.int32).astype(F32)[0:1]
+        part = ref[pl.ds(0, rows)].astype(jnp.int32).astype(F32) * (jnp.exp2(power) * (1.0 / STEP))
         y = part if y is None else y + part
     return y
 
 
-def gram_kernel(*refs):
-    (*before, coded, y_out, gram_out) = refs
+def gram_kernel(shares, *refs):
+    coded, before, (y_out, gram_out) = refs[:shares], refs[shares:-2], refs[-2:]
     y = decode(coded)
     y_out[...] = y
     at = 0
@@ -147,20 +162,20 @@
 
 
 def gram(coded, before):
-    rows = coded.shape[1] - 16
+    rows = coded[0].shape[0] - 16
     height = HALF * (len(before) + 1)
     return pl.pallas_call(
-        gram_kernel,
+        functools.partial(gram_kernel, len(coded)),
         out_shape=(
             jax.ShapeDtypeStruct((rows, HALF), F32),
             jax.ShapeDtypeStruct((height, HALF), F32),
         ),
-        compiler_params=pltpu.CompilerParams(vmem_limit_bytes=40 * 2**20),
+        compiler_params=pltpu.CompilerParams(vmem_limit_bytes=16 * 2**20),
         cost_estimate=pl.CostEstimate(
             flops=12 * rows * height * HALF, bytes_accessed=rows * HALF * 12, transcendentals=0
         ),
         name=f"gram{len(before)}",
-    )(*before, coded)
+    )(*coded, *before)
 
 
 def factor64(a):
@@ -223,7 +238,7 @@
             jax.ShapeDtypeStruct((HALF, HALF), F32),
             jax.ShapeDtypeStruct(y.shape, F32),
         ),
-        compiler_params=pltpu.CompilerParams(vmem_limit_bytes=40 * 2**20),
+        compiler_params=pltpu.CompilerParams(vmem_limit_bytes=16 * 2**20),
         cost_estimate=pl.CostEstimate(
             flops=20 * 2**20 * 1000, bytes_accessed=8 * y.size, transcendentals=0
         ),
@@ -251,7 +266,7 @@
             jax.ShapeDtypeStruct((y.shape[0], 2 * HALF), F32),
             jax.ShapeDtypeStruct((2 * HALF, 2 * HALF), F32),
         ),
-        compiler_params=pltpu.CompilerParams(vmem_limit_bytes=40 * 2**20),
+        compiler_params=pltpu.CompilerParams(vmem_limit_bytes=16 * 2**20),
         name="last",
     )(g, r, t, z, y)
 
@@ -264,6 +279,23 @@
     share = jnp.sum(pieces, axis=0, keepdims=True)
     copies = jnp.broadcast_to(share, (n, height // n, HALF))
     return lax.all_to_all(copies, axes, 0, 0, tiled=True).reshape(height, HALF)
+
+
+def sum_pairs(part):
+    rows, cols = lax.axis_size("row"), lax.axis_size("col")
+    steps = []
+    for axis, size, flip in (
+        ("row", rows, 1),
+        ("col", cols, 1),
+        ("col", cols, 3),
+        ("row", rows, 2),
+        ("row", rows, 6),
+        ("row", rows, 8),
+        ("row", rows, 24),
+    ):
+        part = part + lax.ppermute(part, axis, [(i, i ^ flip) for i in range(size)])
+        steps.append(part)
+    return steps
 
 
 def local(tile_values, tile_rows, tile_source, tile_slot, send_lists, basis_blocks):
@@ -276,15 +308,22 @@
     rows, cols = lax.axis_size("row"), lax.axis_size("col")
     cells = BR_DEV * values.shape[1] * rows
     scale = float(cells) ** 0.5
-
-    def product(half):
-        arrived = lax.all_to_all(pack(lists, owned, half), "row", 0, 0, tiled=True)
-        coded = tiles(places, blocks, values, arrived, cols, half)
-        return lax.all_to_all(coded, "col", 0, 0, tiled=True)
-
-    y0, g0 = gram(product(0), ())
-    r, t, z = first(sum_all(g0), y0, scale)
-    y1, g1 = gram(product(1), (y0,))
+    me = lax.axis_index("col").reshape(1)
+
+    packed = [pack(lists, owned, half) for half in range(2)]
+
+    def product(half, after):
+        arrived = lax.all_to_all(packed[half], "row", 0, 0, tiled=True)
+        own, *others = tiles(me, places, blocks, values, arrived, cols, half, after)
+        return [own] + [
+            lax.ppermute(other, "col", [(i, (i + k) % cols) for i in range(cols)])
+            for k, other in enumerate(others, 1)
+        ]
+
+    y0, g0 = gram(product(0, ()), ())
+    steps = sum_pairs(g0)
+    r, t, z = first(steps[-1], y0, scale)
+    y1, g1 = gram(product(1, (steps[4],)), (y0,))
     return last(sum_all(g1), r, t, z, y1, scale)
 
 

time: 252 us -> 213 us (0.85)
  waiting for transfers between devices: 117 us -> 88.2 us
  Pallas kernels: 83.5 us -> 68.9 us
  starting transfers between devices: 46.2 us -> 52.8 us
    all_to_all x4 -> x2, waiting for transfers between devices: 89.3 us -> 48.3 us  [product(): arrived = lax.all_to_all(packed[half], 'row', 0, 0, tiled=True)]
    ppermute x0 -> x13, waiting for transfers between devices: none -> 34.9 us  [the longest x6 19.2 us: product(): lax.ppermute(other, 'col', [(i, (i + k) % cols) for i in range(cols)])]
    ppermute x0 -> x13, starting transfers between devices: none -> 21.6 us  [the longest x7 11.5 us: sum_pairs(): part = part + lax.ppermute(part, axis, [(i, i ^ flip) for i in range(size)])]
    pallas_call x4, Pallas kernels: 50.1 us -> 35.5 us  [the longest x2 32.8 us: tiles(): pl.pallas_call(functools.partial(tiles_kernel, shares), in_specs=inputs,...]
    all_to_all x2 -> x1, waiting for transfers between devices: 17.8 us -> 4.97 us  [sum_all(): lax.all_to_all(part.reshape(n, height // n, HALF), axes, 0, 0, tiled=True)]
    all_to_all x2 -> x1, waiting for transfers between devices: 9.67 us -> 0.01 us  [sum_all(): return lax.all_to_all(copies, axes, 0, 0, tiled=True).reshape(height, HALF)]
    all_to_all x4 -> x2, starting transfers between devices: 25.1 us -> 16.8 us  [product(): arrived = lax.all_to_all(packed[half], 'row', 0, 0, tiled=True)]
    all_to_all x2 -> x1, starting transfers between devices: 13 us -> 9.21 us  [sum_all(): lax.all_to_all(part.reshape(n, height // n, HALF), axes, 0, 0, tiled=True)]
  transfers between devices with their start and end apart: 8 -> 17, of which waited for: 6 -> 12; matrix products, arithmetic and copies ran while one was open for 0% -> 0% of each run, Pallas kernels for 26% -> 16%
where the time goes in v2:
time: 213 us
  waiting for transfers between devices  88.2 us (41%)
  Pallas kernels  68.9 us (32%)
  starting transfers between devices  52.8 us (25%)
    all_to_all x2, waiting for transfers between devices, product(): arrived = lax.all_to_all(packed[half], 'row', 0, 0, tiled=True)  48.3 us
    pallas_call x2, Pallas kernels, tiles(): pl.pallas_call(functools.partial(tiles_kernel, shares), in_specs=inputs,...  32.8 us
    ppermute x6, waiting for transfers between devices, product(): lax.ppermute(other, 'col', [(i, (i + k) % cols) for i in range(cols)])  19.2 us
    all_to_all x2, starting transfers between devices, product(): arrived = lax.all_to_all(packed[half], 'row', 0, 0, tiled=True)  16.8 us
    ppermute x7, waiting for transfers between devices, sum_pairs(): part = part + lax.ppermute(part, axis, [(i, i ^ flip) for i in range(size)])  15.6 us
    pallas_call x1, Pallas kernels, last(): pl.pallas_call(functools.partial(last_kernel, scale), out_shape=(jax.Shap...  13.8 us
    pallas_call x1, Pallas kernels, first(): pl.pallas_call(functools.partial(first_kernel, scale), out_shape=(jax.Sha...  12 us
    ppermute x7, starting transfers between devices, sum_pairs(): part = part + lax.ppermute(part, axis, [(i, i ^ flip) for i in range(size)])  11.5 us
  transfers between devices with their start and end apart: 17, of which 12 were waited for; matrix products, arithmetic and copies ran while one was open for 0% of the time, Pallas kernels for 16%

profile of v2, /device:TPU:1, one launch (start us, length us, event | category | flops | bytes accessed | tf_op | source)
XLA Modules:
  0.0 213.0 jit_solution(12260849583025718606)
XLA Ops:
  2.0 3.8 %pack0.1 = bf16[64,256,128]{2,1,0:T(8,128)(2,1)} custom-call(s32[64]{0:T(128)} %reshape.21.lists, bf16[8,256,256]{2,1,0:T(8,128)(2,1)} %bitcast.16), custom_call_target="tpu_custom_call" | custom-call | bytes 8388608 | tf_op jit(solution)/shard_map/pack0/pallas_call | solution.py:37
  5.8 9.7 %all-to-all-start.1 = ((bf16[64,256,128]{2,1,0:T(8,128)(2,1)}), bf16[64,256,128]{2,1,0:T(8,128)(2,1)}, u32[]{:S(2)}, u32[]{:S(2)}) async-start(bf16[64,256,128]{2,1,0:T(8,128)(2,1)} %pack0.1), calls=%async_computation.1 | async-start | bytes 8388608 | tf_op jit(solution)/shard_map/all_to_all | solution.py:316
  15.5 3.8 %pack1.1 = bf16[64,256,128]{2,1,0:T(8,128)(2,1)} custom-call(s32[64]{0:T(128)} %reshape.21.lists, bf16[8,256,256]{2,1,0:T(8,128)(2,1)} %bitcast.17), custom_call_target="tpu_custom_call" | custom-call | bytes 8388608 | tf_op jit(solution)/shard_map/pack1/pallas_call | solution.py:37
  19.4 48.3 %all-to-all-done.1.arrived_hbm = bf16[64,256,128]{2,1,0:T(8,128)(2,1)} async-done(((bf16[64,256,128]{2,1,0:T(8,128)(2,1)}), bf16[64,256,128]{2,1,0:T(8,128)(2,1)}, u32[]{:S(2)}, u32[]{:S(2)}) %all-to-all-start.1) | async-done | bytes 4194336 | tf_op jit(solution)/shard_map/all_to_all | solution.py:316
  67.7 7.2 %all-to-all-start = ((bf16[64,256,128]{2,1,0:T(8,128)(2,1)}), bf16[64,256,128]{2,1,0:T(8,128)(2,1)}, u32[]{:S(2)}, u32[]{:S(2)}) async-start(bf16[64,256,128]{2,1,0:T(8,128)(2,1)} %pack1.1), calls=%async_computation | async-start | bytes 8388608 | tf_op jit(solution)/shard_map/all_to_all | solution.py:316
  74.9 16.4 %tiles0.1 = (s16[1040,128]{1,0:T(8,128)(2,1)S(1)}, s16[1040,128]{1,0:T(8,128)(2,1)S(1)}, s16[1040,128]{1,0:T(8,128)(2,1)S(1)}, s16[1040,128]{1,0:T(8,128)(2,1)S(1)}) custom-call(s32[1]{0:T(128)} %bitcast.me, s32[176]{0:T(256)S(1)} %bitcast.10, s32[176]{0:T(256)S(1)} %bitcast.12, bf16[176,256,256]{2,1,0:T(8,128)(2,1)} %bitcast.14, ...), custom_call_target="tpu_custom_call" | custom-call | flops 2952790016 | bytes 27262976 | tf_op jit(solution)/shard_map/tiles0/pallas_call | solution.py:105
  91.3 1.3 collective-permute-start
  92.6 2.5 %collective-permute-start.1 = (s16[1040,128]{1,0:T(8,128)(2,1)S(1)}, s16[1040,128]{1,0:T(8,128)(2,1)S(1)}, u32[]{:S(2)}, u32[]{:S(2)}) collective-permute-start(s16[1040,128]{1,0:T(8,128)(2,1)S(1)} %get-tuple-element.19), channel_id=1, source_target_pairs={{0,2},{1,3},{2,0},{3,1},{4,6},{5,7},{6,4},{7,5},{8,10},{9,11},{10,... | collective-permute-start | bytes 798728 | tf_op jit(solution)/shard_map/ppermute | solution.py:319
  95.1 1.1 collective-permute-start.2
  96.2 4.2 %collective-permute-done.refs_1_ = s16[1040,128]{1,0:T(8,128)(2,1)S(1)} collective-permute-done((s16[1040,128]{1,0:T(8,128)(2,1)S(1)}, s16[1040,128]{1,0:T(8,128)(2,1)S(1)}, u32[]{:S(2)}, u32[]{:S(2)}) %collective-permute-start) | collective-permute-done | bytes 266272 | tf_op jit(solution)/shard_map/ppermute | solution.py:319
  100.4 6.7 %collective-permute-done.1.refs_2_ = s16[1040,128]{1,0:T(8,128)(2,1)S(1)} collective-permute-done((s16[1040,128]{1,0:T(8,128)(2,1)S(1)}, s16[1040,128]{1,0:T(8,128)(2,1)S(1)}, u32[]{:S(2)}, u32[]{:S(2)}) %collective-permute-start.1) | collective-permute-done | bytes 266272 | tf_op jit(solution)/shard_map/ppermute | solution.py:319
  109.9 1.1 collective-permute-start.4
  111.0 2.5 %collective-permute-done.4 = f32[128,128]{1,0:T(8,128)S(1)} collective-permute-done((f32[128,128]{1,0:T(8,128)S(1)}, f32[128,128]{1,0:T(8,128)S(1)}, u32[]{:S(2)}, u32[]{:S(2)}) %collective-permute-start.4) | collective-permute-done | bytes 65568 | tf_op jit(solution)/shard_map/ppermute | solution.py:296
  113.5 2.1 collective-permute-start.5
  115.6 2.7 %collective-permute-done.5 = f32[128,128]{1,0:T(8,128)S(1)} collective-permute-done((f32[128,128]{1,0:T(8,128)S(1)}, f32[128,128]{1,0:T(8,128)S(1)}, u32[]{:S(2)}, u32[]{:S(2)}) %collective-permute-start.5) | collective-permute-done | bytes 65568 | tf_op jit(solution)/shard_map/ppermute | solution.py:296
  119.4 5.6 %collective-permute-done.6 = f32[128,128]{1,0:T(8,128)S(1)} collective-permute-done((f32[128,128]{1,0:T(8,128)S(1)}, f32[128,128]{1,0:T(8,128)S(1)}, u32[]{:S(2)}, u32[]{:S(2)}) %collective-permute-start.6) | collective-permute-done | bytes 65568 | tf_op jit(solution)/shard_map/ppermute | solution.py:296
  125.0 2.9 %collective-permute-start.7 = (f32[128,128]{1,0:T(8,128)S(1)}, f32[128,128]{1,0:T(8,128)S(1)}, u32[]{:S(2)}, u32[]{:S(2)}) collective-permute-start(f32[128,128]{1,0:T(8,128)S(1)} %add.31), channel_id=1, source_target_pairs={{0,24},{4,28},{8,16},{12,20},{16,8},{20,12},{24,0},{28,4},{32,56},... | collective-permute-start | bytes 196616 | tf_op jit(solution)/shard_map/ppermute | solution.py:296
  127.9 1.7 collective-permute-done.7
  129.6 16.4 %tiles1.1 = (s16[1040,128]{1,0:T(8,128)(2,1)S(1)}, s16[1040,128]{1,0:T(8,128)(2,1)S(1)}, s16[1040,128]{1,0:T(8,128)(2,1)S(1)}, s16[1040,128]{1,0:T(8,128)(2,1)S(1)}) custom-call(s32[1]{0:T(128)} %bitcast.me, s32[176]{0:T(256)S(1)} %bitcast.11, s32[176]{0:T(256)S(1)} %bitcast.13, bf16[176,256,256]{2,1,0:T(8,128)(2,1)} %bitcast.15, ...), custom_call_target="tpu_custom_call" | custom-call | flops 2952790016 | bytes 27262976 | tf_op jit(solution)/shard_map/tiles1/pallas_call | solution.py:105
  146.0 1.6 collective-permute-start.8
  147.6 2.4 %collective-permute-start.9 = (s16[1040,128]{1,0:T(8,128)(2,1)S(1)}, s16[1040,128]{1,0:T(8,128)(2,1)S(1)}, u32[]{:S(2)}, u32[]{:S(2)}) collective-permute-start(s16[1040,128]{1,0:T(8,128)(2,1)S(1)} %get-tuple-element.24), channel_id=1, source_target_pairs={{0,2},{1,3},{2,0},{3,1},{4,6},{5,7},{6,4},{7,5},{8,10},{9,11},{10,... | collective-permute-start | bytes 798728 | tf_op jit(solution)/shard_map/ppermute | solution.py:319
  150.0 1.2 collective-permute-start.10
  151.7 1.3 collective-permute-done.8.refs_1_
  153.0 7.1 %collective-permute-done.9.refs_2_ = s16[1040,128]{1,0:T(8,128)(2,1)S(1)} collective-permute-done((s16[1040,128]{1,0:T(8,128)(2,1)S(1)}, s16[1040,128]{1,0:T(8,128)(2,1)S(1)}, u32[]{:S(2)}, u32[]{:S(2)}) %collective-permute-start.9) | collective-permute-done | bytes 266272 | tf_op jit(solution)/shard_map/ppermute | solution.py:319
  160.1 1.9 gram1.1
  162.0 9.2 %all-to-all-start.2 = ((f32[128,2,128]{2,1,0:T(2,128)}), f32[128,2,128]{2,1,0:T(2,128)S(1)}, u32[]{:S(2)}, u32[]{:S(2)}) async-start(f32[128,2,128]{2,1,0:T(2,128)} %bitcast.5), calls=%async_computation.2 | async-start | bytes 262144 | tf_op jit(solution)/shard_map/all_to_all | solution.py:278
  171.2 2.7 %collective-permute-start.12 = (f32[128,128]{1,0:T(8,128)S(1)}, f32[128,128]{1,0:T(8,128)S(1)}, u32[]{:S(2)}, u32[]{:S(2)}) collective-permute-start(f32[128,128]{1,0:T(8,128)S(1)} %add.33), channel_id=1, source_target_pairs={{0,96},{4,100},{8,104},{12,108},{16,112},{20,116},{24,120},{28,124... | collective-permute-start | bytes 196616 | tf_op jit(solution)/shard_map/ppermute | solution.py:296
  174.0 2.3 %collective-permute-done.12 = f32[128,128]{1,0:T(8,128)S(1)} collective-permute-done((f32[128,128]{1,0:T(8,128)S(1)}, f32[128,128]{1,0:T(8,128)S(1)}, u32[]{:S(2)}, u32[]{:S(2)}) %collective-permute-start.12) | collective-permute-done | bytes 65568 | tf_op jit(solution)/shard_map/ppermute | solution.py:296
  176.3 5.0 %all-to-all-done.2 = f32[128,2,128]{2,1,0:T(2,128)S(1)} async-done(((f32[128,2,128]{2,1,0:T(2,128)}), f32[128,2,128]{2,1,0:T(2,128)S(1)}, u32[]{:S(2)}, u32[]{:S(2)}) %all-to-all-start.2) | async-done | bytes 131104 | tf_op jit(solution)/shard_map/all_to_all | solution.py:278
  182.1 5.1 %all-to-all-start.3 = ((f32[128,2,128]{2,1,0:T(2,128)}), f32[128,2,128]{2,1,0:T(2,128)S(1)}, u32[]{:S(2)}, u32[]{:S(2)}) async-start(f32[128,2,128]{2,1,0:T(2,128)} %broadcast_in_dim.2), calls=%async_computation.3 | async-start | bytes 262144 | tf_op jit(solution)/shard_map/all_to_all | solution.py:281
  187.2 12.0 %first.1 = (f32[128,128]{1,0:T(8,128)S(1)}, f32[128,128]{1,0:T(8,128)S(1)}, f32[1024,128]{1,0:T(8,128)S(1)}) custom-call(f32[128,128]{1,0:T(8,128)S(1)} %add.34.g_ref, f32[1024,128]{1,0:T(8,128)S(1)} %get-tuple-element.26.refs_4_.y_ref), custom_call_target="tpu_custom_call" | custom-call | flops 20971520000 | bytes 1048576 | tf_op jit(solution)/shard_map/first/pallas_call | solution.py:234
  199.2 13.8 %last.1 = (f32[1024,256]{1,0:T(8,128)}, f32[256,256]{1,0:T(8,128)}) custom-call(f32[256,128]{1,0:T(8,128)S(1)} %bitcast.9, f32[128,128]{1,0:T(8,128)S(1)} %get-tuple-element.28.r_ref, f32[128,128]{1,0:T(8,128)S(1)} %get-tuple-element.29.t_ref, f32[1024,128]{1,0:T(8,128)S(1)} %get-tuple-element.30.z_ref, f32[1024,128]{1,0:T(8,128)S(1)} %get-tuple-element.31.y_ref), custom_call_target="tpu_custom_call" | custom-call | tf_op jit(solution)/shard_map/last/pallas_call | solution.py:263
  (28 shorter events, 6.7 us)
Async XLA Ops:
  5.8 61.9 %all-to-all-start.1 = ((bf16[64,256,128]{2,1,0:T(8,128)(2,1)}), bf16[64,256,128]{2,1,0:T(8,128)(2,1)}, u32[]{:S(2)}, u32[]{:S(2)}) async-start(bf16[64,256,128]{2,1,0:T(8,128)(2,1)} %pack0.1), calls=%async_computation.1 | async-start | bytes 8388608 | tf_op jit(solution)/shard_map/all_to_all | solution.py:316
  19.3 55.6 %copy-start.1 = (s32[176,1]{0,1:T(1,128)S(1)}, s32[176,1]{0,1:T(1,128)}, u32[]{:S(2)}) copy-start(s32[176,1]{0,1:T(1,128)} %param.9) | copy-start | bytes 2116
  19.3 55.6 %copy-start.2 = (s32[176,1]{0,1:T(1,128)S(1)}, s32[176,1]{0,1:T(1,128)}, u32[]{:S(2)}) copy-start(s32[176,1]{0,1:T(1,128)} %param.8) | copy-start | bytes 2116
  19.4 55.6 %copy-start = (s32[176,1]{0,1:T(1,128)S(1)}, s32[176,1]{0,1:T(1,128)}, u32[]{:S(2)}) copy-start(s32[176,1]{0,1:T(1,128)} %param.7) | copy-start | bytes 2116
  67.7 61.9 %all-to-all-start = ((bf16[64,256,128]{2,1,0:T(8,128)(2,1)}), bf16[64,256,128]{2,1,0:T(8,128)(2,1)}, u32[]{:S(2)}, u32[]{:S(2)}) async-start(bf16[64,256,128]{2,1,0:T(8,128)(2,1)} %pack1.1), calls=%async_computation | async-start | bytes 8388608 | tf_op jit(solution)/shard_map/all_to_all | solution.py:316
  91.3 9.1 %collective-permute-start = (s16[1040,128]{1,0:T(8,128)(2,1)S(1)}, s16[1040,128]{1,0:T(8,128)(2,1)S(1)}, u32[]{:S(2)}, u32[]{:S(2)}) collective-permute-start(s16[1040,128]{1,0:T(8,128)(2,1)S(1)} %get-tuple-element.18), channel_id=1, source_target_pairs={{0,1},{1,2},{2,3},{3,0},{4,5},{5,6},{6,7},{7,4},{8,9},{9,10},{10,1... | collective-permute-start | bytes 798728 | tf_op jit(solution)/shard_map/ppermute | solution.py:319
  92.6 14.5 %collective-permute-start.1 = (s16[1040,128]{1,0:T(8,128)(2,1)S(1)}, s16[1040,128]{1,0:T(8,128)(2,1)S(1)}, u32[]{:S(2)}, u32[]{:S(2)}) collective-permute-start(s16[1040,128]{1,0:T(8,128)(2,1)S(1)} %get-tuple-element.19), channel_id=1, source_target_pairs={{0,2},{1,3},{2,0},{3,1},{4,6},{5,7},{6,4},{7,5},{8,10},{9,11},{10,... | collective-permute-start | bytes 798728 | tf_op jit(solution)/shard_map/ppermute | solution.py:319
  95.1 12.0 %collective-permute-start.2 = (s16[1040,128]{1,0:T(8,128)(2,1)S(1)}, s16[1040,128]{1,0:T(8,128)(2,1)S(1)}, u32[]{:S(2)}, u32[]{:S(2)}) collective-permute-start(s16[1040,128]{1,0:T(8,128)(2,1)S(1)} %get-tuple-element.20), channel_id=1, source_target_pairs={{0,3},{1,0},{2,1},{3,2},{4,7},{5,4},{6,5},{7,6},{8,11},{9,8},{10,9... | collective-permute-start | bytes 798728 | tf_op jit(solution)/shard_map/ppermute | solution.py:319
  107.9 2.0 collective-permute-start.3
  109.9 3.6 %collective-permute-start.4 = (f32[128,128]{1,0:T(8,128)S(1)}, f32[128,128]{1,0:T(8,128)S(1)}, u32[]{:S(2)}, u32[]{:S(2)}) collective-permute-start(f32[128,128]{1,0:T(8,128)S(1)} %add.28), channel_id=1, source_target_pairs={{0,1},{1,0},{2,3},{3,2},{4,5},{5,4},{6,7},{7,6},{8,9},{9,8},{10,11... | collective-permute-start | bytes 196616 | tf_op jit(solution)/shard_map/ppermute | solution.py:296
  113.5 4.8 %collective-permute-start.5 = (f32[128,128]{1,0:T(8,128)S(1)}, f32[128,128]{1,0:T(8,128)S(1)}, u32[]{:S(2)}, u32[]{:S(2)}) collective-permute-start(f32[128,128]{1,0:T(8,128)S(1)} %add.29), channel_id=1, source_target_pairs={{0,3},{1,2},{2,1},{3,0},{4,7},{5,6},{6,5},{7,4},{8,11},{9,10},{10,... | collective-permute-start | bytes 196616 | tf_op jit(solution)/shard_map/ppermute | solution.py:296
  118.3 6.7 %collective-permute-start.6 = (f32[128,128]{1,0:T(8,128)S(1)}, f32[128,128]{1,0:T(8,128)S(1)}, u32[]{:S(2)}, u32[]{:S(2)}) collective-permute-start(f32[128,128]{1,0:T(8,128)S(1)} %add.30), channel_id=1, source_target_pairs={{0,8},{4,12},{8,0},{12,4},{16,24},{20,28},{24,16},{28,20},{32,40},... | collective-permute-start | bytes 196616 | tf_op jit(solution)/shard_map/ppermute | solution.py:296
  125.0 4.6 %collective-permute-start.7 = (f32[128,128]{1,0:T(8,128)S(1)}, f32[128,128]{1,0:T(8,128)S(1)}, u32[]{:S(2)}, u32[]{:S(2)}) collective-permute-start(f32[128,128]{1,0:T(8,128)S(1)} %add.31), channel_id=1, source_target_pairs={{0,24},{4,28},{8,16},{12,20},{16,8},{20,12},{24,0},{28,4},{32,56},... | collective-permute-start | bytes 196616 | tf_op jit(solution)/shard_map/ppermute | solution.py:296
  146.0 7.0 %collective-permute-start.8 = (s16[1040,128]{1,0:T(8,128)(2,1)S(1)}, s16[1040,128]{1,0:T(8,128)(2,1)S(1)}, u32[]{:S(2)}, u32[]{:S(2)}) collective-permute-start(s16[1040,128]{1,0:T(8,128)(2,1)S(1)} %get-tuple-element.23), channel_id=1, source_target_pairs={{0,1},{1,2},{2,3},{3,0},{4,5},{5,6},{6,7},{7,4},{8,9},{9,10},{10,1... | collective-permute-start | bytes 798728 | tf_op jit(solution)/shard_map/ppermute | solution.py:319
  147.6 12.5 %collective-permute-start.9 = (s16[1040,128]{1,0:T(8,128)(2,1)S(1)}, s16[1040,128]{1,0:T(8,128)(2,1)S(1)}, u32[]{:S(2)}, u32[]{:S(2)}) collective-permute-start(s16[1040,128]{1,0:T(8,128)(2,1)S(1)} %get-tuple-element.24), channel_id=1, source_target_pairs={{0,2},{1,3},{2,0},{3,1},{4,6},{5,7},{6,4},{7,5},{8,10},{9,11},{10,... | collective-permute-start | bytes 798728 | tf_op jit(solution)/shard_map/ppermute | solution.py:319
  150.0 10.1 %collective-permute-start.10 = (s16[1040,128]{1,0:T(8,128)(2,1)S(1)}, s16[1040,128]{1,0:T(8,128)(2,1)S(1)}, u32[]{:S(2)}, u32[]{:S(2)}) collective-permute-start(s16[1040,128]{1,0:T(8,128)(2,1)S(1)} %get-tuple-element.25), channel_id=1, source_target_pairs={{0,3},{1,0},{2,1},{3,2},{4,7},{5,4},{6,5},{7,6},{8,11},{9,8},{10,9... | collective-permute-start | bytes 798728 | tf_op jit(solution)/shard_map/ppermute | solution.py:319
  151.2 20.0 %collective-permute-start.11 = (f32[128,128]{1,0:T(8,128)S(1)}, f32[128,128]{1,0:T(8,128)S(1)}, u32[]{:S(2)}, u32[]{:S(2)}) collective-permute-start(f32[128,128]{1,0:T(8,128)S(1)} %add.32.refs_0_), channel_id=1, source_target_pairs={{0,32},{4,36},{8,40},{12,44},{16,48},{20,52},{24,56},{28,60},{32,0... | collective-permute-start | bytes 196616 | tf_op jit(solution)/shard_map/ppermute | solution.py:296
  162.0 19.3 %all-to-all-start.2 = ((f32[128,2,128]{2,1,0:T(2,128)}), f32[128,2,128]{2,1,0:T(2,128)S(1)}, u32[]{:S(2)}, u32[]{:S(2)}) async-start(f32[128,2,128]{2,1,0:T(2,128)} %bitcast.5), calls=%async_computation.2 | async-start | bytes 262144 | tf_op jit(solution)/shard_map/all_to_all | solution.py:278
  171.2 5.0 %collective-permute-start.12 = (f32[128,128]{1,0:T(8,128)S(1)}, f32[128,128]{1,0:T(8,128)S(1)}, u32[]{:S(2)}, u32[]{:S(2)}) collective-permute-start(f32[128,128]{1,0:T(8,128)S(1)} %add.33), channel_id=1, source_target_pairs={{0,96},{4,100},{8,104},{12,108},{16,112},{20,116},{24,120},{28,124... | collective-permute-start | bytes 196616 | tf_op jit(solution)/shard_map/ppermute | solution.py:296
  182.1 17.1 %all-to-all-start.3 = ((f32[128,2,128]{2,1,0:T(2,128)}), f32[128,2,128]{2,1,0:T(2,128)S(1)}, u32[]{:S(2)}, u32[]{:S(2)}) async-start(f32[128,2,128]{2,1,0:T(2,128)} %broadcast_in_dim.2), calls=%async_computation.3 | async-start | bytes 262144 | tf_op jit(solution)/shard_map/all_to_all | solution.py:281

commit v3 on v2

--- a/solution.py
+++ b/solution.py
@@ -186,17 +186,42 @@
     wide = jnp.concatenate([a, unit], axis=1)
     strips = [wide[8 * i : 8 * i + 8] for i in range(n // 8)]
     in_strip = lax.broadcasted_iota(jnp.int32, (8, 2 * n), 0)
-    for j in range(n):
+    for j in range(0, n, 4):
         b, r = divmod(j, 8)
-        row = strips[b][r : r + 1]
-        scaled = row / row[:, j : j + 1]
+        rows = [strips[b][r + i : r + i + 1] for i in range(4)]
+
+        def entry(i, k, rows=rows, j=j):
+            return jnp.broadcast_to(rows[i][:, j + k : j + k + 1], (1, 2 * n))
+
+        p00, p01, p02, p03 = (entry(0, k) for k in range(4))
+        p11, p12, p13 = (entry(1, k) for k in range(1, 4))
+        p22, p23, p33 = entry(2, 2), entry(2, 3), entry(3, 3)
+        share = 1.0 / (p00 * p11 - p01 * p01)
+        w02, w12 = (p11 * p02 - p01 * p12) * share, (p00 * p12 - p01 * p02) * share
+        w03, w13 = (p11 * p03 - p01 * p13) * share, (p00 * p13 - p01 * p03) * share
+        q22 = p22 - (p02 * w02 + p12 * w12)
+        q23 = p23 - (p02 * w03 + p12 * w13)
+        q33 = p33 - (p03 * w03 + p13 * w13)
+        rest = 1.0 / (q22 * q33 - q23 * q23)
+        row2 = rows[2] - (w02 * rows[0] + w12 * rows[1])
+        row3 = rows[3] - (w03 * rows[0] + w13 * rows[1])
+        s2 = (q33 * row2 - q23 * row3) * rest
+        s3 = (q22 * row3 - q23 * row2) * rest
+        s0 = (p11 * rows[0] - p01 * rows[1]) * share - (w02 * s2 + w03 * s3)
+        s1 = (p00 * rows[1] - p01 * rows[0]) * share - (w12 * s2 + w13 * s3)
+        kept = (rows[1] - (p01 / p00) * rows[0], row2, row3 - (q23 / q22) * row2)
         for i in range(b, n // 8):
-            if i == b and r == 7:
-                continue
-            column = jnp.broadcast_to(strips[i][:, j : j + 1], (8, 2 * n))
+            new = strips[i]
+            if i > b or r < 4:
+                c0, c1, c2, c3 = (
+                    jnp.broadcast_to(strips[i][:, j + k : j + k + 1], (8, 2 * n)) for k in range(4)
+                )
+                new = new - ((c0 * s0 + c1 * s1) + (c2 * s2 + c3 * s3))
             if i == b:
-                column = jnp.where(in_strip > r, column, 0.0)
-            strips[i] = strips[i] - column * scaled
+                new = jnp.where(in_strip > r + 3, new, strips[i])
+                for k, row in enumerate(kept, 1):
+                    new = jnp.where(in_strip == r + k, row, new)
+            strips[i] = new
     wide = jnp.concatenate(strips, axis=0)
     square, inverse = wide[:, :n], wide[:, n:]
     pivots = jnp.sum(jnp.where(row_at == col_at, square, 0.0), axis=1, keepdims=True)
@@ -209,6 +234,15 @@
 
 def factor128(a):
     n = a.shape[0] // 2
+    row_at = lax.broadcasted_iota(jnp.int32, a.shape, 0)
+    col_at = lax.broadcasted_iota(jnp.int32, a.shape, 1)
+    diagonal = jnp.where(row_at == col_at, a, 0.0)
+
+    def level(squares):
+        return jnp.exp2(-jnp.floor(0.5 * jnp.log2(squares)))
+
+    along = level(jnp.sum(diagonal, axis=0, keepdims=True))
+    a = a * along * level(jnp.sum(diagonal, axis=1, keepdims=True))
     r00, t00 = factor64(a[:n, :n])
     r01 = dot_n(t00, a[:n, n:])
     r11, t11 = factor64(a[n:, n:] - dot_t(r01, r01))
@@ -220,7 +254,7 @@
     t = jnp.concatenate(
         [jnp.concatenate([t00, none], axis=1), jnp.concatenate([t10, t11], axis=1)], axis=0
     )
-    return r, t
+    return r * (1.0 / along), t * along
 
 
 def first_kernel(scale, g_ref, y_ref, r_out, t_out, z_out):
@@ -251,7 +285,10 @@
     r11, t11 = factor128(g_ref[pl.ds(HALF, HALF)] - dot_t(r01, r01))
     z = z_ref[...]
     basis_out[:, pl.ds(0, HALF)] = z * scale
-    basis_out[:, pl.ds(HALF, HALF)] = dot_bt(y_ref[...] - dot_n(z, r01), t11) * scale
+    basis_out[:, pl.ds(HALF, HALF)] = dot_bt(
+        jnp.concatenate([y_ref[...], z], axis=1),
+        jnp.concatenate([t11, -dot_bt(t11, r01)], axis=1) * scale,
+    )
     share = 1.0 / scale
     triangle_out[pl.ds(0, HALF), pl.ds(0, HALF)] = r_ref[...] * share
     triangle_out[pl.ds(0, HALF), pl.ds(HALF, HALF)] = r01 * share
@@ -281,19 +318,30 @@
     return lax.all_to_all(copies, axes, 0, 0, tiled=True).reshape(height, HALF)
 
 
-def sum_pairs(part):
+def sum_along(part):
     rows, cols = lax.axis_size("row"), lax.axis_size("col")
     steps = []
-    for axis, size, flip in (
-        ("row", rows, 1),
-        ("col", cols, 1),
-        ("col", cols, 3),
-        ("row", rows, 2),
-        ("row", rows, 6),
-        ("row", rows, 8),
-        ("row", rows, 24),
+    for axis, size, stride, length in (
+        ("row", rows, 1, 2),
+        ("col", cols, 1, cols),
+        ("row", rows, 8, 4),
+        ("row", rows, 2, 4),
     ):
-        part = part + lax.ppermute(part, axis, [(i, i ^ flip) for i in range(size)])
+        arrived = [
+            lax.ppermute(
+                part,
+                axis,
+                [
+                    (i, i + ((i // stride + k) % length - i // stride % length) * stride)
+                    for i in range(size)
+                ],
+            )
+            for k in range(1, length)
+        ]
+        if length == 2:
+            part = part + arrived[0]
+        else:
+            part = (part + arrived[1]) + (arrived[0] + arrived[2])
         steps.append(part)
     return steps
 
@@ -321,9 +369,9 @@
         ]
 
     y0, g0 = gram(product(0, ()), ())
-    steps = sum_pairs(g0)
+    steps = sum_along(g0)
     r, t, z = first(steps[-1], y0, scale)
-    y1, g1 = gram(product(1, (steps[4],)), (y0,))
+    y1, g1 = gram(product(1, (steps[2],)), (y0,))
     return last(sum_all(g1), r, t, z, y1, scale)
 
 

time: 213 us -> 206 us (0.967)
  Pallas kernels: 68.9 us -> 57.3 us
  waiting for transfers between devices: 88.2 us -> 91.2 us
    pallas_call x1, Pallas kernels: 12 us -> 5.96 us  [first(): pl.pallas_call(functools.partial(first_kernel, scale), out_shape=(jax.Sha...]
    pallas_call x1, Pallas kernels: 13.8 us -> 8.2 us  [last(): pl.pallas_call(functools.partial(last_kernel, scale), out_shape=(jax.Shap...]
    all_to_all x1, waiting for transfers between devices: 4.97 us -> 10 us  [sum_all(): lax.all_to_all(part.reshape(n, height // n, HALF), axes, 0, 0, tiled=True)]
    all_to_all x1, waiting for transfers between devices: 0.01 us -> 4.09 us  [sum_all(): return lax.all_to_all(copies, axes, 0, 0, tiled=True).reshape(height, HALF)]
    ppermute x7 -> x10, waiting for transfers between devices: 15.6 us -> 12.5 us  [sum_along(): lax.ppermute(part, axis, [(i, i + ((i // stride + k) % length - i // stri...]
    ppermute x6, waiting for transfers between devices: 19.2 us -> 16.3 us  [product(): lax.ppermute(other, 'col', [(i, (i + k) % cols) for i in range(cols)])]
    ppermute x7 -> x10, starting transfers between devices: 11.5 us -> 14.1 us  [sum_along(): lax.ppermute(part, axis, [(i, i + ((i // stride + k) % length - i // stri...]
  transfers between devices with their start and end apart: 17 -> 20, of which waited for: 12 -> 13; matrix products, arithmetic and copies ran while one was open for 0% -> 0% of each run, Pallas kernels for 16% -> 14%
where the time goes in v3:
time: 206 us
  waiting for transfers between devices  91.2 us (44%)
  Pallas kernels  57.3 us (28%)
  starting transfers between devices  54.3 us (26%)
  local copies, waits for them, and re-layouts  2.09 us (1%)
    all_to_all x2, waiting for transfers between devices, product(): arrived = lax.all_to_all(packed[half], 'row', 0, 0, tiled=True)  48.3 us
    pallas_call x2, Pallas kernels, tiles(): pl.pallas_call(functools.partial(tiles_kernel, shares), in_specs=inputs,...  32.8 us
    all_to_all x2, starting transfers between devices, product(): arrived = lax.all_to_all(packed[half], 'row', 0, 0, tiled=True)  16.8 us
    ppermute x6, waiting for transfers between devices, product(): lax.ppermute(other, 'col', [(i, (i + k) % cols) for i in range(cols)])  16.3 us
    ppermute x10, starting transfers between devices, sum_along(): lax.ppermute(part, axis, [(i, i + ((i // stride + k) % length - i // stri...  14.1 us
    ppermute x10, waiting for transfers between devices, sum_along(): lax.ppermute(part, axis, [(i, i + ((i // stride + k) % length - i // stri...  12.5 us
    all_to_all x1, waiting for transfers between devices, sum_all(): lax.all_to_all(part.reshape(n, height // n, HALF), axes, 0, 0, tiled=True)  10 us
    ppermute x6, starting transfers between devices, product(): lax.ppermute(other, 'col', [(i, (i + k) % cols) for i in range(cols)])  9.77 us
  transfers between devices with their start and end apart: 20, of which 13 were waited for; matrix products, arithmetic and copies ran while one was open for 0% of the time, Pallas kernels for 14%

profile of v3, /device:TPU:1, one launch (start us, length us, event | category | flops | bytes accessed | tf_op | source)
XLA Modules:
  0.0 205.9 jit_solution(11347041013478288280)
XLA Ops:
  2.0 3.8 %pack0.1 = bf16[64,256,128]{2,1,0:T(8,128)(2,1)} custom-call(s32[64]{0:T(128)} %reshape.21.lists, bf16[8,256,256]{2,1,0:T(8,128)(2,1)} %bitcast.16), custom_call_target="tpu_custom_call" | custom-call | bytes 8388608 | tf_op jit(solution)/shard_map/pack0/pallas_call | solution.py:37
  5.8 9.7 %all-to-all-start.1 = ((bf16[64,256,128]{2,1,0:T(8,128)(2,1)}), bf16[64,256,128]{2,1,0:T(8,128)(2,1)}, u32[]{:S(2)}, u32[]{:S(2)}) async-start(bf16[64,256,128]{2,1,0:T(8,128)(2,1)} %pack0.1), calls=%async_computation.1 | async-start | bytes 8388608 | tf_op jit(solution)/shard_map/all_to_all | solution.py:364
  15.5 3.8 %pack1.1 = bf16[64,256,128]{2,1,0:T(8,128)(2,1)} custom-call(s32[64]{0:T(128)} %reshape.21.lists, bf16[8,256,256]{2,1,0:T(8,128)(2,1)} %bitcast.17), custom_call_target="tpu_custom_call" | custom-call | bytes 8388608 | tf_op jit(solution)/shard_map/pack1/pallas_call | solution.py:37
  19.4 48.3 %all-to-all-done.1.arrived_hbm = bf16[64,256,128]{2,1,0:T(8,128)(2,1)} async-done(((bf16[64,256,128]{2,1,0:T(8,128)(2,1)}), bf16[64,256,128]{2,1,0:T(8,128)(2,1)}, u32[]{:S(2)}, u32[]{:S(2)}) %all-to-all-start.1) | async-done | bytes 4194336 | tf_op jit(solution)/shard_map/all_to_all | solution.py:364
  67.7 7.2 %all-to-all-start = ((bf16[64,256,128]{2,1,0:T(8,128)(2,1)}), bf16[64,256,128]{2,1,0:T(8,128)(2,1)}, u32[]{:S(2)}, u32[]{:S(2)}) async-start(bf16[64,256,128]{2,1,0:T(8,128)(2,1)} %pack1.1), calls=%async_computation | async-start | bytes 8388608 | tf_op jit(solution)/shard_map/all_to_all | solution.py:364
  74.9 16.4 %tiles0.1 = (s16[1040,128]{1,0:T(8,128)(2,1)S(1)}, s16[1040,128]{1,0:T(8,128)(2,1)S(1)}, s16[1040,128]{1,0:T(8,128)(2,1)S(1)}, s16[1040,128]{1,0:T(8,128)(2,1)S(1)}) custom-call(s32[1]{0:T(128)} %bitcast.me, s32[176]{0:T(256)S(1)} %bitcast.10, s32[176]{0:T(256)S(1)} %bitcast.12, bf16[176,256,256]{2,1,0:T(8,128)(2,1)} %bitcast.14, ...), custom_call_target="tpu_custom_call" | custom-call | flops 2952790016 | bytes 27262976 | tf_op jit(solution)/shard_map/tiles0/pallas_call | solution.py:105
  91.3 1.3 collective-permute-start
  92.6 2.4 %collective-permute-start.1 = (s16[1040,128]{1,0:T(8,128)(2,1)S(1)}, s16[1040,128]{1,0:T(8,128)(2,1)S(1)}, u32[]{:S(2)}, u32[]{:S(2)}) collective-permute-start(s16[1040,128]{1,0:T(8,128)(2,1)S(1)} %get-tuple-element.19), channel_id=1, source_target_pairs={{0,2},{1,3},{2,0},{3,1},{4,6},{5,7},{6,4},{7,5},{8,10},{9,11},{10,... | collective-permute-start | bytes 798728 | tf_op jit(solution)/shard_map/ppermute | solution.py:367
  95.1 1.2 collective-permute-start.2
  96.2 4.2 %collective-permute-done.refs_1_ = s16[1040,128]{1,0:T(8,128)(2,1)S(1)} collective-permute-done((s16[1040,128]{1,0:T(8,128)(2,1)S(1)}, s16[1040,128]{1,0:T(8,128)(2,1)S(1)}, u32[]{:S(2)}, u32[]{:S(2)}) %collective-permute-start) | collective-permute-done | bytes 266272 | tf_op jit(solution)/shard_map/ppermute | solution.py:367
  100.4 6.7 %collective-permute-done.1.refs_2_ = s16[1040,128]{1,0:T(8,128)(2,1)S(1)} collective-permute-done((s16[1040,128]{1,0:T(8,128)(2,1)S(1)}, s16[1040,128]{1,0:T(8,128)(2,1)S(1)}, u32[]{:S(2)}, u32[]{:S(2)}) %collective-permute-start.1) | collective-permute-done | bytes 266272 | tf_op jit(solution)/shard_map/ppermute | solution.py:367
  109.9 2.1 collective-permute-start.6
  112.0 1.9 collective-permute-start.4
  113.8 3.3 %collective-permute-done.5 = f32[128,128]{1,0:T(8,128)S(1)} collective-permute-done((f32[128,128]{1,0:T(8,128)S(1)}, f32[128,128]{1,0:T(8,128)S(1)}, u32[]{:S(2)}, u32[]{:S(2)}) %collective-permute-start.5) | collective-permute-done | bytes 65568 | tf_op jit(solution)/shard_map/ppermute | solution.py:331
  117.7 2.7 %collective-permute-start.9 = (f32[128,128]{1,0:T(8,128)S(1)}, f32[128,128]{1,0:T(8,128)S(1)}, u32[]{:S(2)}, u32[]{:S(2)}) collective-permute-start(f32[128,128]{1,0:T(8,128)S(1)} %add_add_fusion.2), channel_id=1, source_target_pairs={{0,96},{4,100},{8,104},{12,108},{16,112},{20,116},{24,120},{28,124... | collective-permute-start | bytes 196616 | tf_op jit(solution)/shard_map/ppermute | solution.py:331
  120.4 1.7 collective-permute-start.7
  122.1 5.1 %collective-permute-done.9 = f32[128,128]{1,0:T(8,128)S(1)} collective-permute-done((f32[128,128]{1,0:T(8,128)S(1)}, f32[128,128]{1,0:T(8,128)S(1)}, u32[]{:S(2)}, u32[]{:S(2)}) %collective-permute-start.9) | collective-permute-done | bytes 65568 | tf_op jit(solution)/shard_map/ppermute | solution.py:331
  127.2 1.9 collective-permute-done.8
  129.9 16.4 %tiles1.1 = (s16[1040,128]{1,0:T(8,128)(2,1)S(1)}, s16[1040,128]{1,0:T(8,128)(2,1)S(1)}, s16[1040,128]{1,0:T(8,128)(2,1)S(1)}, s16[1040,128]{1,0:T(8,128)(2,1)S(1)}) custom-call(s32[1]{0:T(128)} %bitcast.me, s32[176]{0:T(256)S(1)} %bitcast.11, s32[176]{0:T(256)S(1)} %bitcast.13, bf16[176,256,256]{2,1,0:T(8,128)(2,1)} %bitcast.15, ...), custom_call_target="tpu_custom_call" | custom-call | flops 2952790016 | bytes 27262976 | tf_op jit(solution)/shard_map/tiles1/pallas_call | solution.py:105
  146.3 1.3 collective-permute-start.10
  147.6 2.5 %collective-permute-start.11 = (s16[1040,128]{1,0:T(8,128)(2,1)S(1)}, s16[1040,128]{1,0:T(8,128)(2,1)S(1)}, u32[]{:S(2)}, u32[]{:S(2)}) collective-permute-start(s16[1040,128]{1,0:T(8,128)(2,1)S(1)} %get-tuple-element.24), channel_id=1, source_target_pairs={{0,2},{1,3},{2,0},{3,1},{4,6},{5,7},{6,4},{7,5},{8,10},{9,11},{10,... | collective-permute-start | bytes 798728 | tf_op jit(solution)/shard_map/ppermute | solution.py:367
  150.0 1.2 collective-permute-start.12
  151.8 2.5 %collective-permute-start.14 = (f32[128,128]{1,0:T(8,128)S(1)}, f32[128,128]{1,0:T(8,128)S(1)}, u32[]{:S(2)}, u32[]{:S(2)}) collective-permute-start(f32[128,128]{1,0:T(8,128)S(1)} %add_add_fusion.1.refs_0_), channel_id=1, source_target_pairs={{0,8},{4,12},{8,16},{12,20},{16,24},{20,28},{24,0},{28,4},{32,40},... | collective-permute-start | bytes 196616 | tf_op jit(solution)/shard_map/ppermute | solution.py:331
  154.6 1.5 collective-permute-start.13
  156.1 5.2 %collective-permute-done.11.refs_2_ = s16[1040,128]{1,0:T(8,128)(2,1)S(1)} collective-permute-done((s16[1040,128]{1,0:T(8,128)(2,1)S(1)}, s16[1040,128]{1,0:T(8,128)(2,1)S(1)}, u32[]{:S(2)}, u32[]{:S(2)}) %collective-permute-start.11) | collective-permute-done | bytes 266272 | tf_op jit(solution)/shard_map/ppermute | solution.py:367
  161.3 1.9 gram1.1
  163.2 9.5 %all-to-all-start.2 = ((f32[128,2,128]{2,1,0:T(2,128)}), f32[128,2,128]{2,1,0:T(2,128)S(1)}, u32[]{:S(2)}, u32[]{:S(2)}) async-start(f32[128,2,128]{2,1,0:T(2,128)} %bitcast.5), calls=%async_computation.2 | async-start | bytes 262144 | tf_op jit(solution)/shard_map/all_to_all | solution.py:315
  172.8 10.0 %all-to-all-done.2 = f32[128,2,128]{2,1,0:T(2,128)S(1)} async-done(((f32[128,2,128]{2,1,0:T(2,128)}), f32[128,2,128]{2,1,0:T(2,128)S(1)}, u32[]{:S(2)}, u32[]{:S(2)}) %all-to-all-start.2) | async-done | bytes 131104 | tf_op jit(solution)/shard_map/all_to_all | solution.py:315
  183.6 4.1 %all-to-all-start.3 = ((f32[128,2,128]{2,1,0:T(2,128)}), f32[128,2,128]{2,1,0:T(2,128)S(1)}, u32[]{:S(2)}, u32[]{:S(2)}) async-start(f32[128,2,128]{2,1,0:T(2,128)} %broadcast_in_dim.2), calls=%async_computation.3 | async-start | bytes 262144 | tf_op jit(solution)/shard_map/all_to_all | solution.py:318
  187.7 6.0 %first.1 = (f32[128,128]{1,0:T(8,128)S(1)}, f32[128,128]{1,0:T(8,128)S(1)}, f32[1024,128]{1,0:T(8,128)S(1)}) custom-call(f32[128,128]{1,0:T(8,128)S(1)} %add_add_fusion.g_ref, f32[1024,128]{1,0:T(8,128)S(1)} %get-tuple-element.26.refs_4_.y_ref), custom_call_target="tpu_custom_call" | custom-call | flops 20971520000 | bytes 1048576 | tf_op jit(solution)/shard_map/first/pallas_call | solution.py:268
  193.6 4.1 %all-to-all-done.3 = f32[128,2,128]{2,1,0:T(2,128)S(1)} async-done(((f32[128,2,128]{2,1,0:T(2,128)}), f32[128,2,128]{2,1,0:T(2,128)S(1)}, u32[]{:S(2)}, u32[]{:S(2)}) %all-to-all-start.3) | async-done | bytes 131104 | tf_op jit(solution)/shard_map/all_to_all | solution.py:318
  197.7 8.2 %last.1 = (f32[1024,256]{1,0:T(8,128)}, f32[256,256]{1,0:T(8,128)}) custom-call(f32[256,128]{1,0:T(8,128)S(1)} %bitcast.9, f32[128,128]{1,0:T(8,128)S(1)} %get-tuple-element.28.r_ref, f32[128,128]{1,0:T(8,128)S(1)} %get-tuple-element.29.t_ref, f32[1024,128]{1,0:T(8,128)S(1)} %get-tuple-element.30.z_ref, f32[1024,128]{1,0:T(8,128)S(1)} %get-tuple-element.31.y_ref), custom_call_target="tpu_custom_call" | custom-call | tf_op jit(solution)/shard_map/last/pallas_call | solution.py:300
  (31 shorter events, 7.4 us)
Async XLA Ops:
  5.8 61.9 %all-to-all-start.1 = ((bf16[64,256,128]{2,1,0:T(8,128)(2,1)}), bf16[64,256,128]{2,1,0:T(8,128)(2,1)}, u32[]{:S(2)}, u32[]{:S(2)}) async-start(bf16[64,256,128]{2,1,0:T(8,128)(2,1)} %pack0.1), calls=%async_computation.1 | async-start | bytes 8388608 | tf_op jit(solution)/shard_map/all_to_all | solution.py:364
  19.3 55.5 %copy-start.1 = (s32[176,1]{0,1:T(1,128)S(1)}, s32[176,1]{0,1:T(1,128)}, u32[]{:S(2)}) copy-start(s32[176,1]{0,1:T(1,128)} %param.9) | copy-start | bytes 2116
  19.3 55.5 %copy-start.2 = (s32[176,1]{0,1:T(1,128)S(1)}, s32[176,1]{0,1:T(1,128)}, u32[]{:S(2)}) copy-start(s32[176,1]{0,1:T(1,128)} %param.8) | copy-start | bytes 2116
  19.4 55.6 %copy-start = (s32[176,1]{0,1:T(1,128)S(1)}, s32[176,1]{0,1:T(1,128)}, u32[]{:S(2)}) copy-start(s32[176,1]{0,1:T(1,128)} %param.7) | copy-start | bytes 2116
  67.7 62.2 %all-to-all-start = ((bf16[64,256,128]{2,1,0:T(8,128)(2,1)}), bf16[64,256,128]{2,1,0:T(8,128)(2,1)}, u32[]{:S(2)}, u32[]{:S(2)}) async-start(bf16[64,256,128]{2,1,0:T(8,128)(2,1)} %pack1.1), calls=%async_computation | async-start | bytes 8388608 | tf_op jit(solution)/shard_map/all_to_all | solution.py:364
  91.3 9.1 %collective-permute-start = (s16[1040,128]{1,0:T(8,128)(2,1)S(1)}, s16[1040,128]{1,0:T(8,128)(2,1)S(1)}, u32[]{:S(2)}, u32[]{:S(2)}) collective-permute-start(s16[1040,128]{1,0:T(8,128)(2,1)S(1)} %get-tuple-element.18), channel_id=1, source_target_pairs={{0,1},{1,2},{2,3},{3,0},{4,5},{5,6},{6,7},{7,4},{8,9},{9,10},{10,1... | collective-permute-start | bytes 798728 | tf_op jit(solution)/shard_map/ppermute | solution.py:367
  92.6 14.5 %collective-permute-start.1 = (s16[1040,128]{1,0:T(8,128)(2,1)S(1)}, s16[1040,128]{1,0:T(8,128)(2,1)S(1)}, u32[]{:S(2)}, u32[]{:S(2)}) collective-permute-start(s16[1040,128]{1,0:T(8,128)(2,1)S(1)} %get-tuple-element.19), channel_id=1, source_target_pairs={{0,2},{1,3},{2,0},{3,1},{4,6},{5,7},{6,4},{7,5},{8,10},{9,11},{10,... | collective-permute-start | bytes 798728 | tf_op jit(solution)/shard_map/ppermute | solution.py:367
  95.1 12.0 %collective-permute-start.2 = (s16[1040,128]{1,0:T(8,128)(2,1)S(1)}, s16[1040,128]{1,0:T(8,128)(2,1)S(1)}, u32[]{:S(2)}, u32[]{:S(2)}) collective-permute-start(s16[1040,128]{1,0:T(8,128)(2,1)S(1)} %get-tuple-element.20), channel_id=1, source_target_pairs={{0,3},{1,0},{2,1},{3,2},{4,7},{5,4},{6,5},{7,6},{8,11},{9,8},{10,9... | collective-permute-start | bytes 798728 | tf_op jit(solution)/shard_map/ppermute | solution.py:367
  107.9 2.0 collective-permute-start.3
  109.9 3.9 %collective-permute-start.6 = (f32[128,128]{1,0:T(8,128)S(1)}, f32[128,128]{1,0:T(8,128)S(1)}, u32[]{:S(2)}, u32[]{:S(2)}) collective-permute-start(f32[128,128]{1,0:T(8,128)S(1)} %add.37), channel_id=1, source_target_pairs={{0,3},{1,0},{2,1},{3,2},{4,7},{5,4},{6,5},{7,6},{8,11},{9,8},{10,9... | collective-permute-start | bytes 196616 | tf_op jit(solution)/shard_map/ppermute | solution.py:331
  112.0 5.1 %collective-permute-start.5 = (f32[128,128]{1,0:T(8,128)S(1)}, f32[128,128]{1,0:T(8,128)S(1)}, u32[]{:S(2)}, u32[]{:S(2)}) collective-permute-start(f32[128,128]{1,0:T(8,128)S(1)} %add.37), channel_id=1, source_target_pairs={{0,1},{1,2},{2,3},{3,0},{4,5},{5,6},{6,7},{7,4},{8,9},{9,10},{10,1... | collective-permute-start | bytes 196616 | tf_op jit(solution)/shard_map/ppermute | solution.py:331
  112.0 5.7 %collective-permute-start.4 = (f32[128,128]{1,0:T(8,128)S(1)}, f32[128,128]{1,0:T(8,128)S(1)}, u32[]{:S(2)}, u32[]{:S(2)}) collective-permute-start(f32[128,128]{1,0:T(8,128)S(1)} %add.37), channel_id=1, source_target_pairs={{0,2},{1,3},{2,0},{3,1},{4,6},{5,7},{6,4},{7,5},{8,10},{9,11},{10,... | collective-permute-start | bytes 196616 | tf_op jit(solution)/shard_map/ppermute | solution.py:331
  117.7 9.5 %collective-permute-start.9 = (f32[128,128]{1,0:T(8,128)S(1)}, f32[128,128]{1,0:T(8,128)S(1)}, u32[]{:S(2)}, u32[]{:S(2)}) collective-permute-start(f32[128,128]{1,0:T(8,128)S(1)} %add_add_fusion.2), channel_id=1, source_target_pairs={{0,96},{4,100},{8,104},{12,108},{16,112},{20,116},{24,120},{28,124... | collective-permute-start | bytes 196616 | tf_op jit(solution)/shard_map/ppermute | solution.py:331
  120.4 8.7 %collective-permute-start.8 = (f32[128,128]{1,0:T(8,128)S(1)}, f32[128,128]{1,0:T(8,128)S(1)}, u32[]{:S(2)}, u32[]{:S(2)}) collective-permute-start(f32[128,128]{1,0:T(8,128)S(1)} %add_add_fusion.2), channel_id=1, source_target_pairs={{0,32},{4,36},{8,40},{12,44},{16,48},{20,52},{24,56},{28,60},{32,6... | collective-permute-start | bytes 196616 | tf_op jit(solution)/shard_map/ppermute | solution.py:331
  120.4 9.4 %collective-permute-start.7 = (f32[128,128]{1,0:T(8,128)S(1)}, f32[128,128]{1,0:T(8,128)S(1)}, u32[]{:S(2)}, u32[]{:S(2)}) collective-permute-start(f32[128,128]{1,0:T(8,128)S(1)} %add_add_fusion.2), channel_id=1, source_target_pairs={{0,64},{4,68},{8,72},{12,76},{16,80},{20,84},{24,88},{28,92},{32,9... | collective-permute-start | bytes 196616 | tf_op jit(solution)/shard_map/ppermute | solution.py:331
  146.3 8.3 %collective-permute-start.10 = (s16[1040,128]{1,0:T(8,128)(2,1)S(1)}, s16[1040,128]{1,0:T(8,128)(2,1)S(1)}, u32[]{:S(2)}, u32[]{:S(2)}) collective-permute-start(s16[1040,128]{1,0:T(8,128)(2,1)S(1)} %get-tuple-element.23), channel_id=1, source_target_pairs={{0,1},{1,2},{2,3},{3,0},{4,5},{5,6},{6,7},{7,4},{8,9},{9,10},{10,1... | collective-permute-start | bytes 798728 | tf_op jit(solution)/shard_map/ppermute | solution.py:367
  147.6 13.7 %collective-permute-start.11 = (s16[1040,128]{1,0:T(8,128)(2,1)S(1)}, s16[1040,128]{1,0:T(8,128)(2,1)S(1)}, u32[]{:S(2)}, u32[]{:S(2)}) collective-permute-start(s16[1040,128]{1,0:T(8,128)(2,1)S(1)} %get-tuple-element.24), channel_id=1, source_target_pairs={{0,2},{1,3},{2,0},{3,1},{4,6},{5,7},{6,4},{7,5},{8,10},{9,11},{10,... | collective-permute-start | bytes 798728 | tf_op jit(solution)/shard_map/ppermute | solution.py:367
  150.0 11.3 %collective-permute-start.12 = (s16[1040,128]{1,0:T(8,128)(2,1)S(1)}, s16[1040,128]{1,0:T(8,128)(2,1)S(1)}, u32[]{:S(2)}, u32[]{:S(2)}) collective-permute-start(s16[1040,128]{1,0:T(8,128)(2,1)S(1)} %get-tuple-element.25), channel_id=1, source_target_pairs={{0,3},{1,0},{2,1},{3,2},{4,7},{5,4},{6,5},{7,6},{8,11},{9,8},{10,9... | collective-permute-start | bytes 798728 | tf_op jit(solution)/shard_map/ppermute | solution.py:367
  151.2 21.5 %collective-permute-start.15 = (f32[128,128]{1,0:T(8,128)S(1)}, f32[128,128]{1,0:T(8,128)S(1)}, u32[]{:S(2)}, u32[]{:S(2)}) collective-permute-start(f32[128,128]{1,0:T(8,128)S(1)} %add_add_fusion.1.refs_0_), channel_id=1, source_target_pairs={{0,24},{4,28},{8,0},{12,4},{16,8},{20,12},{24,16},{28,20},{32,56},... | collective-permute-start | bytes 196616 | tf_op jit(solution)/shard_map/ppermute | solution.py:331
  151.8 20.9 %collective-permute-start.14 = (f32[128,128]{1,0:T(8,128)S(1)}, f32[128,128]{1,0:T(8,128)S(1)}, u32[]{:S(2)}, u32[]{:S(2)}) collective-permute-start(f32[128,128]{1,0:T(8,128)S(1)} %add_add_fusion.1.refs_0_), channel_id=1, source_target_pairs={{0,8},{4,12},{8,16},{12,20},{16,24},{20,28},{24,0},{28,4},{32,40},... | collective-permute-start | bytes 196616 | tf_op jit(solution)/shard_map/ppermute | solution.py:331
  154.6 18.1 %collective-permute-start.13 = (f32[128,128]{1,0:T(8,128)S(1)}, f32[128,128]{1,0:T(8,128)S(1)}, u32[]{:S(2)}, u32[]{:S(2)}) collective-permute-start(f32[128,128]{1,0:T(8,128)S(1)} %add_add_fusion.1.refs_0_), channel_id=1, source_target_pairs={{0,16},{4,20},{8,24},{12,28},{16,0},{20,4},{24,8},{28,12},{32,48},... | collective-permute-start | bytes 196616 | tf_op jit(solution)/shard_map/ppermute | solution.py:331
  163.2 19.6 %all-to-all-start.2 = ((f32[128,2,128]{2,1,0:T(2,128)}), f32[128,2,128]{2,1,0:T(2,128)S(1)}, u32[]{:S(2)}, u32[]{:S(2)}) async-start(f32[128,2,128]{2,1,0:T(2,128)} %bitcast.5), calls=%async_computation.2 | async-start | bytes 262144 | tf_op jit(solution)/shard_map/all_to_all | solution.py:315
  183.6 14.1 %all-to-all-start.3 = ((f32[128,2,128]{2,1,0:T(2,128)}), f32[128,2,128]{2,1,0:T(2,128)S(1)}, u32[]{:S(2)}, u32[]{:S(2)}) async-start(f32[128,2,128]{2,1,0:T(2,128)} %broadcast_in_dim.2), calls=%async_computation.3 | async-start | bytes 262144 | tf_op jit(solution)/shard_map/all_to_all | solution.py:318

commit v4 on v3

--- a/solution.py
+++ b/solution.py
@@ -9,8 +9,8 @@
 
 BR_DEV = 16
 HALF = 128
-GROUP = 88
-LOADS = 22
+GROUP = 22
+LOADS = 8
 STEP = 32704.0
 LEAST = 2.0**-80
 HIGHEST = lax.Precision.HIGHEST
@@ -18,11 +18,13 @@
 
 
 def pack_kernel(half, lists, owned, out, sems):
-    count = out.shape[0]
+    count, slots = out.shape[0], lists.shape[0]
 
     def one(i):
         return pltpu.make_async_copy(
-            owned.at[lists[i], :, pl.ds(half * HALF, HALF)], out.at[i], sems.at[i]
+            owned.at[lists[i % slots, i // slots], :, pl.ds(half * HALF, HALF)],
+            out.at[i],
+            sems.at[i],
         )
 
     for i in range(count):
@@ -32,7 +34,7 @@
 
 
 def pack(lists, owned, half):
-    count = lists.shape[0]
+    count = lists.size
     height = owned.shape[1]
     return pl.pallas_call(
         functools.partial(pack_kernel, half),
@@ -61,6 +63,7 @@
     *_, total, values, arrived, value_sems, arrived_sems = refs
     outs = refs[-5 - shares : -5]
     count, loads, parts = values.shape[0], value_sems.shape[0], arrived_sems.shape[0]
+    assert count % GROUP == 0 and loads * GROUP % count == 0 and count % loads == 0
 
     def bring(i):
         part = pl.ds(i * (count // loads), count // loads)
@@ -351,7 +354,7 @@
     blocks = tile_rows[:, 0]
     slots = send_lists.shape[3]
     places = tile_source[:, 0] * slots + tile_slot[:, 0]
-    lists = send_lists.reshape(-1)
+    lists = send_lists[0, 0].T
     owned = basis_blocks[:, 0]
     rows, cols = lax.axis_size("row"), lax.axis_size("col")
     cells = BR_DEV * values.shape[1] * rows
@@ -362,16 +365,16 @@
 
     def product(half, after):
         arrived = lax.all_to_all(packed[half], "row", 0, 0, tiled=True)
-        own, *others = tiles(me, places, blocks, values, arrived, cols, half, after)
-        return [own] + [
-            lax.ppermute(other, "col", [(i, (i + k) % cols) for i in range(cols)])
-            for k, other in enumerate(others, 1)
+        coded = tiles(me, places, blocks, values, arrived, cols, half, after)
+        return [coded[0]] + [
+            lax.ppermute(coded[k], "col", [(i, (i + k) % cols) for i in range(cols)])
+            for k in sorted(range(1, cols), key=lambda k: -min(k, cols - k))
         ]
 
     y0, g0 = gram(product(0, ()), ())
     steps = sum_along(g0)
     r, t, z = first(steps[-1], y0, scale)
-    y1, g1 = gram(product(1, (steps[2],)), (y0,))
+    y1, g1 = gram(product(1, (steps[1],)), (y0,))
     return last(sum_all(g1), r, t, z, y1, scale)
 
 

time: 206 us -> 202 us (0.981)
  waiting for transfers between devices: 91.2 us -> 87.5 us
    ppermute x10, waiting for transfers between devices: 12.5 us -> 5.97 us  [sum_along(): lax.ppermute(part, axis, [(i, i + ((i // stride + k) % length - i // stri...]
    all_to_all x2, waiting for transfers between devices: 48.3 us -> 52.5 us  [product(): arrived = lax.all_to_all(packed[half], 'row', 0, 0, tiled=True)]
  transfers between devices with their start and end apart: 20 -> 20, of which waited for: 13 -> 10; matrix products, arithmetic and copies ran while one was open for 0% -> 0% of each run, Pallas kernels for 14% -> 23%
where the time goes in v4:
time: 202 us
  waiting for transfers between devices  87.5 us (43%)
  Pallas kernels  57.9 us (29%)
  starting transfers between devices  54.4 us (27%)
    all_to_all x2, waiting for transfers between devices, product(): arrived = lax.all_to_all(packed[half], 'row', 0, 0, tiled=True)  52.5 us
    pallas_call x2, Pallas kernels, tiles(): pl.pallas_call(functools.partial(tiles_kernel, shares), in_specs=inputs,...  33.4 us
    all_to_all x2, starting transfers between devices, product(): arrived = lax.all_to_all(packed[half], 'row', 0, 0, tiled=True)  16.8 us
    ppermute x6, waiting for transfers between devices, product(): lax.ppermute(coded[k], 'col', [(i, (i + k) % cols) for i in range(cols)])  14.9 us
    ppermute x10, starting transfers between devices, sum_along(): lax.ppermute(part, axis, [(i, i + ((i // stride + k) % length - i // stri...  13.8 us
    ppermute x6, starting transfers between devices, product(): lax.ppermute(coded[k], 'col', [(i, (i + k) % cols) for i in range(cols)])  11 us
    all_to_all x1, waiting for transfers between devices, sum_all(): lax.all_to_all(part.reshape(n, height // n, HALF), axes, 0, 0, tiled=True)  10 us
    all_to_all x1, starting transfers between devices, sum_all(): lax.all_to_all(part.reshape(n, height // n, HALF), axes, 0, 0, tiled=True)  8.65 us
  transfers between devices with their start and end apart: 20, of which 10 were waited for; matrix products, arithmetic and copies ran while one was open for 0% of the time, Pallas kernels for 23%

profile of v4, /device:TPU:1, one launch (start us, length us, event | category | flops | bytes accessed | tf_op | source)
XLA Modules:
  0.0 201.5 jit_solution(13102075203954244561)
XLA Ops:
  0.6 3.8 %pack0.1 = bf16[64,256,128]{2,1,0:T(8,128)(2,1)} custom-call(s32[2,32]{1,0:T(2,128)} %bitcast.19, bf16[8,256,256]{2,1,0:T(8,128)(2,1)} %bitcast.17), custom_call_target="tpu_custom_call" | custom-call | bytes 8388608 | tf_op jit(solution)/shard_map/pack0/pallas_call | solution.py:39
  4.4 9.7 %all-to-all-start.1 = ((bf16[64,256,128]{2,1,0:T(8,128)(2,1)}), bf16[64,256,128]{2,1,0:T(8,128)(2,1)}, u32[]{:S(2)}, u32[]{:S(2)}) async-start(bf16[64,256,128]{2,1,0:T(8,128)(2,1)} %pack0.1), calls=%async_computation.1 | async-start | bytes 8388608 | tf_op jit(solution)/shard_map/all_to_all | solution.py:367
  14.1 3.8 %pack1.1 = bf16[64,256,128]{2,1,0:T(8,128)(2,1)} custom-call(s32[2,32]{1,0:T(2,128)} %bitcast.20, bf16[8,256,256]{2,1,0:T(8,128)(2,1)} %bitcast.18), custom_call_target="tpu_custom_call" | custom-call | bytes 8388608 | tf_op jit(solution)/shard_map/pack1/pallas_call | solution.py:39
  18.0 48.3 %all-to-all-done.1.arrived_hbm = bf16[64,256,128]{2,1,0:T(8,128)(2,1)} async-done(((bf16[64,256,128]{2,1,0:T(8,128)(2,1)}), bf16[64,256,128]{2,1,0:T(8,128)(2,1)}, u32[]{:S(2)}, u32[]{:S(2)}) %all-to-all-start.1) | async-done | bytes 4194336 | tf_op jit(solution)/shard_map/all_to_all | solution.py:367
  66.3 7.2 %all-to-all-start = ((bf16[64,256,128]{2,1,0:T(8,128)(2,1)}), bf16[64,256,128]{2,1,0:T(8,128)(2,1)}, u32[]{:S(2)}, u32[]{:S(2)}) async-start(bf16[64,256,128]{2,1,0:T(8,128)(2,1)} %pack1.1), calls=%async_computation | async-start | bytes 8388608 | tf_op jit(solution)/shard_map/all_to_all | solution.py:367
  73.5 16.7 %tiles0.1 = (s16[1040,128]{1,0:T(8,128)(2,1)S(1)}, s16[1040,128]{1,0:T(8,128)(2,1)S(1)}, s16[1040,128]{1,0:T(8,128)(2,1)S(1)}, s16[1040,128]{1,0:T(8,128)(2,1)S(1)}) custom-call(s32[1]{0:T(128)} %bitcast.me, s32[176]{0:T(256)S(1)} %bitcast.11, s32[176]{0:T(256)S(1)} %bitcast.13, bf16[176,256,256]{2,1,0:T(8,128)(2,1)} %bitcast.15, ...), custom_call_target="tpu_custom_call" | custom-call | flops 2952790016 | bytes 27262976 | tf_op jit(solution)/shard_map/tiles0/pallas_call | solution.py:108
  90.3 2.8 %collective-permute-start = (s16[1040,128]{1,0:T(8,128)(2,1)S(1)}, s16[1040,128]{1,0:T(8,128)(2,1)S(1)}, u32[]{:S(2)}, u32[]{:S(2)}) collective-permute-start(s16[1040,128]{1,0:T(8,128)(2,1)S(1)} %get-tuple-element.18), channel_id=1, source_target_pairs={{0,2},{1,3},{2,0},{3,1},{4,6},{5,7},{6,4},{7,5},{8,10},{9,11},{10,... | collective-permute-start | bytes 798728 | tf_op jit(solution)/shard_map/ppermute | solution.py:370
  93.4 2.4 %collective-permute-start.2 = (s16[1040,128]{1,0:T(8,128)(2,1)S(1)}, s16[1040,128]{1,0:T(8,128)(2,1)S(1)}, u32[]{:S(2)}, u32[]{:S(2)}) collective-permute-start(s16[1040,128]{1,0:T(8,128)(2,1)S(1)} %get-tuple-element.20), channel_id=1, source_target_pairs={{0,3},{1,0},{2,1},{3,2},{4,7},{5,4},{6,5},{7,6},{8,11},{9,8},{10,9... | collective-permute-start | bytes 798728 | tf_op jit(solution)/shard_map/ppermute | solution.py:370
  95.7 3.9 %collective-permute-done.refs_1_ = s16[1040,128]{1,0:T(8,128)(2,1)S(1)} collective-permute-done((s16[1040,128]{1,0:T(8,128)(2,1)S(1)}, s16[1040,128]{1,0:T(8,128)(2,1)S(1)}, u32[]{:S(2)}, u32[]{:S(2)}) %collective-permute-start) | collective-permute-done | bytes 266272 | tf_op jit(solution)/shard_map/ppermute | solution.py:370
  99.7 6.3 %collective-permute-done.1.refs_2_ = s16[1040,128]{1,0:T(8,128)(2,1)S(1)} collective-permute-done((s16[1040,128]{1,0:T(8,128)(2,1)S(1)}, s16[1040,128]{1,0:T(8,128)(2,1)S(1)}, u32[]{:S(2)}, u32[]{:S(2)}) %collective-permute-start.1) | collective-permute-done | bytes 266272 | tf_op jit(solution)/shard_map/ppermute | solution.py:370
  106.0 0.8 gram0.1
  107.4 0.9 collective-permute-done.3
  108.3 2.4 %collective-permute-start.6 = (f32[128,128]{1,0:T(8,128)S(1)}, f32[128,128]{1,0:T(8,128)S(1)}, u32[]{:S(2)}, u32[]{:S(2)}) collective-permute-start(f32[128,128]{1,0:T(8,128)S(1)} %add.37), channel_id=1, source_target_pairs={{0,3},{1,0},{2,1},{3,2},{4,7},{5,4},{6,5},{7,6},{8,11},{9,8},{10,9... | collective-permute-start | bytes 196616 | tf_op jit(solution)/shard_map/ppermute | solution.py:334
  110.7 1.3 collective-permute-start.4
  112.0 5.0 %collective-permute-done.5 = f32[128,128]{1,0:T(8,128)S(1)} collective-permute-done((f32[128,128]{1,0:T(8,128)S(1)}, f32[128,128]{1,0:T(8,128)S(1)}, u32[]{:S(2)}, u32[]{:S(2)}) %collective-permute-start.5) | collective-permute-done | bytes 65568 | tf_op jit(solution)/shard_map/ppermute | solution.py:334
  117.0 2.8 %collective-permute-start.12 = (f32[128,128]{1,0:T(8,128)S(1)}, f32[128,128]{1,0:T(8,128)S(1)}, u32[]{:S(2)}, u32[]{:S(2)}) collective-permute-start(f32[128,128]{1,0:T(8,128)S(1)} %add_add_fusion.2.refs_0_), channel_id=1, source_target_pairs={{0,96},{4,100},{8,104},{12,108},{16,112},{20,116},{24,120},{28,124... | collective-permute-start | bytes 196616 | tf_op jit(solution)/shard_map/ppermute | solution.py:334
  119.8 1.7 collective-permute-start.10
  121.6 4.2 %all-to-all-done.arrived_hbm = bf16[64,256,128]{2,1,0:T(8,128)(2,1)} async-done(((bf16[64,256,128]{2,1,0:T(8,128)(2,1)}), bf16[64,256,128]{2,1,0:T(8,128)(2,1)}, u32[]{:S(2)}, u32[]{:S(2)}) %all-to-all-start) | async-done | bytes 4194336 | tf_op jit(solution)/shard_map/all_to_all | solution.py:367
  125.8 16.7 %tiles1.1 = (s16[1040,128]{1,0:T(8,128)(2,1)S(1)}, s16[1040,128]{1,0:T(8,128)(2,1)S(1)}, s16[1040,128]{1,0:T(8,128)(2,1)S(1)}, s16[1040,128]{1,0:T(8,128)(2,1)S(1)}) custom-call(s32[1]{0:T(128)} %bitcast.me, s32[176]{0:T(256)S(1)} %bitcast.12, s32[176]{0:T(256)S(1)} %bitcast.14, bf16[176,256,256]{2,1,0:T(8,128)(2,1)} %bitcast.16, ...), custom_call_target="tpu_custom_call" | custom-call | flops 2952790016 | bytes 27262976 | tf_op jit(solution)/shard_map/tiles1/pallas_call | solution.py:108
  142.4 2.8 %collective-permute-start.7 = (s16[1040,128]{1,0:T(8,128)(2,1)S(1)}, s16[1040,128]{1,0:T(8,128)(2,1)S(1)}, u32[]{:S(2)}, u32[]{:S(2)}) collective-permute-start(s16[1040,128]{1,0:T(8,128)(2,1)S(1)} %get-tuple-element.23), channel_id=1, source_target_pairs={{0,2},{1,3},{2,0},{3,1},{4,6},{5,7},{6,4},{7,5},{8,10},{9,11},{10,... | collective-permute-start | bytes 798728 | tf_op jit(solution)/shard_map/ppermute | solution.py:370
  145.6 2.4 %collective-permute-start.9 = (s16[1040,128]{1,0:T(8,128)(2,1)S(1)}, s16[1040,128]{1,0:T(8,128)(2,1)S(1)}, u32[]{:S(2)}, u32[]{:S(2)}) collective-permute-start(s16[1040,128]{1,0:T(8,128)(2,1)S(1)} %get-tuple-element.25), channel_id=1, source_target_pairs={{0,3},{1,0},{2,1},{3,2},{4,7},{5,4},{6,5},{7,6},{8,11},{9,8},{10,9... | collective-permute-start | bytes 798728 | tf_op jit(solution)/shard_map/ppermute | solution.py:370
  148.0 3.2 %collective-permute-start.15 = (f32[128,128]{1,0:T(8,128)S(1)}, f32[128,128]{1,0:T(8,128)S(1)}, u32[]{:S(2)}, u32[]{:S(2)}) collective-permute-start(f32[128,128]{1,0:T(8,128)S(1)} %add_add_fusion.1), channel_id=1, source_target_pairs={{0,24},{4,28},{8,0},{12,4},{16,8},{20,12},{24,16},{28,20},{32,56},... | collective-permute-start | bytes 196616 | tf_op jit(solution)/shard_map/ppermute | solution.py:334
  151.3 1.7 collective-permute-start.13
  153.0 4.7 %collective-permute-done.8.refs_2_ = s16[1040,128]{1,0:T(8,128)(2,1)S(1)} collective-permute-done((s16[1040,128]{1,0:T(8,128)(2,1)S(1)}, s16[1040,128]{1,0:T(8,128)(2,1)S(1)}, u32[]{:S(2)}, u32[]{:S(2)}) %collective-permute-start.8) | collective-permute-done | bytes 266272 | tf_op jit(solution)/shard_map/ppermute | solution.py:370
  157.7 1.9 gram1.1
  159.6 8.6 %all-to-all-start.2 = ((f32[128,2,128]{2,1,0:T(2,128)}), f32[128,2,128]{2,1,0:T(2,128)S(1)}, u32[]{:S(2)}, u32[]{:S(2)}) async-start(f32[128,2,128]{2,1,0:T(2,128)} %bitcast.8), calls=%async_computation.2 | async-start | bytes 262144 | tf_op jit(solution)/shard_map/all_to_all | solution.py:318
  168.3 10.0 %all-to-all-done.2 = f32[128,2,128]{2,1,0:T(2,128)S(1)} async-done(((f32[128,2,128]{2,1,0:T(2,128)}), f32[128,2,128]{2,1,0:T(2,128)S(1)}, u32[]{:S(2)}, u32[]{:S(2)}) %all-to-all-start.2) | async-done | bytes 131104 | tf_op jit(solution)/shard_map/all_to_all | solution.py:318
  178.5 0.7 broadcast_in_dim.2
  179.2 4.1 %all-to-all-start.3 = ((f32[128,2,128]{2,1,0:T(2,128)}), f32[128,2,128]{2,1,0:T(2,128)S(1)}, u32[]{:S(2)}, u32[]{:S(2)}) async-start(f32[128,2,128]{2,1,0:T(2,128)} %broadcast_in_dim.2), calls=%async_computation.3 | async-start | bytes 262144 | tf_op jit(solution)/shard_map/all_to_all | solution.py:321
  183.2 6.0 %first.1 = (f32[128,128]{1,0:T(8,128)S(1)}, f32[128,128]{1,0:T(8,128)S(1)}, f32[1024,128]{1,0:T(8,128)S(1)}) custom-call(f32[128,128]{1,0:T(8,128)S(1)} %add_add_fusion.g_ref, f32[1024,128]{1,0:T(8,128)S(1)} %get-tuple-element.26.refs_4_.y_ref), custom_call_target="tpu_custom_call" | custom-call | flops 20971520000 | bytes 1048576 | tf_op jit(solution)/shard_map/first/pallas_call | solution.py:271
  189.2 4.1 %all-to-all-done.3 = f32[128,2,128]{2,1,0:T(2,128)S(1)} async-done(((f32[128,2,128]{2,1,0:T(2,128)}), f32[128,2,128]{2,1,0:T(2,128)S(1)}, u32[]{:S(2)}, u32[]{:S(2)}) %all-to-all-start.3) | async-done | bytes 131104 | tf_op jit(solution)/shard_map/all_to_all | solution.py:321
  193.3 8.2 %last.1 = (f32[1024,256]{1,0:T(8,128)}, f32[256,256]{1,0:T(8,128)}) custom-call(f32[256,128]{1,0:T(8,128)S(1)} %bitcast.10, f32[128,128]{1,0:T(8,128)S(1)} %get-tuple-element.28.r_ref, f32[128,128]{1,0:T(8,128)S(1)} %get-tuple-element.29.t_ref, f32[1024,128]{1,0:T(8,128)S(1)} %get-tuple-element.30.z_ref, f32[1024,128]{1,0:T(8,128)S(1)} %get-tuple-element.31.y_ref), custom_call_target="tpu_custom_call" | custom-call | tf_op jit(solution)/shard_map/last/pallas_call | solution.py:303
  (29 shorter events, 1.7 us)
Async XLA Ops:
  4.4 61.9 %all-to-all-start.1 = ((bf16[64,256,128]{2,1,0:T(8,128)(2,1)}), bf16[64,256,128]{2,1,0:T(8,128)(2,1)}, u32[]{:S(2)}, u32[]{:S(2)}) async-start(bf16[64,256,128]{2,1,0:T(8,128)(2,1)} %pack0.1), calls=%async_computation.1 | async-start | bytes 8388608 | tf_op jit(solution)/shard_map/all_to_all | solution.py:367
  18.0 55.6 %copy-start.1 = (s32[176,1]{0,1:T(1,128)S(1)}, s32[176,1]{0,1:T(1,128)}, u32[]{:S(2)}) copy-start(s32[176,1]{0,1:T(1,128)} %param.9) | copy-start | bytes 2116
  18.0 55.6 %copy-start.2 = (s32[176,1]{0,1:T(1,128)S(1)}, s32[176,1]{0,1:T(1,128)}, u32[]{:S(2)}) copy-start(s32[176,1]{0,1:T(1,128)} %param.8) | copy-start | bytes 2116
  18.0 55.6 %copy-start = (s32[176,1]{0,1:T(1,128)S(1)}, s32[176,1]{0,1:T(1,128)}, u32[]{:S(2)}) copy-start(s32[176,1]{0,1:T(1,128)} %param.7) | copy-start | bytes 2116
  66.3 59.4 %all-to-all-start = ((bf16[64,256,128]{2,1,0:T(8,128)(2,1)}), bf16[64,256,128]{2,1,0:T(8,128)(2,1)}, u32[]{:S(2)}, u32[]{:S(2)}) async-start(bf16[64,256,128]{2,1,0:T(8,128)(2,1)} %pack1.1), calls=%async_computation | async-start | bytes 8388608 | tf_op jit(solution)/shard_map/all_to_all | solution.py:367
  90.3 9.4 %collective-permute-start = (s16[1040,128]{1,0:T(8,128)(2,1)S(1)}, s16[1040,128]{1,0:T(8,128)(2,1)S(1)}, u32[]{:S(2)}, u32[]{:S(2)}) collective-permute-start(s16[1040,128]{1,0:T(8,128)(2,1)S(1)} %get-tuple-element.18), channel_id=1, source_target_pairs={{0,2},{1,3},{2,0},{3,1},{4,6},{5,7},{6,4},{7,5},{8,10},{9,11},{10,... | collective-permute-start | bytes 798728 | tf_op jit(solution)/shard_map/ppermute | solution.py:370
  93.1 12.9 %collective-permute-start.1 = (s16[1040,128]{1,0:T(8,128)(2,1)S(1)}, s16[1040,128]{1,0:T(8,128)(2,1)S(1)}, u32[]{:S(2)}, u32[]{:S(2)}) collective-permute-start(s16[1040,128]{1,0:T(8,128)(2,1)S(1)} %get-tuple-element.19), channel_id=1, source_target_pairs={{0,1},{1,2},{2,3},{3,0},{4,5},{5,6},{6,7},{7,4},{8,9},{9,10},{10,1... | collective-permute-start | bytes 798728 | tf_op jit(solution)/shard_map/ppermute | solution.py:370
  93.4 12.6 %collective-permute-start.2 = (s16[1040,128]{1,0:T(8,128)(2,1)S(1)}, s16[1040,128]{1,0:T(8,128)(2,1)S(1)}, u32[]{:S(2)}, u32[]{:S(2)}) collective-permute-start(s16[1040,128]{1,0:T(8,128)(2,1)S(1)} %get-tuple-element.20), channel_id=1, source_target_pairs={{0,3},{1,0},{2,1},{3,2},{4,7},{5,4},{6,5},{7,6},{8,11},{9,8},{10,9... | collective-permute-start | bytes 798728 | tf_op jit(solution)/shard_map/ppermute | solution.py:370
  106.8 1.5 collective-permute-start.3
  108.3 3.7 %collective-permute-start.6 = (f32[128,128]{1,0:T(8,128)S(1)}, f32[128,128]{1,0:T(8,128)S(1)}, u32[]{:S(2)}, u32[]{:S(2)}) collective-permute-start(f32[128,128]{1,0:T(8,128)S(1)} %add.37), channel_id=1, source_target_pairs={{0,3},{1,0},{2,1},{3,2},{4,7},{5,4},{6,5},{7,6},{8,11},{9,8},{10,9... | collective-permute-start | bytes 196616 | tf_op jit(solution)/shard_map/ppermute | solution.py:334
  110.7 6.3 %collective-permute-start.5 = (f32[128,128]{1,0:T(8,128)S(1)}, f32[128,128]{1,0:T(8,128)S(1)}, u32[]{:S(2)}, u32[]{:S(2)}) collective-permute-start(f32[128,128]{1,0:T(8,128)S(1)} %add.37), channel_id=1, source_target_pairs={{0,1},{1,2},{2,3},{3,0},{4,5},{5,6},{6,7},{7,4},{8,9},{9,10},{10,1... | collective-permute-start | bytes 196616 | tf_op jit(solution)/shard_map/ppermute | solution.py:334
  110.7 6.3 %collective-permute-start.4 = (f32[128,128]{1,0:T(8,128)S(1)}, f32[128,128]{1,0:T(8,128)S(1)}, u32[]{:S(2)}, u32[]{:S(2)}) collective-permute-start(f32[128,128]{1,0:T(8,128)S(1)} %add.37), channel_id=1, source_target_pairs={{0,2},{1,3},{2,0},{3,1},{4,6},{5,7},{6,4},{7,5},{8,10},{9,11},{10,... | collective-permute-start | bytes 196616 | tf_op jit(solution)/shard_map/ppermute | solution.py:334
  117.0 28.6 %collective-permute-start.12 = (f32[128,128]{1,0:T(8,128)S(1)}, f32[128,128]{1,0:T(8,128)S(1)}, u32[]{:S(2)}, u32[]{:S(2)}) collective-permute-start(f32[128,128]{1,0:T(8,128)S(1)} %add_add_fusion.2.refs_0_), channel_id=1, source_target_pairs={{0,96},{4,100},{8,104},{12,108},{16,112},{20,116},{24,120},{28,124... | collective-permute-start | bytes 196616 | tf_op jit(solution)/shard_map/ppermute | solution.py:334
  119.8 28.1 %collective-permute-start.11 = (f32[128,128]{1,0:T(8,128)S(1)}, f32[128,128]{1,0:T(8,128)S(1)}, u32[]{:S(2)}, u32[]{:S(2)}) collective-permute-start(f32[128,128]{1,0:T(8,128)S(1)} %add_add_fusion.2.refs_0_), channel_id=1, source_target_pairs={{0,32},{4,36},{8,40},{12,44},{16,48},{20,52},{24,56},{28,60},{32,6... | collective-permute-start | bytes 196616 | tf_op jit(solution)/shard_map/ppermute | solution.py:334
  119.8 28.1 %collective-permute-start.10 = (f32[128,128]{1,0:T(8,128)S(1)}, f32[128,128]{1,0:T(8,128)S(1)}, u32[]{:S(2)}, u32[]{:S(2)}) collective-permute-start(f32[128,128]{1,0:T(8,128)S(1)} %add_add_fusion.2.refs_0_), channel_id=1, source_target_pairs={{0,64},{4,68},{8,72},{12,76},{16,80},{20,84},{24,88},{28,92},{32,9... | collective-permute-start | bytes 196616 | tf_op jit(solution)/shard_map/ppermute | solution.py:334
  142.4 8.8 %collective-permute-start.7 = (s16[1040,128]{1,0:T(8,128)(2,1)S(1)}, s16[1040,128]{1,0:T(8,128)(2,1)S(1)}, u32[]{:S(2)}, u32[]{:S(2)}) collective-permute-start(s16[1040,128]{1,0:T(8,128)(2,1)S(1)} %get-tuple-element.23), channel_id=1, source_target_pairs={{0,2},{1,3},{2,0},{3,1},{4,6},{5,7},{6,4},{7,5},{8,10},{9,11},{10,... | collective-permute-start | bytes 798728 | tf_op jit(solution)/shard_map/ppermute | solution.py:370
  145.3 12.4 %collective-permute-start.8 = (s16[1040,128]{1,0:T(8,128)(2,1)S(1)}, s16[1040,128]{1,0:T(8,128)(2,1)S(1)}, u32[]{:S(2)}, u32[]{:S(2)}) collective-permute-start(s16[1040,128]{1,0:T(8,128)(2,1)S(1)} %get-tuple-element.24), channel_id=1, source_target_pairs={{0,1},{1,2},{2,3},{3,0},{4,5},{5,6},{6,7},{7,4},{8,9},{9,10},{10,1... | collective-permute-start | bytes 798728 | tf_op jit(solution)/shard_map/ppermute | solution.py:370
  145.6 12.1 %collective-permute-start.9 = (s16[1040,128]{1,0:T(8,128)(2,1)S(1)}, s16[1040,128]{1,0:T(8,128)(2,1)S(1)}, u32[]{:S(2)}, u32[]{:S(2)}) collective-permute-start(s16[1040,128]{1,0:T(8,128)(2,1)S(1)} %get-tuple-element.25), channel_id=1, source_target_pairs={{0,3},{1,0},{2,1},{3,2},{4,7},{5,4},{6,5},{7,6},{8,11},{9,8},{10,9... | collective-permute-start | bytes 798728 | tf_op jit(solution)/shard_map/ppermute | solution.py:370
  148.0 20.3 %collective-permute-start.15 = (f32[128,128]{1,0:T(8,128)S(1)}, f32[128,128]{1,0:T(8,128)S(1)}, u32[]{:S(2)}, u32[]{:S(2)}) collective-permute-start(f32[128,128]{1,0:T(8,128)S(1)} %add_add_fusion.1), channel_id=1, source_target_pairs={{0,24},{4,28},{8,0},{12,4},{16,8},{20,12},{24,16},{28,20},{32,56},... | collective-permute-start | bytes 196616 | tf_op jit(solution)/shard_map/ppermute | solution.py:334
  151.2 17.1 %collective-permute-start.14 = (f32[128,128]{1,0:T(8,128)S(1)}, f32[128,128]{1,0:T(8,128)S(1)}, u32[]{:S(2)}, u32[]{:S(2)}) collective-permute-start(f32[128,128]{1,0:T(8,128)S(1)} %add_add_fusion.1), channel_id=1, source_target_pairs={{0,8},{4,12},{8,16},{12,20},{16,24},{20,28},{24,0},{28,4},{32,40},... | collective-permute-start | bytes 196616 | tf_op jit(solution)/shard_map/ppermute | solution.py:334
  151.3 17.0 %collective-permute-start.13 = (f32[128,128]{1,0:T(8,128)S(1)}, f32[128,128]{1,0:T(8,128)S(1)}, u32[]{:S(2)}, u32[]{:S(2)}) collective-permute-start(f32[128,128]{1,0:T(8,128)S(1)} %add_add_fusion.1), channel_id=1, source_target_pairs={{0,16},{4,20},{8,24},{12,28},{16,0},{20,4},{24,8},{28,12},{32,48},... | collective-permute-start | bytes 196616 | tf_op jit(solution)/shard_map/ppermute | solution.py:334
  159.6 18.7 %all-to-all-start.2 = ((f32[128,2,128]{2,1,0:T(2,128)}), f32[128,2,128]{2,1,0:T(2,128)S(1)}, u32[]{:S(2)}, u32[]{:S(2)}) async-start(f32[128,2,128]{2,1,0:T(2,128)} %bitcast.8), calls=%async_computation.2 | async-start | bytes 262144 | tf_op jit(solution)/shard_map/all_to_all | solution.py:318
  179.2 14.1 %all-to-all-start.3 = ((f32[128,2,128]{2,1,0:T(2,128)}), f32[128,2,128]{2,1,0:T(2,128)S(1)}, u32[]{:S(2)}, u32[]{:S(2)}) async-start(f32[128,2,128]{2,1,0:T(2,128)} %broadcast_in_dim.2), calls=%async_computation.3 | async-start | bytes 262144 | tf_op jit(solution)/shard_map/all_to_all | solution.py:321

commit v5 on v4

--- a/solution.py
+++ b/solution.py
@@ -9,24 +9,30 @@
 
 BR_DEV = 16
 HALF = 128
-GROUP = 22
 LOADS = 8
+AHEAD = 2
+LIMIT = 44 * 2**20
 STEP = 32704.0
 LEAST = 2.0**-80
 HIGHEST = lax.Precision.HIGHEST
 F32 = jnp.float32
 
 
-def pack_kernel(half, lists, owned, out, sems):
+def pack_kernel(half, lists, owned_hbm, out, owned, owned_sems, sems):
     count, slots = out.shape[0], lists.shape[0]
 
+    def bring(i):
+        part = owned_hbm.at[i, :, pl.ds(half * HALF, HALF)]
+        return pltpu.make_async_copy(part, owned.at[i], owned_sems.at[i])
+
     def one(i):
-        return pltpu.make_async_copy(
-            owned.at[lists[i % slots, i // slots], :, pl.ds(half * HALF, HALF)],
-            out.at[i],
-            sems.at[i],
-        )
-
+        block = owned.at[lists[i % slots, i // slots]]
+        return pltpu.make_async_copy(block, out.at[i], sems.at[i])
+
+    for i in range(owned.shape[0]):
+        bring(i).start()
+    for i in range(owned.shape[0]):
+        bring(i).wait()
     for i in range(count):
         one(i).start()
     for i in range(count):
@@ -35,16 +41,20 @@
 
 def pack(lists, owned, half):
     count = lists.size
-    height = owned.shape[1]
+    blocks, height = owned.shape[:2]
     return pl.pallas_call(
         functools.partial(pack_kernel, half),
         out_shape=jax.ShapeDtypeStruct((count, height, HALF), owned.dtype),
         in_specs=[
             pl.BlockSpec(memory_space=pltpu.SMEM),
-            pl.BlockSpec(memory_space=pltpu.VMEM),
+            pl.BlockSpec(memory_space=pl.ANY),
         ],
         out_specs=pl.BlockSpec(memory_space=pl.ANY),
-        scratch_shapes=[pltpu.SemaphoreType.DMA((count,))],
+        scratch_shapes=[
+            pltpu.VMEM((blocks, height, HALF), owned.dtype),
+            pltpu.SemaphoreType.DMA((blocks,)),
+            pltpu.SemaphoreType.DMA((count,)),
+        ],
         cost_estimate=pl.CostEstimate(
             flops=0, bytes_accessed=2 * count * height * HALF * 2, transcendentals=0
         ),
@@ -63,7 +73,7 @@
     *_, total, values, arrived, value_sems, arrived_sems = refs
     outs = refs[-5 - shares : -5]
     count, loads, parts = values.shape[0], value_sems.shape[0], arrived_sems.shape[0]
-    assert count % GROUP == 0 and loads * GROUP % count == 0 and count % loads == 0
+    assert count % loads == 0 and AHEAD <= loads
 
     def bring(i):
         part = pl.ds(i * (count // loads), count // loads)
@@ -75,18 +85,21 @@
 
     for i in range(parts):
         bring_basis(i).start()
-    for i in range(loads):
+    for i in range(AHEAD):
         bring(i).start()
     total[...] = jnp.zeros_like(total)
     for i in range(parts):
         bring_basis(i).wait()
 
-    @pl.loop(0, count // GROUP)
+    @pl.loop(0, loads)
     def _(step):
-        for i in range(loads * GROUP // count):
-            bring(step * (loads * GROUP // count) + i).wait()
-        for u in range(GROUP):
-            t = step * GROUP + u
+        @pl.when(step + AHEAD < loads)
+        def _():
+            bring(step + AHEAD).start()
+
+        bring(step).wait()
+        for u in range(count // loads):
+            t = step * (count // loads) + u
             total[blocks[t]] += jnp.dot(values[t], arrived[places[t]], preferred_element_type=F32)
 
     each = BR_DEV // shares
@@ -117,7 +130,7 @@
             pltpu.SemaphoreType.DMA((4,)),
         ],
         out_shape=[jax.ShapeDtypeStruct((rows + 16, HALF), jnp.int16)] * shares,
-        compiler_params=pltpu.CompilerParams(vmem_limit_bytes=44 * 2**20),
+        compiler_params=pltpu.CompilerParams(vmem_limit_bytes=LIMIT),
         cost_estimate=pl.CostEstimate(
             flops=2 * count * height * depth * HALF,
             bytes_accessed=count * height * depth * 2 + arrived.size * 2,

time: 202 us -> 198 us (0.980)
  Pallas kernels: 57.9 us -> 50 us
  waiting for transfers between devices: 87.5 us -> 91.7 us
    pallas_call x2, Pallas kernels: 33.4 us -> 24.4 us  [tiles(): pl.pallas_call(functools.partial(tiles_kernel, shares), in_specs=inputs,...]
    all_to_all x2, waiting for transfers between devices: 52.5 us -> 56.5 us  [product(): arrived = lax.all_to_all(packed[half], 'row', 0, 0, tiled=True)]
  transfers between devices with their start and end apart: 20 -> 20, of which waited for: 10 -> 10; matrix products, arithmetic and copies ran while one was open for 0% -> 0% of each run, Pallas kernels for 23% -> 19%
where the time goes in v5:
time: 198 us
  waiting for transfers between devices  91.7 us (46%)
  starting transfers between devices  54.2 us (27%)
  Pallas kernels  50 us (25%)
    all_to_all x2, waiting for transfers between devices, product(): arrived = lax.all_to_all(packed[half], 'row', 0, 0, tiled=True)  56.5 us
    pallas_call x2, Pallas kernels, tiles(): pl.pallas_call(functools.partial(tiles_kernel, shares), in_specs=inputs,...  24.4 us
    all_to_all x2, starting transfers between devices, product(): arrived = lax.all_to_all(packed[half], 'row', 0, 0, tiled=True)  16.8 us
    ppermute x6, waiting for transfers between devices, product(): lax.ppermute(coded[k], 'col', [(i, (i + k) % cols) for i in range(cols)])  15 us
    ppermute x10, starting transfers between devices, sum_along(): lax.ppermute(part, axis, [(i, i + ((i // stride + k) % length - i // stri...  13.8 us
    ppermute x6, starting transfers between devices, product(): lax.ppermute(coded[k], 'col', [(i, (i + k) % cols) for i in range(cols)])  11 us
    all_to_all x1, waiting for transfers between devices, sum_all(): lax.all_to_all(part.reshape(n, height // n, HALF), axes, 0, 0, tiled=True)  10 us
    pallas_call x2, Pallas kernels, pack(): pl.pallas_call(functools.partial(pack_kernel, half), out_shape=jax.ShapeD...  8.79 us
  transfers between devices with their start and end apart: 20, of which 10 were waited for; matrix products, arithmetic and copies ran while one was open for 0% of the time, Pallas kernels for 19%

profile of v5, /device:TPU:1, one launch (start us, length us, event | category | flops | bytes accessed | tf_op | source)
XLA Modules:
  0.0 197.6 jit_solution(14227051864559960602)
XLA Ops:
  0.6 4.4 %pack0.1 = bf16[64,256,128]{2,1,0:T(8,128)(2,1)} custom-call(s32[2,32]{1,0:T(2,128)} %bitcast.19, bf16[8,256,256]{2,1,0:T(8,128)(2,1)} %bitcast.17), custom_call_target="tpu_custom_call" | custom-call | bytes 8388608 | tf_op jit(solution)/shard_map/pack0/pallas_call | solution.py:45
  5.0 9.7 %all-to-all-start.1 = ((bf16[64,256,128]{2,1,0:T(8,128)(2,1)}), bf16[64,256,128]{2,1,0:T(8,128)(2,1)}, u32[]{:S(2)}, u32[]{:S(2)}) async-start(bf16[64,256,128]{2,1,0:T(8,128)(2,1)} %pack0.1), calls=%async_computation.1 | async-start | bytes 8388608 | tf_op jit(solution)/shard_map/all_to_all | solution.py:380
  14.7 4.4 %pack1.1 = bf16[64,256,128]{2,1,0:T(8,128)(2,1)} custom-call(s32[2,32]{1,0:T(2,128)} %bitcast.20, bf16[8,256,256]{2,1,0:T(8,128)(2,1)} %bitcast.18), custom_call_target="tpu_custom_call" | custom-call | bytes 8388608 | tf_op jit(solution)/shard_map/pack1/pallas_call | solution.py:45
  19.1 47.8 %all-to-all-done.1.arrived_hbm = bf16[64,256,128]{2,1,0:T(8,128)(2,1)} async-done(((bf16[64,256,128]{2,1,0:T(8,128)(2,1)}), bf16[64,256,128]{2,1,0:T(8,128)(2,1)}, u32[]{:S(2)}, u32[]{:S(2)}) %all-to-all-start.1) | async-done | bytes 4194336 | tf_op jit(solution)/shard_map/all_to_all | solution.py:380
  66.9 7.2 %all-to-all-start = ((bf16[64,256,128]{2,1,0:T(8,128)(2,1)}), bf16[64,256,128]{2,1,0:T(8,128)(2,1)}, u32[]{:S(2)}, u32[]{:S(2)}) async-start(bf16[64,256,128]{2,1,0:T(8,128)(2,1)} %pack1.1), calls=%async_computation | async-start | bytes 8388608 | tf_op jit(solution)/shard_map/all_to_all | solution.py:380
  74.1 12.2 %tiles0.1 = (s16[1040,128]{1,0:T(8,128)(2,1)S(1)}, s16[1040,128]{1,0:T(8,128)(2,1)S(1)}, s16[1040,128]{1,0:T(8,128)(2,1)S(1)}, s16[1040,128]{1,0:T(8,128)(2,1)S(1)}) custom-call(s32[1]{0:T(128)} %bitcast.me, s32[176]{0:T(256)S(1)} %bitcast.11, s32[176]{0:T(256)S(1)} %bitcast.13, bf16[176,256,256]{2,1,0:T(8,128)(2,1)} %bitcast.15, ...), custom_call_target="tpu_custom_call" | custom-call | flops 2952790016 | bytes 27262976 | tf_op jit(solution)/shard_map/tiles0/pallas_call | solution.py:121
  86.3 2.8 %collective-permute-start = (s16[1040,128]{1,0:T(8,128)(2,1)S(1)}, s16[1040,128]{1,0:T(8,128)(2,1)S(1)}, u32[]{:S(2)}, u32[]{:S(2)}) collective-permute-start(s16[1040,128]{1,0:T(8,128)(2,1)S(1)} %get-tuple-element.18), channel_id=1, source_target_pairs={{0,2},{1,3},{2,0},{3,1},{4,6},{5,7},{6,4},{7,5},{8,10},{9,11},{10,... | collective-permute-start | bytes 798728 | tf_op jit(solution)/shard_map/ppermute | solution.py:383
  89.5 2.4 %collective-permute-start.2 = (s16[1040,128]{1,0:T(8,128)(2,1)S(1)}, s16[1040,128]{1,0:T(8,128)(2,1)S(1)}, u32[]{:S(2)}, u32[]{:S(2)}) collective-permute-start(s16[1040,128]{1,0:T(8,128)(2,1)S(1)} %get-tuple-element.20), channel_id=1, source_target_pairs={{0,3},{1,0},{2,1},{3,2},{4,7},{5,4},{6,5},{7,6},{8,11},{9,8},{10,9... | collective-permute-start | bytes 798728 | tf_op jit(solution)/shard_map/ppermute | solution.py:383
  91.8 3.9 %collective-permute-done.refs_1_ = s16[1040,128]{1,0:T(8,128)(2,1)S(1)} collective-permute-done((s16[1040,128]{1,0:T(8,128)(2,1)S(1)}, s16[1040,128]{1,0:T(8,128)(2,1)S(1)}, u32[]{:S(2)}, u32[]{:S(2)}) %collective-permute-start) | collective-permute-done | bytes 266272 | tf_op jit(solution)/shard_map/ppermute | solution.py:383
  95.7 6.3 %collective-permute-done.1.refs_2_ = s16[1040,128]{1,0:T(8,128)(2,1)S(1)} collective-permute-done((s16[1040,128]{1,0:T(8,128)(2,1)S(1)}, s16[1040,128]{1,0:T(8,128)(2,1)S(1)}, u32[]{:S(2)}, u32[]{:S(2)}) %collective-permute-start.1) | collective-permute-done | bytes 266272 | tf_op jit(solution)/shard_map/ppermute | solution.py:383
  102.0 0.8 gram0.1
  103.4 0.9 collective-permute-done.3
  104.3 2.4 %collective-permute-start.6 = (f32[128,128]{1,0:T(8,128)S(1)}, f32[128,128]{1,0:T(8,128)S(1)}, u32[]{:S(2)}, u32[]{:S(2)}) collective-permute-start(f32[128,128]{1,0:T(8,128)S(1)} %add.37), channel_id=1, source_target_pairs={{0,3},{1,0},{2,1},{3,2},{4,7},{5,4},{6,5},{7,6},{8,11},{9,8},{10,9... | collective-permute-start | bytes 196616 | tf_op jit(solution)/shard_map/ppermute | solution.py:347
  106.8 1.3 collective-permute-start.4
  108.1 5.1 %collective-permute-done.5 = f32[128,128]{1,0:T(8,128)S(1)} collective-permute-done((f32[128,128]{1,0:T(8,128)S(1)}, f32[128,128]{1,0:T(8,128)S(1)}, u32[]{:S(2)}, u32[]{:S(2)}) %collective-permute-start.5) | collective-permute-done | bytes 65568 | tf_op jit(solution)/shard_map/ppermute | solution.py:347
  113.2 2.7 %collective-permute-start.12 = (f32[128,128]{1,0:T(8,128)S(1)}, f32[128,128]{1,0:T(8,128)S(1)}, u32[]{:S(2)}, u32[]{:S(2)}) collective-permute-start(f32[128,128]{1,0:T(8,128)S(1)} %add_add_fusion.2.refs_0_), channel_id=1, source_target_pairs={{0,96},{4,100},{8,104},{12,108},{16,112},{20,116},{24,120},{28,124... | collective-permute-start | bytes 196616 | tf_op jit(solution)/shard_map/ppermute | solution.py:347
  115.9 1.7 collective-permute-start.10
  117.6 8.7 %all-to-all-done.arrived_hbm = bf16[64,256,128]{2,1,0:T(8,128)(2,1)} async-done(((bf16[64,256,128]{2,1,0:T(8,128)(2,1)}), bf16[64,256,128]{2,1,0:T(8,128)(2,1)}, u32[]{:S(2)}, u32[]{:S(2)}) %all-to-all-start) | async-done | bytes 4194336 | tf_op jit(solution)/shard_map/all_to_all | solution.py:380
  126.3 12.2 %tiles1.1 = (s16[1040,128]{1,0:T(8,128)(2,1)S(1)}, s16[1040,128]{1,0:T(8,128)(2,1)S(1)}, s16[1040,128]{1,0:T(8,128)(2,1)S(1)}, s16[1040,128]{1,0:T(8,128)(2,1)S(1)}) custom-call(s32[1]{0:T(128)} %bitcast.me, s32[176]{0:T(256)S(1)} %bitcast.12, s32[176]{0:T(256)S(1)} %bitcast.14, bf16[176,256,256]{2,1,0:T(8,128)(2,1)} %bitcast.16, ...), custom_call_target="tpu_custom_call" | custom-call | flops 2952790016 | bytes 27262976 | tf_op jit(solution)/shard_map/tiles1/pallas_call | solution.py:121
  138.5 2.8 %collective-permute-start.7 = (s16[1040,128]{1,0:T(8,128)(2,1)S(1)}, s16[1040,128]{1,0:T(8,128)(2,1)S(1)}, u32[]{:S(2)}, u32[]{:S(2)}) collective-permute-start(s16[1040,128]{1,0:T(8,128)(2,1)S(1)} %get-tuple-element.23), channel_id=1, source_target_pairs={{0,2},{1,3},{2,0},{3,1},{4,6},{5,7},{6,4},{7,5},{8,10},{9,11},{10,... | collective-permute-start | bytes 798728 | tf_op jit(solution)/shard_map/ppermute | solution.py:383
  141.7 2.3 %collective-permute-start.9 = (s16[1040,128]{1,0:T(8,128)(2,1)S(1)}, s16[1040,128]{1,0:T(8,128)(2,1)S(1)}, u32[]{:S(2)}, u32[]{:S(2)}) collective-permute-start(s16[1040,128]{1,0:T(8,128)(2,1)S(1)} %get-tuple-element.25), channel_id=1, source_target_pairs={{0,3},{1,0},{2,1},{3,2},{4,7},{5,4},{6,5},{7,6},{8,11},{9,8},{10,9... | collective-permute-start | bytes 798728 | tf_op jit(solution)/shard_map/ppermute | solution.py:383
  144.0 3.2 %collective-permute-start.15 = (f32[128,128]{1,0:T(8,128)S(1)}, f32[128,128]{1,0:T(8,128)S(1)}, u32[]{:S(2)}, u32[]{:S(2)}) collective-permute-start(f32[128,128]{1,0:T(8,128)S(1)} %add_add_fusion.1), channel_id=1, source_target_pairs={{0,24},{4,28},{8,0},{12,4},{16,8},{20,12},{24,16},{28,20},{32,56},... | collective-permute-start | bytes 196616 | tf_op jit(solution)/shard_map/ppermute | solution.py:347
  147.4 1.7 collective-permute-start.13
  149.1 4.8 %collective-permute-done.8.refs_2_ = s16[1040,128]{1,0:T(8,128)(2,1)S(1)} collective-permute-done((s16[1040,128]{1,0:T(8,128)(2,1)S(1)}, s16[1040,128]{1,0:T(8,128)(2,1)S(1)}, u32[]{:S(2)}, u32[]{:S(2)}) %collective-permute-start.8) | collective-permute-done | bytes 266272 | tf_op jit(solution)/shard_map/ppermute | solution.py:383
  153.9 1.9 gram1.1
  155.8 8.5 %all-to-all-start.2 = ((f32[128,2,128]{2,1,0:T(2,128)}), f32[128,2,128]{2,1,0:T(2,128)S(1)}, u32[]{:S(2)}, u32[]{:S(2)}) async-start(f32[128,2,128]{2,1,0:T(2,128)} %bitcast.8), calls=%async_computation.2 | async-start | bytes 262144 | tf_op jit(solution)/shard_map/all_to_all | solution.py:331
  164.4 10.0 %all-to-all-done.2 = f32[128,2,128]{2,1,0:T(2,128)S(1)} async-done(((f32[128,2,128]{2,1,0:T(2,128)}), f32[128,2,128]{2,1,0:T(2,128)S(1)}, u32[]{:S(2)}, u32[]{:S(2)}) %all-to-all-start.2) | async-done | bytes 131104 | tf_op jit(solution)/shard_map/all_to_all | solution.py:331
  174.6 0.7 broadcast_in_dim.2
  175.3 4.1 %all-to-all-start.3 = ((f32[128,2,128]{2,1,0:T(2,128)}), f32[128,2,128]{2,1,0:T(2,128)S(1)}, u32[]{:S(2)}, u32[]{:S(2)}) async-start(f32[128,2,128]{2,1,0:T(2,128)} %broadcast_in_dim.2), calls=%async_computation.3 | async-start | bytes 262144 | tf_op jit(solution)/shard_map/all_to_all | solution.py:334
  179.3 6.0 %first.1 = (f32[128,128]{1,0:T(8,128)S(1)}, f32[128,128]{1,0:T(8,128)S(1)}, f32[1024,128]{1,0:T(8,128)S(1)}) custom-call(f32[128,128]{1,0:T(8,128)S(1)} %add_add_fusion.g_ref, f32[1024,128]{1,0:T(8,128)S(1)} %get-tuple-element.26.refs_4_.y_ref), custom_call_target="tpu_custom_call" | custom-call | flops 20971520000 | bytes 1048576 | tf_op jit(solution)/shard_map/first/pallas_call | solution.py:284
  185.3 4.1 %all-to-all-done.3 = f32[128,2,128]{2,1,0:T(2,128)S(1)} async-done(((f32[128,2,128]{2,1,0:T(2,128)}), f32[128,2,128]{2,1,0:T(2,128)S(1)}, u32[]{:S(2)}, u32[]{:S(2)}) %all-to-all-start.3) | async-done | bytes 131104 | tf_op jit(solution)/shard_map/all_to_all | solution.py:334
  189.4 8.2 %last.1 = (f32[1024,256]{1,0:T(8,128)}, f32[256,256]{1,0:T(8,128)}) custom-call(f32[256,128]{1,0:T(8,128)S(1)} %bitcast.10, f32[128,128]{1,0:T(8,128)S(1)} %get-tuple-element.28.r_ref, f32[128,128]{1,0:T(8,128)S(1)} %get-tuple-element.29.t_ref, f32[1024,128]{1,0:T(8,128)S(1)} %get-tuple-element.30.z_ref, f32[1024,128]{1,0:T(8,128)S(1)} %get-tuple-element.31.y_ref), custom_call_target="tpu_custom_call" | custom-call | tf_op jit(solution)/shard_map/last/pallas_call | solution.py:316
  (29 shorter events, 1.7 us)
Async XLA Ops:
  5.0 61.9 %all-to-all-start.1 = ((bf16[64,256,128]{2,1,0:T(8,128)(2,1)}), bf16[64,256,128]{2,1,0:T(8,128)(2,1)}, u32[]{:S(2)}, u32[]{:S(2)}) async-start(bf16[64,256,128]{2,1,0:T(8,128)(2,1)} %pack0.1), calls=%async_computation.1 | async-start | bytes 8388608 | tf_op jit(solution)/shard_map/all_to_all | solution.py:380
  19.1 55.0 %copy-start.1 = (s32[176,1]{0,1:T(1,128)S(1)}, s32[176,1]{0,1:T(1,128)}, u32[]{:S(2)}) copy-start(s32[176,1]{0,1:T(1,128)} %param.9) | copy-start | bytes 2116
  19.1 55.0 %copy-start.2 = (s32[176,1]{0,1:T(1,128)S(1)}, s32[176,1]{0,1:T(1,128)}, u32[]{:S(2)}) copy-start(s32[176,1]{0,1:T(1,128)} %param.8) | copy-start | bytes 2116
  19.1 55.0 %copy-start = (s32[176,1]{0,1:T(1,128)S(1)}, s32[176,1]{0,1:T(1,128)}, u32[]{:S(2)}) copy-start(s32[176,1]{0,1:T(1,128)} %param.7) | copy-start | bytes 2116
  66.9 59.4 %all-to-all-start = ((bf16[64,256,128]{2,1,0:T(8,128)(2,1)}), bf16[64,256,128]{2,1,0:T(8,128)(2,1)}, u32[]{:S(2)}, u32[]{:S(2)}) async-start(bf16[64,256,128]{2,1,0:T(8,128)(2,1)} %pack1.1), calls=%async_computation | async-start | bytes 8388608 | tf_op jit(solution)/shard_map/all_to_all | solution.py:380
  86.3 9.4 %collective-permute-start = (s16[1040,128]{1,0:T(8,128)(2,1)S(1)}, s16[1040,128]{1,0:T(8,128)(2,1)S(1)}, u32[]{:S(2)}, u32[]{:S(2)}) collective-permute-start(s16[1040,128]{1,0:T(8,128)(2,1)S(1)} %get-tuple-element.18), channel_id=1, source_target_pairs={{0,2},{1,3},{2,0},{3,1},{4,6},{5,7},{6,4},{7,5},{8,10},{9,11},{10,... | collective-permute-start | bytes 798728 | tf_op jit(solution)/shard_map/ppermute | solution.py:383
  89.1 12.9 %collective-permute-start.1 = (s16[1040,128]{1,0:T(8,128)(2,1)S(1)}, s16[1040,128]{1,0:T(8,128)(2,1)S(1)}, u32[]{:S(2)}, u32[]{:S(2)}) collective-permute-start(s16[1040,128]{1,0:T(8,128)(2,1)S(1)} %get-tuple-element.19), channel_id=1, source_target_pairs={{0,1},{1,2},{2,3},{3,0},{4,5},{5,6},{6,7},{7,4},{8,9},{9,10},{10,1... | collective-permute-start | bytes 798728 | tf_op jit(solution)/shard_map/ppermute | solution.py:383
  89.5 12.6 %collective-permute-start.2 = (s16[1040,128]{1,0:T(8,128)(2,1)S(1)}, s16[1040,128]{1,0:T(8,128)(2,1)S(1)}, u32[]{:S(2)}, u32[]{:S(2)}) collective-permute-start(s16[1040,128]{1,0:T(8,128)(2,1)S(1)} %get-tuple-element.20), channel_id=1, source_target_pairs={{0,3},{1,0},{2,1},{3,2},{4,7},{5,4},{6,5},{7,6},{8,11},{9,8},{10,9... | collective-permute-start | bytes 798728 | tf_op jit(solution)/shard_map/ppermute | solution.py:383
  102.8 1.5 collective-permute-start.3
  104.3 3.8 %collective-permute-start.6 = (f32[128,128]{1,0:T(8,128)S(1)}, f32[128,128]{1,0:T(8,128)S(1)}, u32[]{:S(2)}, u32[]{:S(2)}) collective-permute-start(f32[128,128]{1,0:T(8,128)S(1)} %add.37), channel_id=1, source_target_pairs={{0,3},{1,0},{2,1},{3,2},{4,7},{5,4},{6,5},{7,6},{8,11},{9,8},{10,9... | collective-permute-start | bytes 196616 | tf_op jit(solution)/shard_map/ppermute | solution.py:347
  106.8 6.4 %collective-permute-start.5 = (f32[128,128]{1,0:T(8,128)S(1)}, f32[128,128]{1,0:T(8,128)S(1)}, u32[]{:S(2)}, u32[]{:S(2)}) collective-permute-start(f32[128,128]{1,0:T(8,128)S(1)} %add.37), channel_id=1, source_target_pairs={{0,1},{1,2},{2,3},{3,0},{4,5},{5,6},{6,7},{7,4},{8,9},{9,10},{10,1... | collective-permute-start | bytes 196616 | tf_op jit(solution)/shard_map/ppermute | solution.py:347
  106.8 6.4 %collective-permute-start.4 = (f32[128,128]{1,0:T(8,128)S(1)}, f32[128,128]{1,0:T(8,128)S(1)}, u32[]{:S(2)}, u32[]{:S(2)}) collective-permute-start(f32[128,128]{1,0:T(8,128)S(1)} %add.37), channel_id=1, source_target_pairs={{0,2},{1,3},{2,0},{3,1},{4,6},{5,7},{6,4},{7,5},{8,10},{9,11},{10,... | collective-permute-start | bytes 196616 | tf_op jit(solution)/shard_map/ppermute | solution.py:347
  113.2 28.5 %collective-permute-start.12 = (f32[128,128]{1,0:T(8,128)S(1)}, f32[128,128]{1,0:T(8,128)S(1)}, u32[]{:S(2)}, u32[]{:S(2)}) collective-permute-start(f32[128,128]{1,0:T(8,128)S(1)} %add_add_fusion.2.refs_0_), channel_id=1, source_target_pairs={{0,96},{4,100},{8,104},{12,108},{16,112},{20,116},{24,120},{28,124... | collective-permute-start | bytes 196616 | tf_op jit(solution)/shard_map/ppermute | solution.py:347
  115.9 28.1 %collective-permute-start.11 = (f32[128,128]{1,0:T(8,128)S(1)}, f32[128,128]{1,0:T(8,128)S(1)}, u32[]{:S(2)}, u32[]{:S(2)}) collective-permute-start(f32[128,128]{1,0:T(8,128)S(1)} %add_add_fusion.2.refs_0_), channel_id=1, source_target_pairs={{0,32},{4,36},{8,40},{12,44},{16,48},{20,52},{24,56},{28,60},{32,6... | collective-permute-start | bytes 196616 | tf_op jit(solution)/shard_map/ppermute | solution.py:347
  115.9 28.1 %collective-permute-start.10 = (f32[128,128]{1,0:T(8,128)S(1)}, f32[128,128]{1,0:T(8,128)S(1)}, u32[]{:S(2)}, u32[]{:S(2)}) collective-permute-start(f32[128,128]{1,0:T(8,128)S(1)} %add_add_fusion.2.refs_0_), channel_id=1, source_target_pairs={{0,64},{4,68},{8,72},{12,76},{16,80},{20,84},{24,88},{28,92},{32,9... | collective-permute-start | bytes 196616 | tf_op jit(solution)/shard_map/ppermute | solution.py:347
  138.5 8.8 %collective-permute-start.7 = (s16[1040,128]{1,0:T(8,128)(2,1)S(1)}, s16[1040,128]{1,0:T(8,128)(2,1)S(1)}, u32[]{:S(2)}, u32[]{:S(2)}) collective-permute-start(s16[1040,128]{1,0:T(8,128)(2,1)S(1)} %get-tuple-element.23), channel_id=1, source_target_pairs={{0,2},{1,3},{2,0},{3,1},{4,6},{5,7},{6,4},{7,5},{8,10},{9,11},{10,... | collective-permute-start | bytes 798728 | tf_op jit(solution)/shard_map/ppermute | solution.py:383
  141.3 12.6 %collective-permute-start.8 = (s16[1040,128]{1,0:T(8,128)(2,1)S(1)}, s16[1040,128]{1,0:T(8,128)(2,1)S(1)}, u32[]{:S(2)}, u32[]{:S(2)}) collective-permute-start(s16[1040,128]{1,0:T(8,128)(2,1)S(1)} %get-tuple-element.24), channel_id=1, source_target_pairs={{0,1},{1,2},{2,3},{3,0},{4,5},{5,6},{6,7},{7,4},{8,9},{9,10},{10,1... | collective-permute-start | bytes 798728 | tf_op jit(solution)/shard_map/ppermute | solution.py:383
  141.7 12.2 %collective-permute-start.9 = (s16[1040,128]{1,0:T(8,128)(2,1)S(1)}, s16[1040,128]{1,0:T(8,128)(2,1)S(1)}, u32[]{:S(2)}, u32[]{:S(2)}) collective-permute-start(s16[1040,128]{1,0:T(8,128)(2,1)S(1)} %get-tuple-element.25), channel_id=1, source_target_pairs={{0,3},{1,0},{2,1},{3,2},{4,7},{5,4},{6,5},{7,6},{8,11},{9,8},{10,9... | collective-permute-start | bytes 798728 | tf_op jit(solution)/shard_map/ppermute | solution.py:383
  144.0 20.3 %collective-permute-start.15 = (f32[128,128]{1,0:T(8,128)S(1)}, f32[128,128]{1,0:T(8,128)S(1)}, u32[]{:S(2)}, u32[]{:S(2)}) collective-permute-start(f32[128,128]{1,0:T(8,128)S(1)} %add_add_fusion.1), channel_id=1, source_target_pairs={{0,24},{4,28},{8,0},{12,4},{16,8},{20,12},{24,16},{28,20},{32,56},... | collective-permute-start | bytes 196616 | tf_op jit(solution)/shard_map/ppermute | solution.py:347
  147.2 17.1 %collective-permute-start.14 = (f32[128,128]{1,0:T(8,128)S(1)}, f32[128,128]{1,0:T(8,128)S(1)}, u32[]{:S(2)}, u32[]{:S(2)}) collective-permute-start(f32[128,128]{1,0:T(8,128)S(1)} %add_add_fusion.1), channel_id=1, source_target_pairs={{0,8},{4,12},{8,16},{12,20},{16,24},{20,28},{24,0},{28,4},{32,40},... | collective-permute-start | bytes 196616 | tf_op jit(solution)/shard_map/ppermute | solution.py:347
  147.4 17.0 %collective-permute-start.13 = (f32[128,128]{1,0:T(8,128)S(1)}, f32[128,128]{1,0:T(8,128)S(1)}, u32[]{:S(2)}, u32[]{:S(2)}) collective-permute-start(f32[128,128]{1,0:T(8,128)S(1)} %add_add_fusion.1), channel_id=1, source_target_pairs={{0,16},{4,20},{8,24},{12,28},{16,0},{20,4},{24,8},{28,12},{32,48},... | collective-permute-start | bytes 196616 | tf_op jit(solution)/shard_map/ppermute | solution.py:347
  155.8 18.6 %all-to-all-start.2 = ((f32[128,2,128]{2,1,0:T(2,128)}), f32[128,2,128]{2,1,0:T(2,128)S(1)}, u32[]{:S(2)}, u32[]{:S(2)}) async-start(f32[128,2,128]{2,1,0:T(2,128)} %bitcast.8), calls=%async_computation.2 | async-start | bytes 262144 | tf_op jit(solution)/shard_map/all_to_all | solution.py:331
  175.3 14.1 %all-to-all-start.3 = ((f32[128,2,128]{2,1,0:T(2,128)}), f32[128,2,128]{2,1,0:T(2,128)S(1)}, u32[]{:S(2)}, u32[]{:S(2)}) async-start(f32[128,2,128]{2,1,0:T(2,128)} %broadcast_in_dim.2), calls=%async_computation.3 | async-start | bytes 262144 | tf_op jit(solution)/shard_map/all_to_all | solution.py:334

commit v6 on v4

--- a/solution.py
+++ b/solution.py
@@ -9,8 +9,9 @@
 
 BR_DEV = 16
 HALF = 128
-GROUP = 22
 LOADS = 8
+AHEAD = 2
+LIMIT = 44 * 2**20
 STEP = 32704.0
 LEAST = 2.0**-80
 HIGHEST = lax.Precision.HIGHEST
@@ -63,7 +64,7 @@
     *_, total, values, arrived, value_sems, arrived_sems = refs
     outs = refs[-5 - shares : -5]
     count, loads, parts = values.shape[0], value_sems.shape[0], arrived_sems.shape[0]
-    assert count % GROUP == 0 and loads * GROUP % count == 0 and count % loads == 0
+    assert count % loads == 0 and AHEAD <= loads
 
     def bring(i):
         part = pl.ds(i * (count // loads), count // loads)
@@ -75,18 +76,21 @@
 
     for i in range(parts):
         bring_basis(i).start()
-    for i in range(loads):
+    for i in range(AHEAD):
         bring(i).start()
     total[...] = jnp.zeros_like(total)
     for i in range(parts):
         bring_basis(i).wait()
 
-    @pl.loop(0, count // GROUP)
+    @pl.loop(0, loads)
     def _(step):
-        for i in range(loads * GROUP // count):
-            bring(step * (loads * GROUP // count) + i).wait()
-        for u in range(GROUP):
-            t = step * GROUP + u
+        @pl.when(step + AHEAD < loads)
+        def _():
+            bring(step + AHEAD).start()
+
+        bring(step).wait()
+        for u in range(count // loads):
+            t = step * (count // loads) + u
             total[blocks[t]] += jnp.dot(values[t], arrived[places[t]], preferred_element_type=F32)
 
     each = BR_DEV // shares
@@ -117,7 +121,7 @@
             pltpu.SemaphoreType.DMA((4,)),
         ],
         out_shape=[jax.ShapeDtypeStruct((rows + 16, HALF), jnp.int16)] * shares,
-        compiler_params=pltpu.CompilerParams(vmem_limit_bytes=44 * 2**20),
+        compiler_params=pltpu.CompilerParams(vmem_limit_bytes=LIMIT),
         cost_estimate=pl.CostEstimate(
             flops=2 * count * height * depth * HALF,
             bytes_accessed=count * height * depth * 2 + arrived.size * 2,
@@ -153,32 +157,50 @@
     return y
 
 
-def gram_kernel(shares, *refs):
-    coded, before, (y_out, gram_out) = refs[:shares], refs[shares:-2], refs[-2:]
+def gram_first_kernel(shares, *refs):
+    coded, (y_out, gram_out) = refs[:shares], refs[shares:]
     y = decode(coded)
     y_out[...] = y
-    at = 0
-    for ref in before:
-        gram_out[pl.ds(at, HALF)] = dot_t(ref[...], y)
-        at += HALF
-    gram_out[pl.ds(at, HALF)] = dot_t(y, y)
-
-
-def gram(coded, before):
-    rows = coded[0].shape[0] - 16
-    height = HALF * (len(before) + 1)
+    gram_out[...] = dot_t(y, y)
+
+
+def gram_last_kernel(shares, core, before, *refs):
+    coded, (y_out, mine_out, other_out) = refs[:shares], refs[-3:]
+    y = decode(coded)
+    y_out[...] = y
+    cross, square = dot_t(before[...], y), dot_t(y, y)
+    mine_out[...] = jnp.where(core[0] == 0, cross, square)
+    other_out[...] = jnp.where(core[0] == 0, square, cross)
+
+
+def gram_call(kernel, operands, in_specs, rows, grams, name):
     return pl.pallas_call(
-        functools.partial(gram_kernel, len(coded)),
-        out_shape=(
-            jax.ShapeDtypeStruct((rows, HALF), F32),
-            jax.ShapeDtypeStruct((height, HALF), F32),
-        ),
+        kernel,
+        in_specs=in_specs,
+        out_shape=[jax.ShapeDtypeStruct((rows, HALF), F32)]
+        + [jax.ShapeDtypeStruct((HALF, HALF), F32)] * grams,
         compiler_params=pltpu.CompilerParams(vmem_limit_bytes=16 * 2**20),
         cost_estimate=pl.CostEstimate(
-            flops=12 * rows * height * HALF, bytes_accessed=rows * HALF * 12, transcendentals=0
-        ),
-        name=f"gram{len(before)}",
-    )(*coded, *before)
+            flops=12 * rows * grams * HALF * HALF, bytes_accessed=rows * HALF * 12, transcendentals=0
+        ),
+        name=name,
+    )(*operands)
+
+
+def gram_first(coded):
+    rows = coded[0].shape[0] - 16
+    whole = pl.BlockSpec(memory_space=pltpu.VMEM)
+    kernel = functools.partial(gram_first_kernel, len(coded))
+    return gram_call(kernel, coded, [whole] * len(coded), rows, 1, "gram0")
+
+
+def gram_last(coded, before, core, after):
+    rows = coded[0].shape[0] - 16
+    whole = pl.BlockSpec(memory_space=pltpu.VMEM)
+    kernel = functools.partial(gram_last_kernel, len(coded))
+    specs = [pl.BlockSpec(memory_space=pltpu.SMEM), whole]
+    specs += [whole] * len(coded) + [pl.BlockSpec(memory_space=pl.ANY)]
+    return gram_call(kernel, [core, before, *coded, after], specs, rows, 2, "gram1")
 
 
 def factor64(a):
@@ -283,9 +305,11 @@
     )(g, y)
 
 
-def last_kernel(scale, g_ref, r_ref, t_ref, z_ref, y_ref, basis_out, triangle_out):
-    r01 = dot_n(t_ref[...], g_ref[pl.ds(0, HALF)])
-    r11, t11 = factor128(g_ref[pl.ds(HALF, HALF)] - dot_t(r01, r01))
+def last_kernel(scale, core, mine, other, r_ref, t_ref, z_ref, y_ref, basis_out, triangle_out):
+    cross = jnp.where(core[0] == 0, mine[...], other[...])
+    square = jnp.where(core[0] == 0, other[...], mine[...])
+    r01 = dot_n(t_ref[...], cross)
+    r11, t11 = factor128(square - dot_t(r01, r01))
     z = z_ref[...]
     basis_out[:, pl.ds(0, HALF)] = z * scale
     basis_out[:, pl.ds(HALF, HALF)] = dot_bt(
@@ -299,52 +323,37 @@
     triangle_out[pl.ds(HALF, HALF), pl.ds(HALF, HALF)] = r11 * share
 
 
-def last(g, r, t, z, y, scale):
+def last(core, mine, other, r, t, z, y, scale):
     return pl.pallas_call(
         functools.partial(last_kernel, scale),
+        in_specs=[pl.BlockSpec(memory_space=pltpu.SMEM)]
+        + [pl.BlockSpec(memory_space=pltpu.VMEM)] * 6,
         out_shape=(
             jax.ShapeDtypeStruct((y.shape[0], 2 * HALF), F32),
             jax.ShapeDtypeStruct((2 * HALF, 2 * HALF), F32),
         ),
         compiler_params=pltpu.CompilerParams(vmem_limit_bytes=16 * 2**20),
         name="last",
-    )(g, r, t, z, y)
-
-
-def sum_all(part):
-    axes = ("row", "col")
-    n = lax.axis_size("row") * lax.axis_size("col")
-    height = part.shape[0]
-    pieces = lax.all_to_all(part.reshape(n, height // n, HALF), axes, 0, 0, tiled=True)
-    share = jnp.sum(pieces, axis=0, keepdims=True)
-    copies = jnp.broadcast_to(share, (n, height // n, HALF))
-    return lax.all_to_all(copies, axes, 0, 0, tiled=True).reshape(height, HALF)
-
-
-def sum_along(part):
+    )(core, mine, other, r, t, z, y)
+
+
+def swap_cores(part):
+    return lax.ppermute(part, "row", [(i, i ^ 1) for i in range(lax.axis_size("row"))])
+
+
+def sum_chips(part):
     rows, cols = lax.axis_size("row"), lax.axis_size("col")
     steps = []
-    for axis, size, stride, length in (
-        ("row", rows, 1, 2),
-        ("col", cols, 1, cols),
-        ("row", rows, 8, 4),
-        ("row", rows, 2, 4),
-    ):
-        arrived = [
+    for axis, size, stride in (("col", cols, 1), ("row", rows, 8), ("row", rows, 2)):
+        two, one, three = (
             lax.ppermute(
                 part,
                 axis,
-                [
-                    (i, i + ((i // stride + k) % length - i // stride % length) * stride)
-                    for i in range(size)
-                ],
+                [(i, i + ((i // stride + k) % 4 - i // stride % 4) * stride) for i in range(size)],
             )
-            for k in range(1, length)
-        ]
-        if length == 2:
-            part = part + arrived[0]
-        else:
-            part = (part + arrived[1]) + (arrived[0] + arrived[2])
+            for k in (2, 1, 3)
+        )
+        part = (part + two) + (one + three)
         steps.append(part)
     return steps
 
@@ -371,11 +380,13 @@
             for k in sorted(range(1, cols), key=lambda k: -min(k, cols - k))
         ]
 
-    y0, g0 = gram(product(0, ()), ())
-    steps = sum_along(g0)
+    core = lax.rem(lax.axis_index("row"), 2).reshape(1)
+    y0, g0 = gram_first(product(0, ()))
+    steps = sum_chips(g0 + swap_cores(g0))
     r, t, z = first(steps[-1], y0, scale)
-    y1, g1 = gram(product(1, (steps[1],)), (y0,))
-    return last(sum_all(g1), r, t, z, y1, scale)
+    y1, mine, other = gram_last(product(1, (steps[1],)), y0, core, z)
+    mine = sum_chips(mine + swap_cores(other))[-1]
+    return last(core, mine, swap_cores(mine), r, t, z, y1, scale)
 
 
 def solution(mesh):

time: 202 us -> 201 us (level)
  Pallas kernels: 57.9 us -> 48.2 us
  waiting for transfers between devices: 87.5 us -> 94.6 us
  starting transfers between devices: 54.4 us -> 57.3 us
    ppermute x10 -> x21, waiting for transfers between devices: 5.97 us -> 32.3 us  [the longest x18 29.6 us: sum_chips(): lax.ppermute(part, axis, [(i, i + ((i // stride + k) % 4 - i // stride %...]
    ppermute x10 -> x21, starting transfers between devices: 13.8 us -> 29.5 us  [the longest x18 22.4 us: sum_chips(): lax.ppermute(part, axis, [(i, i + ((i // stride + k) % 4 - i // stride %...]
    all_to_all x2 -> x0, waiting for transfers between devices: 14.1 us -> none  [the longest x1 10 us: sum_all(): lax.all_to_all(part.reshape(n, height // n, HALF), axes, 0, 0, tiled=True)]
    all_to_all x2 -> x0, starting transfers between devices: 12.7 us -> none  [the longest x1 8.65 us: sum_all(): lax.all_to_all(part.reshape(n, height // n, HALF), axes, 0, 0, tiled=True)]
    pallas_call x2, Pallas kernels: 33.4 us -> 24.4 us  [tiles(): pl.pallas_call(functools.partial(tiles_kernel, shares), in_specs=inputs,...]
    all_to_all x2, waiting for transfers between devices: 52.5 us -> 48.4 us  [product(): arrived = lax.all_to_all(packed[half], 'row', 0, 0, tiled=True)]
  transfers between devices with their start and end apart: 20 -> 29, of which waited for: 10 -> 19; matrix products, arithmetic and copies ran while one was open for 0% -> 0% of each run, Pallas kernels for 23% -> 17%
where the time goes in v6:
time: 201 us
  waiting for transfers between devices  94.6 us (47%)
  starting transfers between devices  57.3 us (29%)
  Pallas kernels  48.2 us (24%)
    all_to_all x2, waiting for transfers between devices, product(): arrived = lax.all_to_all(packed[half], 'row', 0, 0, tiled=True)  48.4 us
    ppermute x18, waiting for transfers between devices, sum_chips(): lax.ppermute(part, axis, [(i, i + ((i // stride + k) % 4 - i // stride %...  29.6 us
    pallas_call x2, Pallas kernels, tiles(): pl.pallas_call(functools.partial(tiles_kernel, shares), in_specs=inputs,...  24.4 us
    ppermute x18, starting transfers between devices, sum_chips(): lax.ppermute(part, axis, [(i, i + ((i // stride + k) % 4 - i // stride %...  22.4 us
    all_to_all x2, starting transfers between devices, product(): arrived = lax.all_to_all(packed[half], 'row', 0, 0, tiled=True)  16.8 us
    ppermute x6, waiting for transfers between devices, product(): lax.ppermute(coded[k], 'col', [(i, (i + k) % cols) for i in range(cols)])  13.9 us
    ppermute x6, starting transfers between devices, product(): lax.ppermute(coded[k], 'col', [(i, (i + k) % cols) for i in range(cols)])  11 us
    pallas_call x1, Pallas kernels, last(): pl.pallas_call(functools.partial(last_kernel, scale), in_specs=[pl.BlockS...  8.2 us
  transfers between devices with their start and end apart: 29, of which 19 were waited for; matrix products, arithmetic and copies ran while one was open for 0% of the time, Pallas kernels for 17%

profile of v6, /device:TPU:1, one launch (start us, length us, event | category | flops | bytes accessed | tf_op | source)
XLA Modules:
  0.0 201.0 jit_solution(229599010445336086)
XLA Ops:
  0.6 3.8 %pack0.1 = bf16[64,256,128]{2,1,0:T(8,128)(2,1)} custom-call(s32[2,32]{1,0:T(2,128)} %bitcast.17, bf16[8,256,256]{2,1,0:T(8,128)(2,1)} %bitcast.15), custom_call_target="tpu_custom_call" | custom-call | bytes 8388608 | tf_op jit(solution)/shard_map/pack0/pallas_call | solution.py:40
  4.4 9.7 %all-to-all-start = ((bf16[64,256,128]{2,1,0:T(8,128)(2,1)}), bf16[64,256,128]{2,1,0:T(8,128)(2,1)}, u32[]{:S(2)}, u32[]{:S(2)}) async-start(bf16[64,256,128]{2,1,0:T(8,128)(2,1)} %pack0.1), calls=%async_computation | async-start | bytes 8388608 | tf_op jit(solution)/shard_map/all_to_all | solution.py:376
  14.1 3.8 %pack1.1 = bf16[64,256,128]{2,1,0:T(8,128)(2,1)} custom-call(s32[2,32]{1,0:T(2,128)} %bitcast.18, bf16[8,256,256]{2,1,0:T(8,128)(2,1)} %bitcast.16), custom_call_target="tpu_custom_call" | custom-call | bytes 8388608 | tf_op jit(solution)/shard_map/pack1/pallas_call | solution.py:40
  17.9 48.4 %all-to-all-done.arrived_hbm = bf16[64,256,128]{2,1,0:T(8,128)(2,1)} async-done(((bf16[64,256,128]{2,1,0:T(8,128)(2,1)}), bf16[64,256,128]{2,1,0:T(8,128)(2,1)}, u32[]{:S(2)}, u32[]{:S(2)}) %all-to-all-start) | async-done | bytes 4194336 | tf_op jit(solution)/shard_map/all_to_all | solution.py:376
  66.3 7.2 %all-to-all-start.1 = ((bf16[64,256,128]{2,1,0:T(8,128)(2,1)}), bf16[64,256,128]{2,1,0:T(8,128)(2,1)}, u32[]{:S(2)}, u32[]{:S(2)}) async-start(bf16[64,256,128]{2,1,0:T(8,128)(2,1)} %pack1.1), calls=%async_computation.1 | async-start | bytes 8388608 | tf_op jit(solution)/shard_map/all_to_all | solution.py:376
  73.6 12.2 %tiles0.1 = (s16[1040,128]{1,0:T(8,128)(2,1)S(1)}, s16[1040,128]{1,0:T(8,128)(2,1)S(1)}, s16[1040,128]{1,0:T(8,128)(2,1)S(1)}, s16[1040,128]{1,0:T(8,128)(2,1)S(1)}) custom-call(s32[1]{0:T(128)} %bitcast.1.me, s32[176]{0:T(256)S(1)} %bitcast.9, s32[176]{0:T(256)S(1)} %bitcast.11, bf16[176,256,256]{2,1,0:T(8,128)(2,1)} %bitcast.13, ...), custom_call_target="tpu_custom_call" | custom-call | flops 2952790016 | bytes 27262976 | tf_op jit(solution)/shard_map/tiles0/pallas_call | solution.py:112
  85.8 2.8 %collective-permute-start = (s16[1040,128]{1,0:T(8,128)(2,1)S(1)}, s16[1040,128]{1,0:T(8,128)(2,1)S(1)}, u32[]{:S(2)}, u32[]{:S(2)}) collective-permute-start(s16[1040,128]{1,0:T(8,128)(2,1)S(1)} %get-tuple-element.19), channel_id=1, source_target_pairs={{0,2},{1,3},{2,0},{3,1},{4,6},{5,7},{6,4},{7,5},{8,10},{9,11},{10,... | collective-permute-start | bytes 798728 | tf_op jit(solution)/shard_map/ppermute | solution.py:379
  88.9 2.4 %collective-permute-start.2 = (s16[1040,128]{1,0:T(8,128)(2,1)S(1)}, s16[1040,128]{1,0:T(8,128)(2,1)S(1)}, u32[]{:S(2)}, u32[]{:S(2)}) collective-permute-start(s16[1040,128]{1,0:T(8,128)(2,1)S(1)} %get-tuple-element.21), channel_id=1, source_target_pairs={{0,3},{1,0},{2,1},{3,2},{4,7},{5,4},{6,5},{7,6},{8,11},{9,8},{10,9... | collective-permute-start | bytes 798728 | tf_op jit(solution)/shard_map/ppermute | solution.py:379
  91.3 3.9 %collective-permute-done.refs_1_ = s16[1040,128]{1,0:T(8,128)(2,1)S(1)} collective-permute-done((s16[1040,128]{1,0:T(8,128)(2,1)S(1)}, s16[1040,128]{1,0:T(8,128)(2,1)S(1)}, u32[]{:S(2)}, u32[]{:S(2)}) %collective-permute-start) | collective-permute-done | bytes 266272 | tf_op jit(solution)/shard_map/ppermute | solution.py:379
  95.2 6.3 %collective-permute-done.1.refs_2_ = s16[1040,128]{1,0:T(8,128)(2,1)S(1)} collective-permute-done((s16[1040,128]{1,0:T(8,128)(2,1)S(1)}, s16[1040,128]{1,0:T(8,128)(2,1)S(1)}, u32[]{:S(2)}, u32[]{:S(2)}) %collective-permute-start.1) | collective-permute-done | bytes 266272 | tf_op jit(solution)/shard_map/ppermute | solution.py:379
  105.0 1.5 collective-permute-start.6
  108.6 3.0 %collective-permute-done.4 = f32[128,128]{1,0:T(8,128)S(1)} collective-permute-done((f32[128,128]{1,0:T(8,128)S(1)}, f32[128,128]{1,0:T(8,128)S(1)}, u32[]{:S(2)}, u32[]{:S(2)}) %collective-permute-start.4) | collective-permute-done | bytes 65568 | tf_op jit(solution)/shard_map/ppermute | solution.py:349
  112.6 1.7 collective-permute-start.9
  115.6 8.9 %collective-permute-done.8 = f32[128,128]{1,0:T(8,128)S(1)} collective-permute-done((f32[128,128]{1,0:T(8,128)S(1)}, f32[128,128]{1,0:T(8,128)S(1)}, u32[]{:S(2)}, u32[]{:S(2)}) %collective-permute-start.8) | collective-permute-done | bytes 65568 | tf_op jit(solution)/shard_map/ppermute | solution.py:349
  124.5 1.3 collective-permute-done.9
  125.8 2.6 %collective-permute-done.7 = f32[128,128]{1,0:T(8,128)S(1)} collective-permute-done((f32[128,128]{1,0:T(8,128)S(1)}, f32[128,128]{1,0:T(8,128)S(1)}, u32[]{:S(2)}, u32[]{:S(2)}) %collective-permute-start.7) | collective-permute-done | bytes 65568 | tf_op jit(solution)/shard_map/ppermute | solution.py:349
  128.5 3.3 %collective-permute-start.14 = (f32[128,128]{1,0:T(8,128)S(1)}, f32[128,128]{1,0:T(8,128)S(1)}, u32[]{:S(2)}, u32[]{:S(2)}) collective-permute-start(f32[128,128]{1,0:T(8,128)S(1)} %add_add_fusion.4.refs_0_), channel_id=1, source_target_pairs={{0,8},{4,12},{8,16},{12,20},{16,24},{20,28},{24,0},{28,4},{32,40},... | collective-permute-start | bytes 196616 | tf_op jit(solution)/shard_map/ppermute | solution.py:349
  131.7 1.9 collective-permute-start.13
  133.6 12.2 %tiles1.1 = (s16[1040,128]{1,0:T(8,128)(2,1)S(1)}, s16[1040,128]{1,0:T(8,128)(2,1)S(1)}, s16[1040,128]{1,0:T(8,128)(2,1)S(1)}, s16[1040,128]{1,0:T(8,128)(2,1)S(1)}) custom-call(s32[1]{0:T(128)} %bitcast.1.me, s32[176]{0:T(256)S(1)} %bitcast.10, s32[176]{0:T(256)S(1)} %bitcast.12, bf16[176,256,256]{2,1,0:T(8,128)(2,1)} %bitcast.14, ...), custom_call_target="tpu_custom_call" | custom-call | flops 2952790016 | bytes 27262976 | tf_op jit(solution)/shard_map/tiles1/pallas_call | solution.py:112
  145.8 2.8 %collective-permute-start.10 = (s16[1040,128]{1,0:T(8,128)(2,1)S(1)}, s16[1040,128]{1,0:T(8,128)(2,1)S(1)}, u32[]{:S(2)}, u32[]{:S(2)}) collective-permute-start(s16[1040,128]{1,0:T(8,128)(2,1)S(1)} %get-tuple-element.25), channel_id=1, source_target_pairs={{0,2},{1,3},{2,0},{3,1},{4,6},{5,7},{6,4},{7,5},{8,10},{9,11},{10,... | collective-permute-start | bytes 798728 | tf_op jit(solution)/shard_map/ppermute | solution.py:379
  148.9 2.4 %collective-permute-start.12 = (s16[1040,128]{1,0:T(8,128)(2,1)S(1)}, s16[1040,128]{1,0:T(8,128)(2,1)S(1)}, u32[]{:S(2)}, u32[]{:S(2)}) collective-permute-start(s16[1040,128]{1,0:T(8,128)(2,1)S(1)} %get-tuple-element.27), channel_id=1, source_target_pairs={{0,3},{1,0},{2,1},{3,2},{4,7},{5,4},{6,5},{7,6},{8,11},{9,8},{10,9... | collective-permute-start | bytes 798728 | tf_op jit(solution)/shard_map/ppermute | solution.py:379
  151.3 6.0 %first.1 = (f32[128,128]{1,0:T(8,128)S(1)}, f32[128,128]{1,0:T(8,128)S(1)}, f32[1024,128]{1,0:T(8,128)S(1)}) custom-call(f32[128,128]{1,0:T(8,128)S(1)} %add_add_fusion.3.g_ref, f32[1024,128]{1,0:T(8,128)S(1)} %get-tuple-element.22.y_ref.before), custom_call_target="tpu_custom_call" | custom-call | flops 20971520000 | bytes 1048576 | tf_op jit(solution)/shard_map/first/pallas_call | solution.py:293
  157.3 3.7 %collective-permute-done.11.refs_2_ = s16[1040,128]{1,0:T(8,128)(2,1)S(1)} collective-permute-done((s16[1040,128]{1,0:T(8,128)(2,1)S(1)}, s16[1040,128]{1,0:T(8,128)(2,1)S(1)}, u32[]{:S(2)}, u32[]{:S(2)}) %collective-permute-start.11) | collective-permute-done | bytes 266272 | tf_op jit(solution)/shard_map/ppermute | solution.py:379
  165.5 1.5 collective-permute-start.19
  168.6 3.0 %collective-permute-done.17 = f32[128,128]{1,0:T(8,128)S(1)} collective-permute-done((f32[128,128]{1,0:T(8,128)S(1)}, f32[128,128]{1,0:T(8,128)S(1)}, u32[]{:S(2)}, u32[]{:S(2)}) %collective-permute-start.17) | collective-permute-done | bytes 65568 | tf_op jit(solution)/shard_map/ppermute | solution.py:349
  171.7 2.7 %collective-permute-start.22 = (f32[128,128]{1,0:T(8,128)S(1)}, f32[128,128]{1,0:T(8,128)S(1)}, u32[]{:S(2)}, u32[]{:S(2)}) collective-permute-start(f32[128,128]{1,0:T(8,128)S(1)} %add_add_fusion.2), channel_id=1, source_target_pairs={{0,96},{4,100},{8,104},{12,108},{16,112},{20,116},{24,120},{28,124... | collective-permute-start | bytes 196616 | tf_op jit(solution)/shard_map/ppermute | solution.py:349
  174.3 1.6 collective-permute-done.21
  176.3 2.8 %collective-permute-done.20 = f32[128,128]{1,0:T(8,128)S(1)} collective-permute-done((f32[128,128]{1,0:T(8,128)S(1)}, f32[128,128]{1,0:T(8,128)S(1)}, u32[]{:S(2)}, u32[]{:S(2)}) %collective-permute-start.20) | collective-permute-done | bytes 65568 | tf_op jit(solution)/shard_map/ppermute | solution.py:349
  179.2 2.7 %collective-permute-start.25 = (f32[128,128]{1,0:T(8,128)S(1)}, f32[128,128]{1,0:T(8,128)S(1)}, u32[]{:S(2)}, u32[]{:S(2)}) collective-permute-start(f32[128,128]{1,0:T(8,128)S(1)} %add_add_fusion.1), channel_id=1, source_target_pairs={{0,24},{4,28},{8,0},{12,4},{16,8},{20,12},{24,16},{28,20},{32,56},... | collective-permute-start | bytes 196616 | tf_op jit(solution)/shard_map/ppermute | solution.py:349
  183.5 3.0 %collective-permute-done.23 = f32[128,128]{1,0:T(8,128)S(1)} collective-permute-done((f32[128,128]{1,0:T(8,128)S(1)}, f32[128,128]{1,0:T(8,128)S(1)}, u32[]{:S(2)}, u32[]{:S(2)}) %collective-permute-start.23) | collective-permute-done | bytes 65568 | tf_op jit(solution)/shard_map/ppermute | solution.py:349
  186.5 5.5 %collective-permute-start.26 = (f32[128,128]{1,0:T(8,128)S(1)}, f32[128,128]{1,0:T(8,128)S(1)}, u32[]{:S(2)}, u32[]{:S(2)}) collective-permute-start(f32[128,128]{1,0:T(8,128)S(1)} %add_add_fusion.mine), channel_id=1, source_target_pairs={{0,4},{4,0},{8,12},{12,8},{16,20},{20,16},{24,28},{28,24},{32,36},... | collective-permute-start | bytes 196616 | tf_op jit(solution)/shard_map/ppermute | solution.py:341
  192.8 8.2 %last.1 = (f32[1024,256]{1,0:T(8,128)}, f32[256,256]{1,0:T(8,128)}) custom-call(s32[1]{0:T(128)} %bitcast.core, f32[128,128]{1,0:T(8,128)S(1)} %add_add_fusion.mine, f32[128,128]{1,0:T(8,128)S(1)} %collective-permute-done.26.other, f32[128,128]{1,0:T(8,128)S(1)} %get-tuple-element.31.r_ref, f32[128,128]{1,0:T(8,128)S(1)} %get-tuple-element.32.t_ref, ...), custom_call_target="tpu_custom_call" | custom-call | tf_op jit(solution)/shard_map/last/pallas_call | solution.py:327
  (49 shorter events, 17.8 us)
Async XLA Ops:
  4.4 61.9 %all-to-all-start = ((bf16[64,256,128]{2,1,0:T(8,128)(2,1)}), bf16[64,256,128]{2,1,0:T(8,128)(2,1)}, u32[]{:S(2)}, u32[]{:S(2)}) async-start(bf16[64,256,128]{2,1,0:T(8,128)(2,1)} %pack0.1), calls=%async_computation | async-start | bytes 8388608 | tf_op jit(solution)/shard_map/all_to_all | solution.py:376
  17.9 55.6 %copy-start.1 = (s32[176,1]{0,1:T(1,128)S(1)}, s32[176,1]{0,1:T(1,128)}, u32[]{:S(2)}) copy-start(s32[176,1]{0,1:T(1,128)} %param.9) | copy-start | bytes 2116
  17.9 55.6 %copy-start.2 = (s32[176,1]{0,1:T(1,128)S(1)}, s32[176,1]{0,1:T(1,128)}, u32[]{:S(2)}) copy-start(s32[176,1]{0,1:T(1,128)} %param.8) | copy-start | bytes 2116
  17.9 55.6 %copy-start = (s32[176,1]{0,1:T(1,128)S(1)}, s32[176,1]{0,1:T(1,128)}, u32[]{:S(2)}) copy-start(s32[176,1]{0,1:T(1,128)} %param.7) | copy-start | bytes 2116
  66.3 67.3 %all-to-all-start.1 = ((bf16[64,256,128]{2,1,0:T(8,128)(2,1)}), bf16[64,256,128]{2,1,0:T(8,128)(2,1)}, u32[]{:S(2)}, u32[]{:S(2)}) async-start(bf16[64,256,128]{2,1,0:T(8,128)(2,1)} %pack1.1), calls=%async_computation.1 | async-start | bytes 8388608 | tf_op jit(solution)/shard_map/all_to_all | solution.py:376
  85.8 9.4 %collective-permute-start = (s16[1040,128]{1,0:T(8,128)(2,1)S(1)}, s16[1040,128]{1,0:T(8,128)(2,1)S(1)}, u32[]{:S(2)}, u32[]{:S(2)}) collective-permute-start(s16[1040,128]{1,0:T(8,128)(2,1)S(1)} %get-tuple-element.19), channel_id=1, source_target_pairs={{0,2},{1,3},{2,0},{3,1},{4,6},{5,7},{6,4},{7,5},{8,10},{9,11},{10,... | collective-permute-start | bytes 798728 | tf_op jit(solution)/shard_map/ppermute | solution.py:379
  88.6 12.9 %collective-permute-start.1 = (s16[1040,128]{1,0:T(8,128)(2,1)S(1)}, s16[1040,128]{1,0:T(8,128)(2,1)S(1)}, u32[]{:S(2)}, u32[]{:S(2)}) collective-permute-start(s16[1040,128]{1,0:T(8,128)(2,1)S(1)} %get-tuple-element.20), channel_id=1, source_target_pairs={{0,1},{1,2},{2,3},{3,0},{4,5},{5,6},{6,7},{7,4},{8,9},{9,10},{10,1... | collective-permute-start | bytes 798728 | tf_op jit(solution)/shard_map/ppermute | solution.py:379
  88.9 12.6 %collective-permute-start.2 = (s16[1040,128]{1,0:T(8,128)(2,1)S(1)}, s16[1040,128]{1,0:T(8,128)(2,1)S(1)}, u32[]{:S(2)}, u32[]{:S(2)}) collective-permute-start(s16[1040,128]{1,0:T(8,128)(2,1)S(1)} %get-tuple-element.21), channel_id=1, source_target_pairs={{0,3},{1,0},{2,1},{3,2},{4,7},{5,4},{6,5},{7,6},{8,11},{9,8},{10,9... | collective-permute-start | bytes 798728 | tf_op jit(solution)/shard_map/ppermute | solution.py:379
  102.3 1.5 collective-permute-start.3
  103.8 4.8 %collective-permute-start.5 = (f32[128,128]{1,0:T(8,128)S(1)}, f32[128,128]{1,0:T(8,128)S(1)}, u32[]{:S(2)}, u32[]{:S(2)}) collective-permute-start(f32[128,128]{1,0:T(8,128)S(1)} %add.67), channel_id=1, source_target_pairs={{0,1},{1,2},{2,3},{3,0},{4,5},{5,6},{6,7},{7,4},{8,9},{9,10},{10,1... | collective-permute-start | bytes 196616 | tf_op jit(solution)/shard_map/ppermute | solution.py:349
  105.0 3.6 %collective-permute-start.6 = (f32[128,128]{1,0:T(8,128)S(1)}, f32[128,128]{1,0:T(8,128)S(1)}, u32[]{:S(2)}, u32[]{:S(2)}) collective-permute-start(f32[128,128]{1,0:T(8,128)S(1)} %add.67), channel_id=1, source_target_pairs={{0,3},{1,0},{2,1},{3,2},{4,7},{5,4},{6,5},{7,6},{8,11},{9,8},{10,9... | collective-permute-start | bytes 196616 | tf_op jit(solution)/shard_map/ppermute | solution.py:349
  106.5 5.0 %collective-permute-start.4 = (f32[128,128]{1,0:T(8,128)S(1)}, f32[128,128]{1,0:T(8,128)S(1)}, u32[]{:S(2)}, u32[]{:S(2)}) collective-permute-start(f32[128,128]{1,0:T(8,128)S(1)} %add.67), channel_id=1, source_target_pairs={{0,2},{1,3},{2,0},{3,1},{4,6},{5,7},{6,4},{7,5},{8,10},{9,11},{10,... | collective-permute-start | bytes 196616 | tf_op jit(solution)/shard_map/ppermute | solution.py:349
  111.6 13.0 %collective-permute-start.8 = (f32[128,128]{1,0:T(8,128)S(1)}, f32[128,128]{1,0:T(8,128)S(1)}, u32[]{:S(2)}, u32[]{:S(2)}) collective-permute-start(f32[128,128]{1,0:T(8,128)S(1)} %add_add_fusion.5), channel_id=1, source_target_pairs={{0,32},{4,36},{8,40},{12,44},{16,48},{20,52},{24,56},{28,60},{32,6... | collective-permute-start | bytes 196616 | tf_op jit(solution)/shard_map/ppermute | solution.py:349
  112.6 13.2 %collective-permute-start.9 = (f32[128,128]{1,0:T(8,128)S(1)}, f32[128,128]{1,0:T(8,128)S(1)}, u32[]{:S(2)}, u32[]{:S(2)}) collective-permute-start(f32[128,128]{1,0:T(8,128)S(1)} %add_add_fusion.5), channel_id=1, source_target_pairs={{0,96},{4,100},{8,104},{12,108},{16,112},{20,116},{24,120},{28,124... | collective-permute-start | bytes 196616 | tf_op jit(solution)/shard_map/ppermute | solution.py:349
  114.4 14.1 %collective-permute-start.7 = (f32[128,128]{1,0:T(8,128)S(1)}, f32[128,128]{1,0:T(8,128)S(1)}, u32[]{:S(2)}, u32[]{:S(2)}) collective-permute-start(f32[128,128]{1,0:T(8,128)S(1)} %add_add_fusion.5), channel_id=1, source_target_pairs={{0,64},{4,68},{8,72},{12,76},{16,80},{20,84},{24,88},{28,92},{32,9... | collective-permute-start | bytes 196616 | tf_op jit(solution)/shard_map/ppermute | solution.py:349
  128.5 20.5 %collective-permute-start.14 = (f32[128,128]{1,0:T(8,128)S(1)}, f32[128,128]{1,0:T(8,128)S(1)}, u32[]{:S(2)}, u32[]{:S(2)}) collective-permute-start(f32[128,128]{1,0:T(8,128)S(1)} %add_add_fusion.4.refs_0_), channel_id=1, source_target_pairs={{0,8},{4,12},{8,16},{12,20},{16,24},{20,28},{24,0},{28,4},{32,40},... | collective-permute-start | bytes 196616 | tf_op jit(solution)/shard_map/ppermute | solution.py:349
  131.7 19.6 %collective-permute-start.15 = (f32[128,128]{1,0:T(8,128)S(1)}, f32[128,128]{1,0:T(8,128)S(1)}, u32[]{:S(2)}, u32[]{:S(2)}) collective-permute-start(f32[128,128]{1,0:T(8,128)S(1)} %add_add_fusion.4.refs_0_), channel_id=1, source_target_pairs={{0,24},{4,28},{8,0},{12,4},{16,8},{20,12},{24,16},{28,20},{32,56},... | collective-permute-start | bytes 196616 | tf_op jit(solution)/shard_map/ppermute | solution.py:349
  131.7 19.6 %collective-permute-start.13 = (f32[128,128]{1,0:T(8,128)S(1)}, f32[128,128]{1,0:T(8,128)S(1)}, u32[]{:S(2)}, u32[]{:S(2)}) collective-permute-start(f32[128,128]{1,0:T(8,128)S(1)} %add_add_fusion.4.refs_0_), channel_id=1, source_target_pairs={{0,16},{4,20},{8,24},{12,28},{16,0},{20,4},{24,8},{28,12},{32,48},... | collective-permute-start | bytes 196616 | tf_op jit(solution)/shard_map/ppermute | solution.py:349
  145.8 11.5 %collective-permute-start.10 = (s16[1040,128]{1,0:T(8,128)(2,1)S(1)}, s16[1040,128]{1,0:T(8,128)(2,1)S(1)}, u32[]{:S(2)}, u32[]{:S(2)}) collective-permute-start(s16[1040,128]{1,0:T(8,128)(2,1)S(1)} %get-tuple-element.25), channel_id=1, source_target_pairs={{0,2},{1,3},{2,0},{3,1},{4,6},{5,7},{6,4},{7,5},{8,10},{9,11},{10,... | collective-permute-start | bytes 798728 | tf_op jit(solution)/shard_map/ppermute | solution.py:379
  148.6 12.4 %collective-permute-start.11 = (s16[1040,128]{1,0:T(8,128)(2,1)S(1)}, s16[1040,128]{1,0:T(8,128)(2,1)S(1)}, u32[]{:S(2)}, u32[]{:S(2)}) collective-permute-start(s16[1040,128]{1,0:T(8,128)(2,1)S(1)} %get-tuple-element.26), channel_id=1, source_target_pairs={{0,1},{1,2},{2,3},{3,0},{4,5},{5,6},{6,7},{7,4},{8,9},{9,10},{10,1... | collective-permute-start | bytes 798728 | tf_op jit(solution)/shard_map/ppermute | solution.py:379
  148.9 12.1 %collective-permute-start.12 = (s16[1040,128]{1,0:T(8,128)(2,1)S(1)}, s16[1040,128]{1,0:T(8,128)(2,1)S(1)}, u32[]{:S(2)}, u32[]{:S(2)}) collective-permute-start(s16[1040,128]{1,0:T(8,128)(2,1)S(1)} %get-tuple-element.27), channel_id=1, source_target_pairs={{0,3},{1,0},{2,1},{3,2},{4,7},{5,4},{6,5},{7,6},{8,11},{9,8},{10,9... | collective-permute-start | bytes 798728 | tf_op jit(solution)/shard_map/ppermute | solution.py:379
  162.2 2.0 collective-permute-start.16
  164.2 4.4 %collective-permute-start.18 = (f32[128,128]{1,0:T(8,128)S(1)}, f32[128,128]{1,0:T(8,128)S(1)}, u32[]{:S(2)}, u32[]{:S(2)}) collective-permute-start(f32[128,128]{1,0:T(8,128)S(1)} %add.77), channel_id=1, source_target_pairs={{0,1},{1,2},{2,3},{3,0},{4,5},{5,6},{6,7},{7,4},{8,9},{9,10},{10,1... | collective-permute-start | bytes 196616 | tf_op jit(solution)/shard_map/ppermute | solution.py:349
  165.5 3.1 %collective-permute-start.19 = (f32[128,128]{1,0:T(8,128)S(1)}, f32[128,128]{1,0:T(8,128)S(1)}, u32[]{:S(2)}, u32[]{:S(2)}) collective-permute-start(f32[128,128]{1,0:T(8,128)S(1)} %add.77), channel_id=1, source_target_pairs={{0,3},{1,0},{2,1},{3,2},{4,7},{5,4},{6,5},{7,6},{8,11},{9,8},{10,9... | collective-permute-start | bytes 196616 | tf_op jit(solution)/shard_map/ppermute | solution.py:349
  167.0 4.6 %collective-permute-start.17 = (f32[128,128]{1,0:T(8,128)S(1)}, f32[128,128]{1,0:T(8,128)S(1)}, u32[]{:S(2)}, u32[]{:S(2)}) collective-permute-start(f32[128,128]{1,0:T(8,128)S(1)} %add.77), channel_id=1, source_target_pairs={{0,2},{1,3},{2,0},{3,1},{4,6},{5,7},{6,4},{7,5},{8,10},{9,11},{10,... | collective-permute-start | bytes 196616 | tf_op jit(solution)/shard_map/ppermute | solution.py:349
  171.6 4.4 %collective-permute-start.21 = (f32[128,128]{1,0:T(8,128)S(1)}, f32[128,128]{1,0:T(8,128)S(1)}, u32[]{:S(2)}, u32[]{:S(2)}) collective-permute-start(f32[128,128]{1,0:T(8,128)S(1)} %add_add_fusion.2), channel_id=1, source_target_pairs={{0,32},{4,36},{8,40},{12,44},{16,48},{20,52},{24,56},{28,60},{32,6... | collective-permute-start | bytes 196616 | tf_op jit(solution)/shard_map/ppermute | solution.py:349
  171.7 4.6 %collective-permute-start.22 = (f32[128,128]{1,0:T(8,128)S(1)}, f32[128,128]{1,0:T(8,128)S(1)}, u32[]{:S(2)}, u32[]{:S(2)}) collective-permute-start(f32[128,128]{1,0:T(8,128)S(1)} %add_add_fusion.2), channel_id=1, source_target_pairs={{0,96},{4,100},{8,104},{12,108},{16,112},{20,116},{24,120},{28,124... | collective-permute-start | bytes 196616 | tf_op jit(solution)/shard_map/ppermute | solution.py:349
  174.3 4.7 %collective-permute-start.20 = (f32[128,128]{1,0:T(8,128)S(1)}, f32[128,128]{1,0:T(8,128)S(1)}, u32[]{:S(2)}, u32[]{:S(2)}) collective-permute-start(f32[128,128]{1,0:T(8,128)S(1)} %add_add_fusion.2), channel_id=1, source_target_pairs={{0,64},{4,68},{8,72},{12,76},{16,80},{20,84},{24,88},{28,92},{32,9... | collective-permute-start | bytes 196616 | tf_op jit(solution)/shard_map/ppermute | solution.py:349
  179.1 4.4 %collective-permute-start.24 = (f32[128,128]{1,0:T(8,128)S(1)}, f32[128,128]{1,0:T(8,128)S(1)}, u32[]{:S(2)}, u32[]{:S(2)}) collective-permute-start(f32[128,128]{1,0:T(8,128)S(1)} %add_add_fusion.1), channel_id=1, source_target_pairs={{0,8},{4,12},{8,16},{12,20},{16,24},{20,28},{24,0},{28,4},{32,40},... | collective-permute-start | bytes 196616 | tf_op jit(solution)/shard_map/ppermute | solution.py:349
  179.2 4.3 %collective-permute-start.25 = (f32[128,128]{1,0:T(8,128)S(1)}, f32[128,128]{1,0:T(8,128)S(1)}, u32[]{:S(2)}, u32[]{:S(2)}) collective-permute-start(f32[128,128]{1,0:T(8,128)S(1)} %add_add_fusion.1), channel_id=1, source_target_pairs={{0,24},{4,28},{8,0},{12,4},{16,8},{20,12},{24,16},{28,20},{32,56},... | collective-permute-start | bytes 196616 | tf_op jit(solution)/shard_map/ppermute | solution.py:349
  181.8 4.6 %collective-permute-start.23 = (f32[128,128]{1,0:T(8,128)S(1)}, f32[128,128]{1,0:T(8,128)S(1)}, u32[]{:S(2)}, u32[]{:S(2)}) collective-permute-start(f32[128,128]{1,0:T(8,128)S(1)} %add_add_fusion.1), channel_id=1, source_target_pairs={{0,16},{4,20},{8,24},{12,28},{16,0},{20,4},{24,8},{28,12},{32,48},... | collective-permute-start | bytes 196616 | tf_op jit(solution)/shard_map/ppermute | solution.py:349
  186.5 6.4 %collective-permute-start.26 = (f32[128,128]{1,0:T(8,128)S(1)}, f32[128,128]{1,0:T(8,128)S(1)}, u32[]{:S(2)}, u32[]{:S(2)}) collective-permute-start(f32[128,128]{1,0:T(8,128)S(1)} %add_add_fusion.mine), channel_id=1, source_target_pairs={{0,4},{4,0},{8,12},{12,8},{16,20},{20,16},{24,28},{28,24},{32,36},... | collective-permute-start | bytes 196616 | tf_op jit(solution)/shard_map/ppermute | solution.py:341

commit v7 on v4

--- a/solution.py
+++ b/solution.py
@@ -9,8 +9,9 @@
 
 BR_DEV = 16
 HALF = 128
-GROUP = 22
 LOADS = 8
+AHEAD = 2
+LIMIT = 44 * 2**20
 STEP = 32704.0
 LEAST = 2.0**-80
 HIGHEST = lax.Precision.HIGHEST
@@ -63,7 +64,7 @@
     *_, total, values, arrived, value_sems, arrived_sems = refs
     outs = refs[-5 - shares : -5]
     count, loads, parts = values.shape[0], value_sems.shape[0], arrived_sems.shape[0]
-    assert count % GROUP == 0 and loads * GROUP % count == 0 and count % loads == 0
+    assert count % loads == 0 and AHEAD <= loads
 
     def bring(i):
         part = pl.ds(i * (count // loads), count // loads)
@@ -75,18 +76,21 @@
 
     for i in range(parts):
         bring_basis(i).start()
-    for i in range(loads):
+    for i in range(AHEAD):
         bring(i).start()
     total[...] = jnp.zeros_like(total)
     for i in range(parts):
         bring_basis(i).wait()
 
-    @pl.loop(0, count // GROUP)
+    @pl.loop(0, loads)
     def _(step):
-        for i in range(loads * GROUP // count):
-            bring(step * (loads * GROUP // count) + i).wait()
-        for u in range(GROUP):
-            t = step * GROUP + u
+        @pl.when(step + AHEAD < loads)
+        def _():
+            bring(step + AHEAD).start()
+
+        bring(step).wait()
+        for u in range(count // loads):
+            t = step * (count // loads) + u
             total[blocks[t]] += jnp.dot(values[t], arrived[places[t]], preferred_element_type=F32)
 
     each = BR_DEV // shares
@@ -117,7 +121,7 @@
             pltpu.SemaphoreType.DMA((4,)),
         ],
         out_shape=[jax.ShapeDtypeStruct((rows + 16, HALF), jnp.int16)] * shares,
-        compiler_params=pltpu.CompilerParams(vmem_limit_bytes=44 * 2**20),
+        compiler_params=pltpu.CompilerParams(vmem_limit_bytes=LIMIT),
         cost_estimate=pl.CostEstimate(
             flops=2 * count * height * depth * HALF,
             bytes_accessed=count * height * depth * 2 + arrived.size * 2,

time: 202 us -> 197 us (0.975)
  Pallas kernels: 57.9 us -> 48.8 us
  waiting for transfers between devices: 87.5 us -> 92.3 us
    pallas_call x2, Pallas kernels: 33.4 us -> 24.4 us  [tiles(): pl.pallas_call(functools.partial(tiles_kernel, shares), in_specs=inputs,...]
    all_to_all x2, waiting for transfers between devices: 52.5 us -> 57 us  [product(): arrived = lax.all_to_all(packed[half], 'row', 0, 0, tiled=True)]
  transfers between devices with their start and end apart: 20 -> 20, of which waited for: 10 -> 10; matrix products, arithmetic and copies ran while one was open for 0% -> 0% of each run, Pallas kernels for 23% -> 19%
where the time goes in v7:
time: 197 us
  waiting for transfers between devices  92.3 us (47%)
  starting transfers between devices  54.2 us (28%)
  Pallas kernels  48.8 us (25%)
    all_to_all x2, waiting for transfers between devices, product(): arrived = lax.all_to_all(packed[half], 'row', 0, 0, tiled=True)  57 us
    pallas_call x2, Pallas kernels, tiles(): pl.pallas_call(functools.partial(tiles_kernel, shares), in_specs=inputs,...  24.4 us
    all_to_all x2, starting transfers between devices, product(): arrived = lax.all_to_all(packed[half], 'row', 0, 0, tiled=True)  16.8 us
    ppermute x6, waiting for transfers between devices, product(): lax.ppermute(coded[k], 'col', [(i, (i + k) % cols) for i in range(cols)])  15 us
    ppermute x10, starting transfers between devices, sum_along(): lax.ppermute(part, axis, [(i, i + ((i // stride + k) % length - i // stri...  13.8 us
    ppermute x6, starting transfers between devices, product(): lax.ppermute(coded[k], 'col', [(i, (i + k) % cols) for i in range(cols)])  11 us
    all_to_all x1, waiting for transfers between devices, sum_all(): lax.all_to_all(part.reshape(n, height // n, HALF), axes, 0, 0, tiled=True)  10 us
    all_to_all x1, starting transfers between devices, sum_all(): lax.all_to_all(part.reshape(n, height // n, HALF), axes, 0, 0, tiled=True)  8.55 us
  transfers between devices with their start and end apart: 20, of which 10 were waited for; matrix products, arithmetic and copies ran while one was open for 0% of the time, Pallas kernels for 19%

profile of v7, /device:TPU:1, one launch (start us, length us, event | category | flops | bytes accessed | tf_op | source)
XLA Modules:
  0.0 197.0 jit_solution(6972923325364855775)
XLA Ops:
  0.6 3.8 %pack0.1 = bf16[64,256,128]{2,1,0:T(8,128)(2,1)} custom-call(s32[2,32]{1,0:T(2,128)} %bitcast.19, bf16[8,256,256]{2,1,0:T(8,128)(2,1)} %bitcast.17), custom_call_target="tpu_custom_call" | custom-call | bytes 8388608 | tf_op jit(solution)/shard_map/pack0/pallas_call | solution.py:40
  4.4 9.7 %all-to-all-start.1 = ((bf16[64,256,128]{2,1,0:T(8,128)(2,1)}), bf16[64,256,128]{2,1,0:T(8,128)(2,1)}, u32[]{:S(2)}, u32[]{:S(2)}) async-start(bf16[64,256,128]{2,1,0:T(8,128)(2,1)} %pack0.1), calls=%async_computation.1 | async-start | bytes 8388608 | tf_op jit(solution)/shard_map/all_to_all | solution.py:371
  14.1 3.8 %pack1.1 = bf16[64,256,128]{2,1,0:T(8,128)(2,1)} custom-call(s32[2,32]{1,0:T(2,128)} %bitcast.20, bf16[8,256,256]{2,1,0:T(8,128)(2,1)} %bitcast.18), custom_call_target="tpu_custom_call" | custom-call | bytes 8388608 | tf_op jit(solution)/shard_map/pack1/pallas_call | solution.py:40
  18.0 48.3 %all-to-all-done.1.arrived_hbm = bf16[64,256,128]{2,1,0:T(8,128)(2,1)} async-done(((bf16[64,256,128]{2,1,0:T(8,128)(2,1)}), bf16[64,256,128]{2,1,0:T(8,128)(2,1)}, u32[]{:S(2)}, u32[]{:S(2)}) %all-to-all-start.1) | async-done | bytes 4194336 | tf_op jit(solution)/shard_map/all_to_all | solution.py:371
  66.3 7.2 %all-to-all-start = ((bf16[64,256,128]{2,1,0:T(8,128)(2,1)}), bf16[64,256,128]{2,1,0:T(8,128)(2,1)}, u32[]{:S(2)}, u32[]{:S(2)}) async-start(bf16[64,256,128]{2,1,0:T(8,128)(2,1)} %pack1.1), calls=%async_computation | async-start | bytes 8388608 | tf_op jit(solution)/shard_map/all_to_all | solution.py:371
  73.5 12.2 %tiles0.1 = (s16[1040,128]{1,0:T(8,128)(2,1)S(1)}, s16[1040,128]{1,0:T(8,128)(2,1)S(1)}, s16[1040,128]{1,0:T(8,128)(2,1)S(1)}, s16[1040,128]{1,0:T(8,128)(2,1)S(1)}) custom-call(s32[1]{0:T(128)} %bitcast.me, s32[176]{0:T(256)S(1)} %bitcast.11, s32[176]{0:T(256)S(1)} %bitcast.13, bf16[176,256,256]{2,1,0:T(8,128)(2,1)} %bitcast.15, ...), custom_call_target="tpu_custom_call" | custom-call | flops 2952790016 | bytes 27262976 | tf_op jit(solution)/shard_map/tiles0/pallas_call | solution.py:112
  85.7 2.8 %collective-permute-start = (s16[1040,128]{1,0:T(8,128)(2,1)S(1)}, s16[1040,128]{1,0:T(8,128)(2,1)S(1)}, u32[]{:S(2)}, u32[]{:S(2)}) collective-permute-start(s16[1040,128]{1,0:T(8,128)(2,1)S(1)} %get-tuple-element.18), channel_id=1, source_target_pairs={{0,2},{1,3},{2,0},{3,1},{4,6},{5,7},{6,4},{7,5},{8,10},{9,11},{10,... | collective-permute-start | bytes 798728 | tf_op jit(solution)/shard_map/ppermute | solution.py:374
  88.9 2.4 %collective-permute-start.2 = (s16[1040,128]{1,0:T(8,128)(2,1)S(1)}, s16[1040,128]{1,0:T(8,128)(2,1)S(1)}, u32[]{:S(2)}, u32[]{:S(2)}) collective-permute-start(s16[1040,128]{1,0:T(8,128)(2,1)S(1)} %get-tuple-element.20), channel_id=1, source_target_pairs={{0,3},{1,0},{2,1},{3,2},{4,7},{5,4},{6,5},{7,6},{8,11},{9,8},{10,9... | collective-permute-start | bytes 798728 | tf_op jit(solution)/shard_map/ppermute | solution.py:374
  91.2 3.9 %collective-permute-done.refs_1_ = s16[1040,128]{1,0:T(8,128)(2,1)S(1)} collective-permute-done((s16[1040,128]{1,0:T(8,128)(2,1)S(1)}, s16[1040,128]{1,0:T(8,128)(2,1)S(1)}, u32[]{:S(2)}, u32[]{:S(2)}) %collective-permute-start) | collective-permute-done | bytes 266272 | tf_op jit(solution)/shard_map/ppermute | solution.py:374
  95.2 6.3 %collective-permute-done.1.refs_2_ = s16[1040,128]{1,0:T(8,128)(2,1)S(1)} collective-permute-done((s16[1040,128]{1,0:T(8,128)(2,1)S(1)}, s16[1040,128]{1,0:T(8,128)(2,1)S(1)}, u32[]{:S(2)}, u32[]{:S(2)}) %collective-permute-start.1) | collective-permute-done | bytes 266272 | tf_op jit(solution)/shard_map/ppermute | solution.py:374
  101.5 0.8 gram0.1
  102.9 0.9 collective-permute-done.3
  103.8 2.4 %collective-permute-start.6 = (f32[128,128]{1,0:T(8,128)S(1)}, f32[128,128]{1,0:T(8,128)S(1)}, u32[]{:S(2)}, u32[]{:S(2)}) collective-permute-start(f32[128,128]{1,0:T(8,128)S(1)} %add.37), channel_id=1, source_target_pairs={{0,3},{1,0},{2,1},{3,2},{4,7},{5,4},{6,5},{7,6},{8,11},{9,8},{10,9... | collective-permute-start | bytes 196616 | tf_op jit(solution)/shard_map/ppermute | solution.py:338
  106.2 1.3 collective-permute-start.4
  107.5 5.1 %collective-permute-done.5 = f32[128,128]{1,0:T(8,128)S(1)} collective-permute-done((f32[128,128]{1,0:T(8,128)S(1)}, f32[128,128]{1,0:T(8,128)S(1)}, u32[]{:S(2)}, u32[]{:S(2)}) %collective-permute-start.5) | collective-permute-done | bytes 65568 | tf_op jit(solution)/shard_map/ppermute | solution.py:338
  112.6 2.7 %collective-permute-start.12 = (f32[128,128]{1,0:T(8,128)S(1)}, f32[128,128]{1,0:T(8,128)S(1)}, u32[]{:S(2)}, u32[]{:S(2)}) collective-permute-start(f32[128,128]{1,0:T(8,128)S(1)} %add_add_fusion.2.refs_0_), channel_id=1, source_target_pairs={{0,96},{4,100},{8,104},{12,108},{16,112},{20,116},{24,120},{28,124... | collective-permute-start | bytes 196616 | tf_op jit(solution)/shard_map/ppermute | solution.py:338
  115.3 1.7 collective-permute-start.10
  117.1 8.7 %all-to-all-done.arrived_hbm = bf16[64,256,128]{2,1,0:T(8,128)(2,1)} async-done(((bf16[64,256,128]{2,1,0:T(8,128)(2,1)}), bf16[64,256,128]{2,1,0:T(8,128)(2,1)}, u32[]{:S(2)}, u32[]{:S(2)}) %all-to-all-start) | async-done | bytes 4194336 | tf_op jit(solution)/shard_map/all_to_all | solution.py:371
  125.8 12.2 %tiles1.1 = (s16[1040,128]{1,0:T(8,128)(2,1)S(1)}, s16[1040,128]{1,0:T(8,128)(2,1)S(1)}, s16[1040,128]{1,0:T(8,128)(2,1)S(1)}, s16[1040,128]{1,0:T(8,128)(2,1)S(1)}) custom-call(s32[1]{0:T(128)} %bitcast.me, s32[176]{0:T(256)S(1)} %bitcast.12, s32[176]{0:T(256)S(1)} %bitcast.14, bf16[176,256,256]{2,1,0:T(8,128)(2,1)} %bitcast.16, ...), custom_call_target="tpu_custom_call" | custom-call | flops 2952790016 | bytes 27262976 | tf_op jit(solution)/shard_map/tiles1/pallas_call | solution.py:112
  137.9 2.8 %collective-permute-start.7 = (s16[1040,128]{1,0:T(8,128)(2,1)S(1)}, s16[1040,128]{1,0:T(8,128)(2,1)S(1)}, u32[]{:S(2)}, u32[]{:S(2)}) collective-permute-start(s16[1040,128]{1,0:T(8,128)(2,1)S(1)} %get-tuple-element.23), channel_id=1, source_target_pairs={{0,2},{1,3},{2,0},{3,1},{4,6},{5,7},{6,4},{7,5},{8,10},{9,11},{10,... | collective-permute-start | bytes 798728 | tf_op jit(solution)/shard_map/ppermute | solution.py:374
  141.1 2.3 %collective-permute-start.9 = (s16[1040,128]{1,0:T(8,128)(2,1)S(1)}, s16[1040,128]{1,0:T(8,128)(2,1)S(1)}, u32[]{:S(2)}, u32[]{:S(2)}) collective-permute-start(s16[1040,128]{1,0:T(8,128)(2,1)S(1)} %get-tuple-element.25), channel_id=1, source_target_pairs={{0,3},{1,0},{2,1},{3,2},{4,7},{5,4},{6,5},{7,6},{8,11},{9,8},{10,9... | collective-permute-start | bytes 798728 | tf_op jit(solution)/shard_map/ppermute | solution.py:374
  143.4 3.2 %collective-permute-start.15 = (f32[128,128]{1,0:T(8,128)S(1)}, f32[128,128]{1,0:T(8,128)S(1)}, u32[]{:S(2)}, u32[]{:S(2)}) collective-permute-start(f32[128,128]{1,0:T(8,128)S(1)} %add_add_fusion.1), channel_id=1, source_target_pairs={{0,24},{4,28},{8,0},{12,4},{16,8},{20,12},{24,16},{28,20},{32,56},... | collective-permute-start | bytes 196616 | tf_op jit(solution)/shard_map/ppermute | solution.py:338
  146.8 1.7 collective-permute-start.13
  148.5 4.8 %collective-permute-done.8.refs_2_ = s16[1040,128]{1,0:T(8,128)(2,1)S(1)} collective-permute-done((s16[1040,128]{1,0:T(8,128)(2,1)S(1)}, s16[1040,128]{1,0:T(8,128)(2,1)S(1)}, u32[]{:S(2)}, u32[]{:S(2)}) %collective-permute-start.8) | collective-permute-done | bytes 266272 | tf_op jit(solution)/shard_map/ppermute | solution.py:374
  153.3 1.9 gram1.1
  155.2 8.6 %all-to-all-start.2 = ((f32[128,2,128]{2,1,0:T(2,128)}), f32[128,2,128]{2,1,0:T(2,128)S(1)}, u32[]{:S(2)}, u32[]{:S(2)}) async-start(f32[128,2,128]{2,1,0:T(2,128)} %bitcast.8), calls=%async_computation.2 | async-start | bytes 262144 | tf_op jit(solution)/shard_map/all_to_all | solution.py:322
  163.8 10.0 %all-to-all-done.2 = f32[128,2,128]{2,1,0:T(2,128)S(1)} async-done(((f32[128,2,128]{2,1,0:T(2,128)}), f32[128,2,128]{2,1,0:T(2,128)S(1)}, u32[]{:S(2)}, u32[]{:S(2)}) %all-to-all-start.2) | async-done | bytes 131104 | tf_op jit(solution)/shard_map/all_to_all | solution.py:322
  174.0 0.7 broadcast_in_dim.2
  174.7 4.1 %all-to-all-start.3 = ((f32[128,2,128]{2,1,0:T(2,128)}), f32[128,2,128]{2,1,0:T(2,128)S(1)}, u32[]{:S(2)}, u32[]{:S(2)}) async-start(f32[128,2,128]{2,1,0:T(2,128)} %broadcast_in_dim.2), calls=%async_computation.3 | async-start | bytes 262144 | tf_op jit(solution)/shard_map/all_to_all | solution.py:325
  178.7 6.0 %first.1 = (f32[128,128]{1,0:T(8,128)S(1)}, f32[128,128]{1,0:T(8,128)S(1)}, f32[1024,128]{1,0:T(8,128)S(1)}) custom-call(f32[128,128]{1,0:T(8,128)S(1)} %add_add_fusion.g_ref, f32[1024,128]{1,0:T(8,128)S(1)} %get-tuple-element.26.refs_4_.y_ref), custom_call_target="tpu_custom_call" | custom-call | flops 20971520000 | bytes 1048576 | tf_op jit(solution)/shard_map/first/pallas_call | solution.py:275
  184.7 4.1 %all-to-all-done.3 = f32[128,2,128]{2,1,0:T(2,128)S(1)} async-done(((f32[128,2,128]{2,1,0:T(2,128)}), f32[128,2,128]{2,1,0:T(2,128)S(1)}, u32[]{:S(2)}, u32[]{:S(2)}) %all-to-all-start.3) | async-done | bytes 131104 | tf_op jit(solution)/shard_map/all_to_all | solution.py:325
  188.8 8.2 %last.1 = (f32[1024,256]{1,0:T(8,128)}, f32[256,256]{1,0:T(8,128)}) custom-call(f32[256,128]{1,0:T(8,128)S(1)} %bitcast.10, f32[128,128]{1,0:T(8,128)S(1)} %get-tuple-element.28.r_ref, f32[128,128]{1,0:T(8,128)S(1)} %get-tuple-element.29.t_ref, f32[1024,128]{1,0:T(8,128)S(1)} %get-tuple-element.30.z_ref, f32[1024,128]{1,0:T(8,128)S(1)} %get-tuple-element.31.y_ref), custom_call_target="tpu_custom_call" | custom-call | tf_op jit(solution)/shard_map/last/pallas_call | solution.py:307
  (29 shorter events, 1.7 us)
Async XLA Ops:
  4.4 61.9 %all-to-all-start.1 = ((bf16[64,256,128]{2,1,0:T(8,128)(2,1)}), bf16[64,256,128]{2,1,0:T(8,128)(2,1)}, u32[]{:S(2)}, u32[]{:S(2)}) async-start(bf16[64,256,128]{2,1,0:T(8,128)(2,1)} %pack0.1), calls=%async_computation.1 | async-start | bytes 8388608 | tf_op jit(solution)/shard_map/all_to_all | solution.py:371
  18.0 55.6 %copy-start.1 = (s32[176,1]{0,1:T(1,128)S(1)}, s32[176,1]{0,1:T(1,128)}, u32[]{:S(2)}) copy-start(s32[176,1]{0,1:T(1,128)} %param.9) | copy-start | bytes 2116
  18.0 55.6 %copy-start.2 = (s32[176,1]{0,1:T(1,128)S(1)}, s32[176,1]{0,1:T(1,128)}, u32[]{:S(2)}) copy-start(s32[176,1]{0,1:T(1,128)} %param.8) | copy-start | bytes 2116
  18.0 55.6 %copy-start = (s32[176,1]{0,1:T(1,128)S(1)}, s32[176,1]{0,1:T(1,128)}, u32[]{:S(2)}) copy-start(s32[176,1]{0,1:T(1,128)} %param.7) | copy-start | bytes 2116
  66.3 59.4 %all-to-all-start = ((bf16[64,256,128]{2,1,0:T(8,128)(2,1)}), bf16[64,256,128]{2,1,0:T(8,128)(2,1)}, u32[]{:S(2)}, u32[]{:S(2)}) async-start(bf16[64,256,128]{2,1,0:T(8,128)(2,1)} %pack1.1), calls=%async_computation | async-start | bytes 8388608 | tf_op jit(solution)/shard_map/all_to_all | solution.py:371
  85.7 9.4 %collective-permute-start = (s16[1040,128]{1,0:T(8,128)(2,1)S(1)}, s16[1040,128]{1,0:T(8,128)(2,1)S(1)}, u32[]{:S(2)}, u32[]{:S(2)}) collective-permute-start(s16[1040,128]{1,0:T(8,128)(2,1)S(1)} %get-tuple-element.18), channel_id=1, source_target_pairs={{0,2},{1,3},{2,0},{3,1},{4,6},{5,7},{6,4},{7,5},{8,10},{9,11},{10,... | collective-permute-start | bytes 798728 | tf_op jit(solution)/shard_map/ppermute | solution.py:374
  88.6 12.9 %collective-permute-start.1 = (s16[1040,128]{1,0:T(8,128)(2,1)S(1)}, s16[1040,128]{1,0:T(8,128)(2,1)S(1)}, u32[]{:S(2)}, u32[]{:S(2)}) collective-permute-start(s16[1040,128]{1,0:T(8,128)(2,1)S(1)} %get-tuple-element.19), channel_id=1, source_target_pairs={{0,1},{1,2},{2,3},{3,0},{4,5},{5,6},{6,7},{7,4},{8,9},{9,10},{10,1... | collective-permute-start | bytes 798728 | tf_op jit(solution)/shard_map/ppermute | solution.py:374
  88.9 12.6 %collective-permute-start.2 = (s16[1040,128]{1,0:T(8,128)(2,1)S(1)}, s16[1040,128]{1,0:T(8,128)(2,1)S(1)}, u32[]{:S(2)}, u32[]{:S(2)}) collective-permute-start(s16[1040,128]{1,0:T(8,128)(2,1)S(1)} %get-tuple-element.20), channel_id=1, source_target_pairs={{0,3},{1,0},{2,1},{3,2},{4,7},{5,4},{6,5},{7,6},{8,11},{9,8},{10,9... | collective-permute-start | bytes 798728 | tf_op jit(solution)/shard_map/ppermute | solution.py:374
  102.3 1.5 collective-permute-start.3
  103.8 3.7 %collective-permute-start.6 = (f32[128,128]{1,0:T(8,128)S(1)}, f32[128,128]{1,0:T(8,128)S(1)}, u32[]{:S(2)}, u32[]{:S(2)}) collective-permute-start(f32[128,128]{1,0:T(8,128)S(1)} %add.37), channel_id=1, source_target_pairs={{0,3},{1,0},{2,1},{3,2},{4,7},{5,4},{6,5},{7,6},{8,11},{9,8},{10,9... | collective-permute-start | bytes 196616 | tf_op jit(solution)/shard_map/ppermute | solution.py:338
  106.2 6.4 %collective-permute-start.5 = (f32[128,128]{1,0:T(8,128)S(1)}, f32[128,128]{1,0:T(8,128)S(1)}, u32[]{:S(2)}, u32[]{:S(2)}) collective-permute-start(f32[128,128]{1,0:T(8,128)S(1)} %add.37), channel_id=1, source_target_pairs={{0,1},{1,2},{2,3},{3,0},{4,5},{5,6},{6,7},{7,4},{8,9},{9,10},{10,1... | collective-permute-start | bytes 196616 | tf_op jit(solution)/shard_map/ppermute | solution.py:338
  106.2 6.4 %collective-permute-start.4 = (f32[128,128]{1,0:T(8,128)S(1)}, f32[128,128]{1,0:T(8,128)S(1)}, u32[]{:S(2)}, u32[]{:S(2)}) collective-permute-start(f32[128,128]{1,0:T(8,128)S(1)} %add.37), channel_id=1, source_target_pairs={{0,2},{1,3},{2,0},{3,1},{4,6},{5,7},{6,4},{7,5},{8,10},{9,11},{10,... | collective-permute-start | bytes 196616 | tf_op jit(solution)/shard_map/ppermute | solution.py:338
  112.6 28.5 %collective-permute-start.12 = (f32[128,128]{1,0:T(8,128)S(1)}, f32[128,128]{1,0:T(8,128)S(1)}, u32[]{:S(2)}, u32[]{:S(2)}) collective-permute-start(f32[128,128]{1,0:T(8,128)S(1)} %add_add_fusion.2.refs_0_), channel_id=1, source_target_pairs={{0,96},{4,100},{8,104},{12,108},{16,112},{20,116},{24,120},{28,124... | collective-permute-start | bytes 196616 | tf_op jit(solution)/shard_map/ppermute | solution.py:338
  115.3 28.1 %collective-permute-start.11 = (f32[128,128]{1,0:T(8,128)S(1)}, f32[128,128]{1,0:T(8,128)S(1)}, u32[]{:S(2)}, u32[]{:S(2)}) collective-permute-start(f32[128,128]{1,0:T(8,128)S(1)} %add_add_fusion.2.refs_0_), channel_id=1, source_target_pairs={{0,32},{4,36},{8,40},{12,44},{16,48},{20,52},{24,56},{28,60},{32,6... | collective-permute-start | bytes 196616 | tf_op jit(solution)/shard_map/ppermute | solution.py:338
  115.3 28.1 %collective-permute-start.10 = (f32[128,128]{1,0:T(8,128)S(1)}, f32[128,128]{1,0:T(8,128)S(1)}, u32[]{:S(2)}, u32[]{:S(2)}) collective-permute-start(f32[128,128]{1,0:T(8,128)S(1)} %add_add_fusion.2.refs_0_), channel_id=1, source_target_pairs={{0,64},{4,68},{8,72},{12,76},{16,80},{20,84},{24,88},{28,92},{32,9... | collective-permute-start | bytes 196616 | tf_op jit(solution)/shard_map/ppermute | solution.py:338
  137.9 8.8 %collective-permute-start.7 = (s16[1040,128]{1,0:T(8,128)(2,1)S(1)}, s16[1040,128]{1,0:T(8,128)(2,1)S(1)}, u32[]{:S(2)}, u32[]{:S(2)}) collective-permute-start(s16[1040,128]{1,0:T(8,128)(2,1)S(1)} %get-tuple-element.23), channel_id=1, source_target_pairs={{0,2},{1,3},{2,0},{3,1},{4,6},{5,7},{6,4},{7,5},{8,10},{9,11},{10,... | collective-permute-start | bytes 798728 | tf_op jit(solution)/shard_map/ppermute | solution.py:374
  140.7 12.6 %collective-permute-start.8 = (s16[1040,128]{1,0:T(8,128)(2,1)S(1)}, s16[1040,128]{1,0:T(8,128)(2,1)S(1)}, u32[]{:S(2)}, u32[]{:S(2)}) collective-permute-start(s16[1040,128]{1,0:T(8,128)(2,1)S(1)} %get-tuple-element.24), channel_id=1, source_target_pairs={{0,1},{1,2},{2,3},{3,0},{4,5},{5,6},{6,7},{7,4},{8,9},{9,10},{10,1... | collective-permute-start | bytes 798728 | tf_op jit(solution)/shard_map/ppermute | solution.py:374
  141.1 12.2 %collective-permute-start.9 = (s16[1040,128]{1,0:T(8,128)(2,1)S(1)}, s16[1040,128]{1,0:T(8,128)(2,1)S(1)}, u32[]{:S(2)}, u32[]{:S(2)}) collective-permute-start(s16[1040,128]{1,0:T(8,128)(2,1)S(1)} %get-tuple-element.25), channel_id=1, source_target_pairs={{0,3},{1,0},{2,1},{3,2},{4,7},{5,4},{6,5},{7,6},{8,11},{9,8},{10,9... | collective-permute-start | bytes 798728 | tf_op jit(solution)/shard_map/ppermute | solution.py:374
  143.4 20.3 %collective-permute-start.15 = (f32[128,128]{1,0:T(8,128)S(1)}, f32[128,128]{1,0:T(8,128)S(1)}, u32[]{:S(2)}, u32[]{:S(2)}) collective-permute-start(f32[128,128]{1,0:T(8,128)S(1)} %add_add_fusion.1), channel_id=1, source_target_pairs={{0,24},{4,28},{8,0},{12,4},{16,8},{20,12},{24,16},{28,20},{32,56},... | collective-permute-start | bytes 196616 | tf_op jit(solution)/shard_map/ppermute | solution.py:338
  146.7 17.1 %collective-permute-start.14 = (f32[128,128]{1,0:T(8,128)S(1)}, f32[128,128]{1,0:T(8,128)S(1)}, u32[]{:S(2)}, u32[]{:S(2)}) collective-permute-start(f32[128,128]{1,0:T(8,128)S(1)} %add_add_fusion.1), channel_id=1, source_target_pairs={{0,8},{4,12},{8,16},{12,20},{16,24},{20,28},{24,0},{28,4},{32,40},... | collective-permute-start | bytes 196616 | tf_op jit(solution)/shard_map/ppermute | solution.py:338
  146.8 17.0 %collective-permute-start.13 = (f32[128,128]{1,0:T(8,128)S(1)}, f32[128,128]{1,0:T(8,128)S(1)}, u32[]{:S(2)}, u32[]{:S(2)}) collective-permute-start(f32[128,128]{1,0:T(8,128)S(1)} %add_add_fusion.1), channel_id=1, source_target_pairs={{0,16},{4,20},{8,24},{12,28},{16,0},{20,4},{24,8},{28,12},{32,48},... | collective-permute-start | bytes 196616 | tf_op jit(solution)/shard_map/ppermute | solution.py:338
  155.2 18.6 %all-to-all-start.2 = ((f32[128,2,128]{2,1,0:T(2,128)}), f32[128,2,128]{2,1,0:T(2,128)S(1)}, u32[]{:S(2)}, u32[]{:S(2)}) async-start(f32[128,2,128]{2,1,0:T(2,128)} %bitcast.8), calls=%async_computation.2 | async-start | bytes 262144 | tf_op jit(solution)/shard_map/all_to_all | solution.py:322
  174.7 14.1 %all-to-all-start.3 = ((f32[128,2,128]{2,1,0:T(2,128)}), f32[128,2,128]{2,1,0:T(2,128)S(1)}, u32[]{:S(2)}, u32[]{:S(2)}) async-start(f32[128,2,128]{2,1,0:T(2,128)} %broadcast_in_dim.2), calls=%async_computation.3 | async-start | bytes 262144 | tf_op jit(solution)/shard_map/all_to_all | solution.py:325
